TPU v7x, 32 devices: a whole 2x2x4 slice. The times are simulated.
32 devices in a mesh: dp: 8 (over z, x), seq: 4 (over y, core).
Axes of the slice: x: 2, y: 2, z: 4, core: 2. Of those that a mesh axis runs over, the one named last changes fastest.
Arguments:
- tokens: bfloat16 [2, 16, 1024, 1536], P(None, 'dp', 'seq'), may hold values from -6 to 6
- cotangent: bfloat16 [2, 16, 1024, 1536], P(None, 'dp', 'seq'), may hold values from -6 to 6
- lengths: int32 [2, 16], P(None, 'dp'), may hold values from 256 to 1024, as said below
- buckets: int32 [2047], replicated, may hold values from 0 to 31, as said below
- gain_one: bfloat16 [1536], P('dp'), may hold values from 0.25 to 1.75
- gain_two: bfloat16 [1536], P('dp'), may hold values from 0.25 to 1.75
- table: bfloat16 [32, 12], P('dp'), may hold values from -3 to 3
- w_query: bfloat16 [1536, 768], P('dp'), may hold values from -0.078125 to 0.078125
- w_key: bfloat16 [1536, 768], P('dp'), may hold values from -0.078125 to 0.078125
- w_value: bfloat16 [1536, 768], P('dp'), may hold values from -0.15625 to 0.15625
- w_out: bfloat16 [768, 1536], P(None, 'dp'), may hold values from -1.75 to 1.75
- w_gate: bfloat16 [1536, 3968], P('dp'), may hold values from -0.15625 to 0.15625
- w_up: bfloat16 [1536, 3968], P('dp'), may hold values from -0.15625 to 0.15625
- w_down: bfloat16 [3968, 1536], P(None, 'dp'), may hold values from -0.09375 to 0.09375
Outputs:
- output: bfloat16 [2, 16, 1024, 1536], P(None, 'dp', 'seq')
- input_grad: float32 [2, 16, 1024, 1536], P(None, 'dp', 'seq')
- grad_gain_one: float32 [1536], P('dp')
- grad_gain_two: float32 [1536], P('dp')
- grad_table: float32 [32, 12], P('dp')
- grad_query: float32 [1536, 768], P('dp')
- grad_key: float32 [1536, 768], P('dp')
- grad_value: float32 [1536, 768], P('dp')
- grad_out: float32 [768, 1536], P(None, 'dp')
- grad_gate: float32 [1536, 3968], P('dp')
- grad_up: float32 [1536, 3968], P('dp')
- grad_down: float32 [3968, 1536], P(None, 'dp')
Inputs may be any that keep to these rules, and one draw needn't show every extreme that they name: `lengths`: among the 4 rows that one dp index holds over all micro-batches, one is 1024 long. `buckets`: entry 1023 + o is the bucket of the offset o = key position - query position: 0 at o = 0, below 16 for o < 0, 16 or more for o > 0, never falling as |o| grows on either side.
All inputs are finite; a program needn't handle non-finite values.
Results may differ from a plain program's by a relative error of at most 0.014.
The roundings to bfloat16 on the way count: a program that leaves them out, or rounds other values in their place, can miss the bound.
Values may be sent and summed in bfloat16 or wider, within the bound.
A program may use at most 320 MiB of HBM per device.

v0:
```python
import jax
import jax.numpy as jnp
from jax import lax
from jax.sharding import PartitionSpec as P

eps = 1e-06
masked_value = -1e30
highest = lax.Precision.HIGHEST


def rms_scale(values, gain):
    return values * lax.rsqrt(jnp.mean(values * values, axis=-1, keepdims=True) + eps) * gain


def gated(gate, up):
    return jax.nn.gelu(gate, approximate=True) * up


def fetch_each(shards):
    return (
        lax.all_gather(shards[0], "dp", axis=0, tiled=True),
        lax.all_gather(shards[1], "dp", axis=0, tiled=True),
        lax.all_gather(shards[2], "dp", axis=0, tiled=True),
        lax.all_gather(shards[3], "dp", axis=0, tiled=True),
        lax.all_gather(shards[4], "dp", axis=0, tiled=True),
        lax.all_gather(shards[5], "dp", axis=0, tiled=True),
        lax.all_gather(shards[6], "dp", axis=1, tiled=True),
        lax.all_gather(shards[7], "dp", axis=0, tiled=True),
        lax.all_gather(shards[8], "dp", axis=0, tiled=True),
        lax.all_gather(shards[9], "dp", axis=1, tiled=True),
    )


def reduce_each(grads):
    summed = (
        lax.psum_scatter(grads[0], "dp", scatter_dimension=0, tiled=True),
        lax.psum_scatter(grads[1], "dp", scatter_dimension=0, tiled=True),
        lax.psum_scatter(grads[2], "dp", scatter_dimension=0, tiled=True),
        lax.psum_scatter(grads[3], "dp", scatter_dimension=0, tiled=True),
        lax.psum_scatter(grads[4], "dp", scatter_dimension=0, tiled=True),
        lax.psum_scatter(grads[5], "dp", scatter_dimension=0, tiled=True),
        lax.psum_scatter(grads[6], "dp", scatter_dimension=1, tiled=True),
        lax.psum_scatter(grads[7], "dp", scatter_dimension=0, tiled=True),
        lax.psum_scatter(grads[8], "dp", scatter_dimension=0, tiled=True),
        lax.psum_scatter(grads[9], "dp", scatter_dimension=1, tiled=True),
    )
    return lax.psum(
        (
            summed[0],
            summed[1],
            summed[2],
            summed[3],
            summed[4],
            summed[5],
            summed[6],
            summed[7],
            summed[8],
            summed[9],
        ),
        "seq",
    )


def item_columns(full_table, head_of):
    chooser = (head_of[:, None] == jnp.arange(full_table.shape[1])[None, :]).astype(jnp.float32)
    columns = jnp.dot(full_table, chooser.T, precision=highest)
    return (columns.astype(jnp.bfloat16), chooser)


def block_onehot(buckets, start, block, seq_len, levels):
    span = block + seq_len - 1
    window = lax.dynamic_slice_in_dim(buckets, seq_len - start - block, span, 0)
    padded = jnp.concatenate([window, jnp.zeros((1,), jnp.int32)])
    rolled = jnp.roll(padded, -(block - 1))
    skewed = jnp.tile(rolled, block)[: block * span].reshape(block, span)[:, :seq_len]
    return (skewed[:, :, None] == jnp.arange(levels)[None, None, :]).astype(jnp.bfloat16)


def block_bias(buckets, columns, start, block, seq_len):
    onehot = block_onehot(buckets, start, block, seq_len, columns.shape[0])
    return (jnp.einsum("qkb,bi->iqk", onehot, columns, preferred_element_type=jnp.float32), onehot)


def attend(query, key, value, buckets, columns, valid, block):
    seq_len, count, head_dim = key.shape

    def one_block(start):
        query_block = lax.dynamic_slice_in_dim(query, start, block, 0)
        bias_block, onehot = block_bias(buckets, columns, start, block, seq_len)
        raw = jnp.einsum("qie,kie->iqk", query_block, key, preferred_element_type=jnp.float32)
        scores = jnp.where(valid[:, None, :], raw + bias_block, masked_value)
        top = jnp.max(scores, axis=-1, keepdims=True)
        expo = jnp.exp(scores - top)
        total = jnp.sum(expo, axis=-1, keepdims=True)
        probs = (expo / total).astype(jnp.bfloat16)
        mixed = jnp.einsum("iqk,kie->qie", probs, value, preferred_element_type=jnp.float32)
        return (mixed.astype(jnp.bfloat16), (top + jnp.log(total))[..., 0])

    starts = jnp.arange(seq_len // block) * block
    mixed, lses = lax.map(one_block, starts)
    return (mixed.reshape(seq_len, count * head_dim), lses)


def attend_back(query, key, value, grad_mixed, lses, buckets, columns, valid, block):
    seq_len, count, head_dim = key.shape
    levels = columns.shape[0]

    def one_block(carry, inputs):
        grad_key, grad_value, grad_bias = carry
        start, lse_block = inputs
        query_block = lax.dynamic_slice_in_dim(query, start, block, 0)
        grad_block = lax.dynamic_slice_in_dim(grad_mixed, start, block, 0)
        bias_block, onehot = block_bias(buckets, columns, start, block, seq_len)
        raw = jnp.einsum("qie,kie->iqk", query_block, key, preferred_element_type=jnp.float32)
        scores = jnp.where(valid[:, None, :], raw + bias_block, masked_value)
        probs = jnp.exp(scores - lse_block[..., None])
        grad_value = grad_value + jnp.einsum(
            "iqk,qie->kie",
            probs.astype(jnp.bfloat16),
            grad_block,
            preferred_element_type=jnp.float32,
        )
        grad_probs = jnp.einsum(
            "qie,kie->iqk", grad_block, value, preferred_element_type=jnp.float32
        )
        inner_sum = jnp.sum(probs * grad_probs, axis=-1, keepdims=True)
        grad_scores = probs * (grad_probs - inner_sum)
        grad_bias = grad_bias + jnp.einsum(
            "iqk,qkb->ib", grad_scores, onehot.astype(jnp.float32), precision=highest
        )
        rounded = grad_scores.astype(jnp.bfloat16)
        grad_query = jnp.einsum(
            "iqk,kie->qie", rounded, key, preferred_element_type=jnp.float32
        ).astype(jnp.bfloat16)
        grad_key = grad_key + jnp.einsum(
            "iqk,qie->kie", rounded, query_block, preferred_element_type=jnp.float32
        )
        return ((grad_key, grad_value, grad_bias), grad_query)

    starts = jnp.arange(seq_len // block) * block
    zeros_kv = jnp.zeros((seq_len, count, head_dim), jnp.float32)
    zeros_bias = jnp.zeros((count, levels), jnp.float32)
    (grad_key, grad_value, grad_bias), grad_query = lax.scan(
        one_block, (zeros_kv, zeros_kv, zeros_bias), (starts, lses)
    )
    flat = count * head_dim
    return (
        grad_query.reshape(seq_len, flat),
        grad_key.astype(jnp.bfloat16).reshape(seq_len, flat),
        grad_value.astype(jnp.bfloat16).reshape(seq_len, flat),
        grad_bias,
    )


def body(
    tokens,
    cotangent,
    lengths,
    buckets,
    gain_one,
    gain_two,
    table,
    w_query,
    w_key,
    w_value,
    w_out,
    w_gate,
    w_up,
    w_down,
):
    micro, rows, local, width = tokens.shape
    seq_devices = lax.axis_size("seq")
    seq_rank = lax.axis_index("seq")
    heads = table.shape[1]
    inner = w_query.shape[1]
    head_dim = inner // heads
    seq_len = local * seq_devices
    block = min(512, seq_len)
    count = rows * heads // seq_devices
    items = seq_rank * count + jnp.arange(count)
    row_of = items // heads
    head_of = items % heads
    row_match = row_of[:, None] == jnp.arange(rows)[None, :]
    shards = (gain_one, gain_two, table, w_query, w_key, w_value, w_out, w_gate, w_up, w_down)
    gathered = shards
    totals = None
    outputs = []
    input_grads = []
    for micro_step in range(micro):
        gathered = fetch_each(shards)
        columns, chooser = item_columns(gathered[2].astype(jnp.float32), head_of)
        item_len = jnp.sum(jnp.where(row_match, lengths[micro_step][None, :], 0), axis=1)
        valid = jnp.arange(seq_len)[None, :] < item_len[:, None]
        tokens_now = tokens[micro_step].astype(jnp.float32)
        gain_first = gathered[0].astype(jnp.float32)
        gain_second = gathered[1].astype(jnp.float32)
        normed = rms_scale(tokens_now, gain_first).astype(jnp.bfloat16)

        def project(weight):
            made = jnp.einsum("rld,de->lre", normed, weight, preferred_element_type=jnp.float32)
            return made.astype(jnp.bfloat16).reshape(local, rows * inner)

        moved = (
            lax.all_to_all(project(gathered[3]), "seq", split_axis=1, concat_axis=0, tiled=True),
            lax.all_to_all(project(gathered[4]), "seq", split_axis=1, concat_axis=0, tiled=True),
            lax.all_to_all(project(gathered[5]), "seq", split_axis=1, concat_axis=0, tiled=True),
        )
        query = moved[0].reshape(seq_len, count, head_dim)
        key = moved[1].reshape(seq_len, count, head_dim)
        value = moved[2].reshape(seq_len, count, head_dim)
        mixed, lses = attend(query, key, value, buckets, columns, valid, block)
        mixed_tok = lax.all_to_all(mixed, "seq", split_axis=0, concat_axis=1, tiled=True).reshape(
            local, rows, inner
        )
        resid = tokens_now + jnp.einsum(
            "lre,ed->rld", mixed_tok, gathered[6], preferred_element_type=jnp.float32
        )
        normed_two = rms_scale(resid, gain_second).astype(jnp.bfloat16)
        gate = jnp.einsum(
            "rld,df->rlf", normed_two, gathered[7], preferred_element_type=jnp.float32
        )
        up = jnp.einsum("rld,df->rlf", normed_two, gathered[8], preferred_element_type=jnp.float32)
        hidden = gated(gate, up).astype(jnp.bfloat16)
        result = resid + jnp.einsum(
            "rlf,fd->rld", hidden, gathered[9], preferred_element_type=jnp.float32
        )
        outputs.append(result.astype(jnp.bfloat16))
        gathered = fetch_each(shards)
        grad_result = cotangent[micro_step].astype(jnp.float32)
        down_in = grad_result.astype(jnp.bfloat16)
        grad_down = jnp.einsum("rlf,rld->fd", hidden, down_in, preferred_element_type=jnp.float32)
        grad_hidden = jnp.einsum(
            "rld,fd->rlf", down_in, gathered[9], preferred_element_type=jnp.float32
        )
        unused, pull_gate = jax.vjp(gated, gate, up)
        grad_gate_in, grad_up_in = pull_gate(grad_hidden)
        grad_gate_in = grad_gate_in.astype(jnp.bfloat16)
        grad_up_in = grad_up_in.astype(jnp.bfloat16)
        grad_gate = jnp.einsum(
            "rld,rlf->df", normed_two, grad_gate_in, preferred_element_type=jnp.float32
        )
        grad_up = jnp.einsum(
            "rld,rlf->df", normed_two, grad_up_in, preferred_element_type=jnp.float32
        )
        grad_normed_two = jnp.einsum(
            "rlf,df->rld", grad_gate_in, gathered[7], preferred_element_type=jnp.float32
        )
        grad_normed_two = grad_normed_two + jnp.einsum(
            "rlf,df->rld", grad_up_in, gathered[8], preferred_element_type=jnp.float32
        )
        unused, pull_two = jax.vjp(rms_scale, resid, gain_second)
        grad_resid, grad_gain_two = pull_two(grad_normed_two)
        grad_resid = grad_result + grad_resid
        attn_in = grad_resid.astype(jnp.bfloat16)
        grad_out = jnp.einsum("lre,rld->ed", mixed_tok, attn_in, preferred_element_type=jnp.float32)
        grad_mixed = jnp.einsum(
            "rld,ed->lre", attn_in, gathered[6], preferred_element_type=jnp.float32
        )
        grad_mixed = grad_mixed.astype(jnp.bfloat16).reshape(local, rows * inner)
        grad_mixed = lax.all_to_all(
            grad_mixed, "seq", split_axis=1, concat_axis=0, tiled=True
        ).reshape(seq_len, count, head_dim)
        grad_q, grad_k, grad_v, grad_bias = attend_back(
            query, key, value, grad_mixed, lses, buckets, columns, valid, block
        )
        grad_table = jnp.dot(grad_bias.T, chooser, precision=highest)
        returned = (
            lax.all_to_all(grad_q, "seq", split_axis=0, concat_axis=1, tiled=True),
            lax.all_to_all(grad_k, "seq", split_axis=0, concat_axis=1, tiled=True),
            lax.all_to_all(grad_v, "seq", split_axis=0, concat_axis=1, tiled=True),
        )
        query_tok = returned[0].reshape(local, rows, inner)
        key_tok = returned[1].reshape(local, rows, inner)
        value_tok = returned[2].reshape(local, rows, inner)
        grad_query = jnp.einsum(
            "rld,lre->de", normed, query_tok, preferred_element_type=jnp.float32
        )
        grad_key = jnp.einsum("rld,lre->de", normed, key_tok, preferred_element_type=jnp.float32)
        grad_value = jnp.einsum(
            "rld,lre->de", normed, value_tok, preferred_element_type=jnp.float32
        )
        grad_normed = jnp.einsum(
            "lre,de->rld", query_tok, gathered[3], preferred_element_type=jnp.float32
        )
        grad_normed = grad_normed + jnp.einsum(
            "lre,de->rld", key_tok, gathered[4], preferred_element_type=jnp.float32
        )
        grad_normed = grad_normed + jnp.einsum(
            "lre,de->rld", value_tok, gathered[5], preferred_element_type=jnp.float32
        )
        unused, pull_one = jax.vjp(rms_scale, tokens_now, gain_first)
        grad_tokens, grad_gain_one = pull_one(grad_normed)
        input_grads.append(grad_resid + grad_tokens)
        local_grads = (
            grad_gain_one,
            grad_gain_two,
            grad_table,
            grad_query,
            grad_key,
            grad_value,
            grad_out,
            grad_gate,
            grad_up,
            grad_down,
        )
        reduced = reduce_each(local_grads)
        totals = reduced if totals is None else jax.tree.map(jnp.add, totals, reduced)
    return (
        jnp.stack(outputs),
        jnp.stack(input_grads),
        totals[0],
        totals[1],
        totals[2],
        totals[3],
        totals[4],
        totals[5],
        totals[6],
        totals[7],
        totals[8],
        totals[9],
    )


def solution(mesh):
    return jax.shard_map(
        body,
        mesh=mesh,
        in_specs=(
            P(None, "dp", "seq", None),
            P(None, "dp", "seq", None),
            P(None, "dp"),
            P(),
            P("dp"),
            P("dp"),
            P("dp", None),
            P("dp", None),
            P("dp", None),
            P("dp", None),
            P(None, "dp"),
            P("dp", None),
            P("dp", None),
            P(None, "dp"),
        ),
        out_specs=(
            P(None, "dp", "seq", None),
            P(None, "dp", "seq", None),
            P("dp"),
            P("dp"),
            P("dp", None),
            P("dp", None),
            P("dp", None),
            P("dp", None),
            P(None, "dp"),
            P("dp", None),
            P("dp", None),
            P(None, "dp"),
        ),
        check_vma=False,
    )
```

profile of v0, /device:TPU:0, one launch (start us, length us, event | category | flops | bytes accessed | tf_op | source)
XLA Modules:
  0.0 3273.7 jit_solution(31756992329698726)
XLA Ops:
  13.0 23.4 all-reduce.8
  37.7 27.7 all-gather.9.cloned.1.call-done
  92.6 18.2 all-gather
  129.1 42.1 %all-gather.13.cloned.1.call-done = bf16[1536,768]{1,0:T(8,128)(2,1)} async-done(((bf16[192,768]{1,0:T(8,128)(2,1)}), bf16[1536,768]{1,0:T(8,128)(2,1)}) %all-gather.13.cloned.1.call-update) | async-done | bytes 2359312 | tf_op jit(solution)/shard_map/all_gather | solution.py:26
  220.1 90.6 %while.76 = (s32[]{:T(128)}, bf16[2,512,6,64]{1,3,2,0:T(8,128)(2,1)}, f32[2,6,512]{2,1,0:T(8,128)S(1)}, s32[2]{0:T(128)S(1)}, bf16[1024,6,64]{0,2,1:T(8,128)(2,1...) while((s32[]{:T(128)}, ...), condition=%wide.region_5.6_spmd.clone, body=%wide.region_2.5_spmd.clone.sunk | while | flops 1048778240 | bytes 103197464 | solution.py:100
  228.8 12.6 fusion.404
  243.4 14.7 fusion.405
  273.9 12.6 fusion.404
  288.5 14.7 fusion.405
  327.8 90.7 %while.77 = (s32[]{:T(128)}, bf16[2,512,6,64]{1,3,2,0:T(8,128)(2,1)}, f32[2,6,512]{2,1,0:T(8,128)S(1)}, s32[2]{0:T(128)S(1)}, bf16[1024,6,64]{0,2,1:T(8,128)(2,1...) while((s32[]{:T(128)}, ...), condition=%wide.region_12.13_spmd.clone, body=%wide.region_9.12_spmd.clone.sunk | while | flops 1048778240 | bytes 103197464 | solution.py:100
  336.6 12.6 fusion.411
  351.1 14.7 fusion.412
  381.6 12.6 fusion.411
  396.2 14.7 fusion.412
  450.6 11.6 fusion.108
  462.2 105.9 %all-gather.19.cloned.1.call-done = bf16[1536,3968]{1,0:T(8,128)(2,1)} async-done(((bf16[192,3968]{1,0:T(8,128)(2,1)}), bf16[1536,3968]{1,0:T(8,128)(2,1)}) %all-gather.19.cloned.1.call-update) | async-done | bytes 12189712 | tf_op jit(solution)/shard_map/all_gather | solution.py:29
  568.1 13.6 fusion.120
  581.7 158.4 %all-gather.17.cloned.1.call-done = bf16[1536,3968]{1,0:T(8,128)(2,1)} async-done(((bf16[192,3968]{1,0:T(8,128)(2,1)}), bf16[1536,3968]{1,0:T(8,128)(2,1)}) %all-gather.17.cloned.1.call-update) | async-done | bytes 12189712 | tf_op jit(solution)/shard_map/all_gather | solution.py:28
  740.1 19.9 fusion.136
  760.0 12.3 fusion.116
  772.3 14.6 multiply_reduce_fusion.3
  787.0 12.4 fusion.106
  799.3 11.7 fusion.118
  811.0 20.2 fusion.143
  831.2 10.6 fusion.114
  841.9 12.1 multiply_reduce_fusion.2
  899.3 318.6 %while.78 = (s32[]{:T(128)}, f32[1024,6,64]{0,2,1:T(8,128)}, f32[1024,6,64]{0,2,1:T(8,128)}, f32[6,32]{1,0:T(8,128)S(1)}, bf16[2,512,6,64]{1,3,2,0:T(8,128)(2,1)...) while((s32[]{:T(128)}, f32[1024,6,64]{0,2,1:T(8,128)}, ...), condition=%wide.region_17.18_spmd.clone, body=%wide.region_15.17_spmd.clone.sunk | while | flops 3489339392 | bytes 367249984 | solution.py:143
  921.9 12.6 fusion.427
  934.5 15.9 copy.341
  950.5 15.1 multiply_reduce_fusion.10
  967.1 10.5 subtract_multiply_fusion.4
  989.3 16.2 copy.342
  1005.5 37.1 %fusion.428 = f32[6,32]{1,0:T(8,128)S(1)} fusion(f32[6,512,1024]{1,0,2:T(8,128)} %copy.342, s32[512,1024]{0,1:T(8,128)S(1)} %copy-done.3, f32[6,32]{1,0:T(8,128)S(1)} %get-tuple-element.1762, pred[]{:T(512)S(6)} %compare.6), kind=kOutput, calls=%fused_computation.65.clone.1 | convolution fusion | flops 1224737152 | bytes 14681601 | tf_op jit(solution)/shard_map/while/body/eval_jaxpr/iqk,qkb->ib/dot_general | solution.py:128
  1070.7 12.6 fusion.427
  1083.3 15.8 copy.341
  1099.2 14.7 multiply_reduce_fusion.10
  1115.6 10.5 subtract_multiply_fusion.4
  1139.3 16.2 copy.342
  1155.5 37.1 %fusion.428 = f32[6,32]{1,0:T(8,128)S(1)} fusion(f32[6,512,1024]{1,0,2:T(8,128)} %copy.342, s32[512,1024]{0,1:T(8,128)S(1)} %copy-done.3, f32[6,32]{1,0:T(8,128)S(1)} %get-tuple-element.1762, pred[]{:T(512)S(6)} %compare.6), kind=kOutput, calls=%fused_computation.65.clone.1 | convolution fusion | flops 1224737152 | bytes 14681601 | tf_op jit(solution)/shard_map/while/body/eval_jaxpr/iqk,qkb->ib/dot_general | solution.py:128
  1227.0 308.5 %while.79 = (s32[]{:T(128)}, f32[1024,6,64]{0,2,1:T(8,128)}, f32[1024,6,64]{0,2,1:T(8,128)}, f32[6,32]{1,0:T(8,128)S(1)}, bf16[2,512,6,64]{1,3,2,0:T(8,128)(2,1)...) while((s32[]{:T(128)}, f32[1024,6,64]{0,2,1:T(8,128)}, ...), condition=%wide.region_22.23_spmd.clone, body=%wide.region_20.22_spmd.clone.sunk | while | flops 3489339392 | bytes 360958464 | solution.py:143
  1248.4 12.6 fusion.442
  1261.0 15.8 copy.344
  1276.9 14.7 multiply_reduce_fusion.11
  1315.2 16.2 copy.345
  1331.4 37.1 %fusion.443 = f32[6,32]{1,0:T(8,128)S(1)} fusion(f32[6,512,1024]{1,0,2:T(8,128)} %copy.345, s32[512,1024]{0,1:T(8,128)S(1)} %copy-done.5, f32[6,32]{1,0:T(8,128)S(1)} %get-tuple-element.1702, pred[]{:T(512)S(6)} %compare.7), kind=kOutput, calls=%fused_computation.103.clone.1 | convolution fusion | flops 1224737152 | bytes 14681601 | tf_op jit(solution)/shard_map/while/body/eval_jaxpr/iqk,qkb->ib/dot_general | solution.py:128
  1397.5 12.6 fusion.442
  1410.1 15.8 copy.344
  1425.9 14.7 multiply_reduce_fusion.11
  1466.1 16.2 copy.345
  1482.3 37.1 %fusion.443 = f32[6,32]{1,0:T(8,128)S(1)} fusion(f32[6,512,1024]{1,0,2:T(8,128)} %copy.345, s32[512,1024]{0,1:T(8,128)S(1)} %copy-done.5, f32[6,32]{1,0:T(8,128)S(1)} %get-tuple-element.1702, pred[]{:T(512)S(6)} %compare.7), kind=kOutput, calls=%fused_computation.103.clone.1 | convolution fusion | flops 1224737152 | bytes 14681601 | tf_op jit(solution)/shard_map/while/body/eval_jaxpr/iqk,qkb->ib/dot_general | solution.py:128
  1655.6 14.6 fusion.304
  1670.2 17.7 bitcast_add_fusion.10
  1688.0 14.6 fusion.305
  1702.6 17.9 bitcast_add_fusion.9
  1720.5 14.0 fusion.216
  1734.6 18.0 bitcast_add_fusion.8
  1753.9 12.4 fusion.185
  1766.4 11.2 fusion.182
  1777.6 78.9 %reduce-scatter.12.cloned.1.call-done = f32[192,768]{1,0:T(8,128)} async-done(((f32[1536,768]{1,0:T(8,128)}), f32[192,768]{1,0:T(8,128)}) %reduce-scatter.12.cloned.1.call-update) | async-done | bytes 589840 | tf_op jit(solution)/shard_map/reduce_scatter | solution.py:41
  1856.5 396.0 %reduce-scatter.16.cloned.1.call-done = f32[192,3968]{1,0:T(8,128)} async-done(((f32[1536,3968]{1,0:T(8,128)}), f32[192,3968]{1,0:T(8,128)}) %reduce-scatter.16.cloned.1.call-update) | async-done | bytes 3047440 | tf_op jit(solution)/shard_map/reduce_scatter | solution.py:43
  2252.6 395.5 %reduce-scatter.18.cloned.1.call-done = f32[192,3968]{1,0:T(8,128)} async-done(((f32[1536,3968]{1,0:T(8,128)}), f32[192,3968]{1,0:T(8,128)}) %reduce-scatter.18.cloned.1.call-update) | async-done | bytes 3047440 | tf_op jit(solution)/shard_map/reduce_scatter | solution.py:44
  2648.1 395.4 %reduce-scatter.20.cloned.1.call-done = f32[3968,192]{0,1:T(8,128)} async-done(((f32[3968,1536]{0,1:T(8,128)}), f32[3968,192]{0,1:T(8,128)}) %reduce-scatter.20.cloned.1.call-update) | async-done | bytes 3047440 | tf_op jit(solution)/shard_map/reduce_scatter | solution.py:45
  3067.2 35.0 %all-reduce.5 = (f32[1536]{0:T(1024)S(1)}, f32[1536]{0:T(1024)S(1)}, f32[32,12]{1,0:T(8,128)S(1)}) all-reduce(f32[1536]{0:T(1024)S(1)} %add.561, f32[1536]{0:T(1024)S(1)} %add.562, f32[32,12]{1,0:T(8,128)S(1)} %convolution_add_fusion.4), channel_id=12, replica_groups=mesh['dp'=8,'seq'=4] {'dp'}, use_global_device_ids=true, to_apply=%region_25.26.clone | all-reduce | flops 3456 | bytes 27648
  3117.9 133.7 %all-reduce.11.cloned.1.call-done = (f32[192,768]{1,0:T(8,128)}, f32[192,768]{1,0:T(8,128)}, f32[192,768]{1,0:T(8,128)}, f32[768,192]{0,1:T(8,128)}, f32[192,396...) async-done(((f32[192,768]{1,0:T(8,128)}, f32[192,768]{1,0:T(8,128)}, f32[192,768]{1,0:T(8,128)}, f32[768,192]{0,1:T(8,128)}, f32[192,3968]{1,0:T(8,128)}, ...) | async-done | bytes 11501584 | tf_op jit(solution)/shard_map/psum | solution.py:47
  (599 shorter events, 614.9 us)
Async XLA Ops:
  7.2 29.2 copy-start.14
  7.2 58.1 %all-gather.9.cloned.1.call-start = ((), (), s32[]{:S(2)}) async-start(), calls=%async_computation.23 | async-start | bytes 2654208 | tf_op jit(solution)/shard_map/all_gather | solution.py:24
  8.0 110.4 %all-gather.11.cloned.1.call-start = ((), (), s32[]{:S(2)}) async-start(), calls=%async_computation.24 | async-start | bytes 2654208 | tf_op jit(solution)/shard_map/all_gather | solution.py:25
  8.7 162.5 %all-gather.13.cloned.1.call-start = ((), (), s32[]{:S(2)}) async-start(), calls=%async_computation.25 | async-start | bytes 2654208 | tf_op jit(solution)/shard_map/all_gather | solution.py:26
  9.4 421.8 %all-gather.15.cloned.1.call-start = ((), (), s32[]{:S(2)}) async-start(), calls=%async_computation.26 | async-start | bytes 2654208 | tf_op jit(solution)/shard_map/all_gather | solution.py:27
  10.0 439.6 %all-gather.21.cloned.1.call-start = ((), (), s32[]{:S(2)}) async-start(), calls=%async_computation.29 | async-start | bytes 13713408 | tf_op jit(solution)/shard_map/all_gather | solution.py:30
  10.6 557.5 %all-gather.19.cloned.1.call-start = ((), (), s32[]{:S(2)}) async-start(), calls=%async_computation.28 | async-start | bytes 13713408 | tf_op jit(solution)/shard_map/all_gather | solution.py:29
  36.4 162.6 %copy-start.65 = (f32[1536]{0:T(1024)}, f32[1536]{0:T(1024)S(1)}, u32[]{:S(2)}) copy-start(f32[1536]{0:T(1024)S(1)} %convert_element_type.251) | copy-start | bytes 18436
  37.1 38.7 %copy-start.74 = (f32[2,256]{1,0:T(2,128)}, f32[2,256]{1,0:T(2,128)S(1)}, u32[]{:S(2)}) copy-start(f32[2,256]{1,0:T(2,128)S(1)} %get-tuple-element.1128) | copy-start | bytes 6148
  37.7 161.3 %copy-start.72 = (f32[2,256]{1,0:T(2,128)}, f32[2,256]{1,0:T(2,128)S(1)}, u32[]{:S(2)}) copy-start(f32[2,256]{1,0:T(2,128)S(1)} %fusion.283) | copy-start | bytes 6148
  71.6 15.9 all-to-all-start.4
  75.9 95.3 %copy-start.78 = (f32[2,256]{1,0:T(2,128)}, f32[2,256]{1,0:T(2,128)S(1)}, u32[]{:S(2)}) copy-start(f32[2,256]{1,0:T(2,128)S(1)} %fusion.281) | copy-start | bytes 6148
  87.6 37.1 %all-to-all-start = ((bf16[256,4,384]{0,2,1:T(8,128)(2,1)}), bf16[256,4,384]{0,2,1:T(8,128)(2,1)}, u32[]{:S(2)}, u32[]{:S(2)}) async-start(bf16[256,4,384]{0,2,1:T(8,128)(2,1)} %bitcast.539), calls=%async_computation | async-start | bytes 1572864 | tf_op jit(solution)/shard_map/all_to_all | solution.py:204
  91.8 648.3 %all-gather.17.cloned.1.call-start = ((), (), s32[]{:S(2)}) async-start(), calls=%async_computation.27 | async-start | bytes 13713408 | tf_op jit(solution)/shard_map/all_gather | solution.py:28
  110.8 18.1 copy-start.99
  124.6 52.9 %all-to-all-start.1 = ((bf16[256,4,384]{0,2,1:T(8,128)(2,1)}), bf16[256,4,384]{0,2,1:T(8,128)(2,1)}, u32[]{:S(2)}, u32[]{:S(2)}) async-start(bf16[256,4,384]{0,2,1:T(8,128)(2,1)} %bitcast.541), calls=%async_computation.1 | async-start | bytes 1572864 | tf_op jit(solution)/shard_map/all_to_all | solution.py:205
  177.5 15.9 all-to-all-start.2
  193.4 21.6 all-to-all-start.5
  215.0 102.3 %all-to-all-start.6 = ((bf16[256,4,384]{0,2,1:T(8,128)(2,1)}), bf16[256,4,384]{0,2,1:T(8,128)(2,1)}, u32[]{:S(2)}, u32[]{:S(2)}) async-start(bf16[256,4,384]{0,2,1:T(8,128)(2,1)} %bitcast.36), calls=%async_computation.6 | async-start | bytes 1572864 | tf_op jit(solution)/shard_map/all_to_all | solution.py:206
  322.6 104.4 %all-to-all-start.3 = ((bf16[4,256,384]{1,2,0:T(8,128)(2,1)}), bf16[4,256,384]{1,2,0:T(8,128)(2,1)}, u32[]{:S(2)}, u32[]{:S(2)}) async-start(bf16[4,256,384]{1,2,0:T(8,128)(2,1)} %copy.251), calls=%async_computation.3 | async-start | bytes 1572864 | tf_op jit(solution)/shard_map/all_to_all | solution.py:212
  427.0 15.9 all-to-all-start.7
  462.2 277.9 %copy-start.58 = (bf16[2,256,1536]{2,1,0:T(8,128)(2,1)S(1)}, bf16[2,256,1536]{2,1,0:T(8,128)(2,1)}, u32[]{:S(2)}) copy-start(bf16[2,256,1536]{2,1,0:T(8,128)(2,1)} %multiply_convert_fusion.5) | copy-start | bytes 4718596
  786.9 24.1 copy-start.36
  857.9 26.9 copy-start.22
  864.1 15.9 all-to-all-start.12
  880.0 15.9 all-to-all-start.8
  884.3 893.3 %reduce-scatter.14.cloned.1.call-start = ((), (), s32[]{:S(2)}) async-start(), calls=%async_computation.33 | async-start | bytes 5308416 | tf_op jit(solution)/shard_map/reduce_scatter | solution.py:42
  934.5 16.0 copy-start.9
  950.4 15.2 slice-start
  950.5 15.2 slice-start.1
  950.5 16.6 slice-start.2
  989.3 16.2 copy-start.3
  1005.5 37.1 %copy-start.47 = (bf16[2,512,6,64]{1,3,2,0:T(8,128)(2,1)S(1)}, bf16[2,512,6,64]{1,3,2,0:T(8,128)(2,1)}, u32[]{:S(2)}) copy-start(bf16[2,512,6,64]{1,3,2,0:T(8,128)(2,1)} %get-tuple-element.1763) | copy-start | bytes 2359300 | tf_op jit(solution)/shard_map/while
  1083.3 15.9 copy-start.9
  1099.1 14.8 slice-start
  1099.2 16.4 slice-start.2
  1139.3 16.2 copy-start.3
  1155.5 37.1 %copy-start.47 = (bf16[2,512,6,64]{1,3,2,0:T(8,128)(2,1)S(1)}, bf16[2,512,6,64]{1,3,2,0:T(8,128)(2,1)}, u32[]{:S(2)}) copy-start(bf16[2,512,6,64]{1,3,2,0:T(8,128)(2,1)} %get-tuple-element.1763) | copy-start | bytes 2359300 | tf_op jit(solution)/shard_map/while
  1221.8 322.2 %all-to-all-start.9 = ((bf16[4,256,384]{1,2,0:T(8,128)(2,1)}), bf16[4,256,384]{1,2,0:T(8,128)(2,1)}, u32[]{:S(2)}, u32[]{:S(2)}) async-start(bf16[4,256,384]{1,2,0:T(8,128)(2,1)} %copy.265), calls=%async_computation.9 | async-start | bytes 1572864 | tf_op jit(solution)/shard_map/all_to_all | solution.py:268
  1261.0 15.9 copy-start.7
  1276.8 14.8 slice-start.3
  1276.9 16.4 slice-start.5
  1315.2 16.2 copy-start.5
  1331.4 37.1 %copy-start.45 = (bf16[2,512,6,64]{1,3,2,0:T(8,128)(2,1)S(1)}, bf16[2,512,6,64]{1,3,2,0:T(8,128)(2,1)}, u32[]{:S(2)}) copy-start(bf16[2,512,6,64]{1,3,2,0:T(8,128)(2,1)} %get-tuple-element.1703) | copy-start | bytes 2359300 | tf_op jit(solution)/shard_map/while
  1410.1 15.9 copy-start.7
  1425.9 14.8 slice-start.3
  1425.9 16.4 slice-start.5
  1466.1 16.2 copy-start.5
  1482.3 37.1 %copy-start.45 = (bf16[2,512,6,64]{1,3,2,0:T(8,128)(2,1)S(1)}, bf16[2,512,6,64]{1,3,2,0:T(8,128)(2,1)}, u32[]{:S(2)}) copy-start(bf16[2,512,6,64]{1,3,2,0:T(8,128)(2,1)} %get-tuple-element.1703) | copy-start | bytes 2359300 | tf_op jit(solution)/shard_map/while
  1544.0 15.9 all-to-all-start.13
  1548.2 229.4 %reduce-scatter.8.cloned.1.call-start = ((), (), s32[]{:S(2)}) async-start(), calls=%async_computation.30 | async-start | bytes 5308416 | tf_op jit(solution)/shard_map/reduce_scatter | solution.py:39
  1571.7 15.9 all-to-all-start.10
  1576.9 15.0 copy-start.17
  1587.6 15.9 all-to-all-start.14
  1591.8 185.8 %reduce-scatter.10.cloned.1.call-start = ((), (), s32[]{:S(2)}) async-start(), calls=%async_computation.31 | async-start | bytes 5308416 | tf_op jit(solution)/shard_map/reduce_scatter | solution.py:40
  1617.3 15.9 all-to-all-start.11
  1633.2 15.9 all-to-all-start.15
  1637.4 219.1 %reduce-scatter.12.cloned.1.call-start = ((), (), s32[]{:S(2)}) async-start(), calls=%async_computation.32 | async-start | bytes 5308416 | tf_op jit(solution)/shard_map/reduce_scatter | solution.py:41
  1655.6 597.0 %reduce-scatter.16.cloned.1.call-start = ((), (), s32[]{:S(2)}) async-start(), calls=%async_computation.34 | async-start | bytes 27426816 | tf_op jit(solution)/shard_map/reduce_scatter | solution.py:43
  1688.0 960.1 %reduce-scatter.18.cloned.1.call-start = ((), (), s32[]{:S(2)}) async-start(), calls=%async_computation.35 | async-start | bytes 27426816 | tf_op jit(solution)/shard_map/reduce_scatter | solution.py:44
  1720.5 1323.0 %reduce-scatter.20.cloned.1.call-start = ((), (), s32[]{:S(2)}) async-start(), calls=%async_computation.36 | async-start | bytes 27426816 | tf_op jit(solution)/shard_map/reduce_scatter | solution.py:45
  1752.6 1499.0 %all-reduce.11.cloned.1.call-start = ((), (), s32[]{:S(2)}) async-start(), calls=%async_computation.37 | async-start | bytes 23003136 | tf_op jit(solution)/shard_map/psum | solution.py:47
  3062.2 46.9 %copy-start.75 = (f32[2,256]{1,0:T(2,128)S(1)}, f32[2,256]{1,0:T(2,128)}, u32[]{:S(2)}) copy-start(f32[2,256]{1,0:T(2,128)} %copy-done.74) | copy-start | bytes 6148
  3062.2 46.9 %copy-start.77 = (f32[2,256]{1,0:T(2,128)S(1)}, f32[2,256]{1,0:T(2,128)}, u32[]{:S(2)}) copy-start(f32[2,256]{1,0:T(2,128)} %copy-done.76) | copy-start | bytes 6148
  (109 other events, 800.5 us)
Sparse Core Ops, SparseCore 0:
  10.2 55.0 all-gather.8
  67.6 50.7 all-gather.10
  120.6 50.6 all-gather.12
  173.2 50.6 all-gather.14
  225.9 170.1 all-gather.20
  398.2 169.8 all-gather.18
  570.3 169.8 all-gather.16
  892.3 93.8 reduce-scatter.13
  1566.4 92.7 reduce-scatter.7
  1662.7 95.0 reduce-scatter.9
  1761.4 95.0 reduce-scatter.11
  1860.3 392.2 reduce-scatter.15
  2256.5 391.5 reduce-scatter.17
  2651.9 391.5 reduce-scatter.19
  3046.6 204.9 all-reduce.10
where the time goes:
time: 3290 us; the launch traced here: 3270 us
  waiting for transfers between devices  1800 us (55%)
  matrix products  839 us (26%)
  local copies, waits for them, and re-layouts  328 us (10%)
  blocking collectives  83.4 us (3%)
  other arithmetic  82.1 us (2%)
  starting transfers between devices  68.5 us (2%)
  loops' own time  55.9 us (2%)
    reduce_scatter x1, waiting for transfers between devices, reduce_each(): lax.psum_scatter(grads[7], 'dp', scatter_dimension=0, tiled=True)  396 us
    reduce_scatter x1, waiting for transfers between devices, reduce_each(): lax.psum_scatter(grads[8], 'dp', scatter_dimension=0, tiled=True)  396 us
    reduce_scatter x1, waiting for transfers between devices, reduce_each(): lax.psum_scatter(grads[9], 'dp', scatter_dimension=1, tiled=True)  395 us
    all_gather x1, waiting for transfers between devices, fetch_each(): lax.all_gather(shards[7], 'dp', axis=0, tiled=True)  158 us
    dot_general x4, matrix products, one_block(): jnp.einsum('iqk,qkb->ib', grad_scores, onehot.astype(jnp.float32), precis...  149 us
    psum x1, waiting for transfers between devices, reduce_each(): lax.psum((summed[0], summed[1], summed[2], summed[3], summed[4], summed[5...  134 us
    dot_general x8, matrix products, one_block(): jnp.einsum('qie,kie->iqk', query_block, key, preferred_element_type=jnp.f...  118 us
    all_gather x1, waiting for transfers between devices, fetch_each(): lax.all_gather(shards[8], 'dp', axis=0, tiled=True)  106 us
  transfers between devices with their start and end apart: 31, of which 20 were waited for; matrix products, arithmetic and copies ran while one was open for 33% of the time, Pallas kernels for 0%

commit v1 on v0

v1 whole, which is shorter than its diff:
```python
import functools

import jax
import jax.numpy as jnp
from jax import lax
from jax.experimental import pallas as pl
from jax.experimental.pallas import tpu as pltpu
from jax.sharding import PartitionSpec as P

eps = 1e-06
masked_value = -1e30
highest = lax.Precision.HIGHEST
gelu_scale = 0.7978845608028654
gelu_cubic = 0.044715
LANES = 128
VMEM_LIMIT = 56 * 1024 * 1024
NT = (((1,), (1,)), ((), ()))
NN = (((1,), (0,)), ((), ()))
TN = (((0,), (0,)), ((), ()))


def dot32(a, b, dims):
    return lax.dot_general(a, b, dims, preferred_element_type=jnp.float32)


def toeplitz_strip(diag_row, span):
    wide = jnp.broadcast_to(diag_row, (LANES, span))
    return pltpu.roll(wide, span - (LANES - 1), 1, stride=1, stride_axis=0)


def with_mask_lane(key_pair, lanes, here, spare, length):
    rows = lax.broadcasted_iota(jnp.int32, key_pair.shape, 0)
    mask = jnp.where(rows < length, 0.0, masked_value).astype(key_pair.dtype)
    zero = jnp.zeros_like(key_pair)
    return jnp.where(here, key_pair, jnp.where(lanes == spare, mask, zero))


def attend_kernel(head_dim, block, len_ref, diag_ref, q_ref, k_ref, v_ref, mixed_ref, lse_ref, strip, keys):
    step = pl.program_id(1)
    seq_len = k_ref.shape[0]
    span = diag_ref.shape[-1]
    length = len_ref[0]
    per = LANES // head_dim
    lanes_k = lax.broadcasted_iota(jnp.int32, (seq_len, LANES), 1)
    lanes_q = lax.broadcasted_iota(jnp.int32, (block, LANES), 1)

    @pl.when(step == 0)
    def _():
        for head in range(per):
            strip[head] = toeplitz_strip(diag_ref[head], span)
            here = lanes_k // head_dim == head
            spare = ((head + 1) % per) * head_dim
            keys[head] = with_mask_lane(k_ref[...], lanes_k, here, spare, length)

    mixed = None
    for head in range(per):
        here = lanes_q // head_dim == head
        spare = ((head + 1) % per) * head_dim
        one = (lanes_q == spare).astype(q_ref.dtype)
        query = jnp.where(here, q_ref[...], one)
        raw = dot32(query, keys[head], NT)
        parts = []
        for sub in range(block // LANES):
            offset = seq_len - LANES - (step * block + sub * LANES)
            offset = pl.multiple_of(offset, LANES)
            parts.append(raw[sub * LANES : (sub + 1) * LANES] + strip[head, :, pl.ds(offset, seq_len)])
        scores = jnp.concatenate(parts, axis=0)
        top = jnp.max(scores, axis=1, keepdims=True)
        expo = jnp.exp(scores - top)
        total = jnp.sum(expo, axis=1, keepdims=True)
        made = dot32(expo.astype(jnp.bfloat16), v_ref[...], NN) / total
        mixed = made if mixed is None else jnp.where(here, made, mixed)
        lse = jnp.broadcast_to(top + jnp.log(total), (block, LANES))
        lse_ref[head] = lse.T[:1]
    mixed_ref[...] = mixed.astype(mixed_ref.dtype)


def attend(qkv, diag, length, head_dim, block=256):
    seq_len, cols = qkv.shape[0], qkv.shape[1] // 3
    pairs = cols // LANES
    per = LANES // head_dim
    span = diag.shape[-1]
    flops = 2 * 2 * seq_len * seq_len * LANES * 2 * cols // head_dim
    return pl.pallas_call(
        functools.partial(attend_kernel, head_dim, block),
        grid=(pairs, seq_len // block),
        in_specs=[
            pl.BlockSpec(memory_space=pltpu.SMEM),
            pl.BlockSpec((per, 1, span), lambda p, b: (p, 0, 0)),
            pl.BlockSpec((block, LANES), lambda p, b: (b, p)),
            pl.BlockSpec((seq_len, LANES), lambda p, b: (0, pairs + p)),
            pl.BlockSpec((seq_len, LANES), lambda p, b: (0, 2 * pairs + p)),
        ],
        out_specs=[
            pl.BlockSpec((block, LANES), lambda p, b: (b, p)),
            pl.BlockSpec((per, 1, block), lambda p, b: (p, 0, b)),
        ],
        out_shape=[
            jax.ShapeDtypeStruct((seq_len, cols), jnp.bfloat16),
            jax.ShapeDtypeStruct((cols // head_dim, 1, seq_len), jnp.float32),
        ],
        scratch_shapes=[
            pltpu.VMEM((per, LANES, span), jnp.float32),
            pltpu.VMEM((per, seq_len, LANES), jnp.bfloat16),
        ],
        compiler_params=pltpu.CompilerParams(vmem_limit_bytes=VMEM_LIMIT),
        cost_estimate=pl.CostEstimate(flops=flops, bytes_accessed=8 * seq_len * cols, transcendentals=0),
        name="attend",
    )(length, diag, qkv, qkv, qkv)


def attend_back_kernel(
    head_dim, block, len_ref, diag_ref, q_ref, k_ref, v_ref, do_ref, lse_ref,
    dq_ref, dk_ref, dv_ref, dd_ref, strip, keys, acc_bias, acc_k, acc_v,
):
    step = pl.program_id(1)
    steps = pl.num_programs(1)
    seq_len = k_ref.shape[0]
    span = diag_ref.shape[-1]
    length = len_ref[0]
    per = LANES // head_dim
    lanes_k = lax.broadcasted_iota(jnp.int32, (seq_len, LANES), 1)
    lanes_q = lax.broadcasted_iota(jnp.int32, (block, LANES), 1)
    subs = block // LANES

    @pl.when(step == 0)
    def _():
        for head in range(per):
            strip[head] = toeplitz_strip(diag_ref[head], span).T
            here = lanes_k // head_dim == head
            spare = ((head + 1) % per) * head_dim
            keys[head] = with_mask_lane(k_ref[...], lanes_k, here, spare, length)
        acc_bias[...] = jnp.zeros_like(acc_bias)
        acc_k[...] = jnp.zeros_like(acc_k)
        acc_v[...] = jnp.zeros_like(acc_v)

    grad_query = None
    for head in range(per):
        here = lanes_q // head_dim == head
        spare = ((head + 1) % per) * head_dim
        zero = jnp.zeros_like(q_ref[...])
        one = (lanes_q == spare).astype(q_ref.dtype)
        query = jnp.where(here, q_ref[...], zero)
        grad = jnp.where(here, do_ref[...], zero)
        raw = dot32(keys[head], query + one, NT)
        grad_probs = dot32(v_ref[...], grad, NT)
        parts = []
        offsets = []
        for sub in range(subs):
            offset = seq_len - LANES - (step * block + sub * LANES)
            offset = pl.multiple_of(offset, LANES)
            offsets.append(offset)
            parts.append(raw[:, sub * LANES : (sub + 1) * LANES] + strip[head, pl.ds(offset, seq_len), :])
        scores = jnp.concatenate(parts, axis=1)
        probs = jnp.exp(scores - lse_ref[head])
        product = probs * grad_probs
        inner = jnp.sum(product, axis=0, keepdims=True)
        grad_scores = product - probs * inner
        for sub in range(subs):
            rows = pl.ds(offsets[sub], seq_len)
            acc_bias[head, rows, :] += grad_scores[:, sub * LANES : (sub + 1) * LANES]
        rounded = grad_scores.astype(jnp.bfloat16)
        acc_v[...] += dot32(probs.astype(jnp.bfloat16), grad, NN)
        acc_k[...] += dot32(rounded, query, NN)
        made = dot32(rounded, k_ref[...], TN)
        grad_query = made if grad_query is None else jnp.where(here, made, grad_query)
    dq_ref[...] = grad_query.astype(dq_ref.dtype)

    @pl.when(step == steps - 1)
    def _():
        dk_ref[...] = acc_k[...].astype(dk_ref.dtype)
        dv_ref[...] = acc_v[...].astype(dv_ref.dtype)
        row = lax.broadcasted_iota(jnp.int32, (LANES, LANES), 0)
        col = lax.broadcasted_iota(jnp.int32, (LANES, LANES), 1)
        flip = (row + col == LANES - 1).astype(jnp.float32)
        for head in range(per):
            turned = lax.dot_general(
                flip, acc_bias[head], NT, precision=lax.Precision.HIGHEST, preferred_element_type=jnp.float32
            )
            aligned = pltpu.roll(turned, 0, 1, stride=1, stride_axis=0)
            dd_ref[head] = jnp.sum(aligned, axis=0, keepdims=True)


def attend_back(qkv, grad_mixed, lse, diag, length, head_dim, block=256):
    seq_len, cols = qkv.shape[0], qkv.shape[1] // 3
    pairs = cols // LANES
    per = LANES // head_dim
    span = diag.shape[-1]
    flops = 5 * 2 * seq_len * seq_len * LANES * 2 * cols // head_dim
    whole = lambda p, b: (0, p)
    part = lambda p, b: (b, p)
    flat = jax.ShapeDtypeStruct((seq_len, cols), jnp.bfloat16)
    return pl.pallas_call(
        functools.partial(attend_back_kernel, head_dim, block),
        grid=(pairs, seq_len // block),
        in_specs=[
            pl.BlockSpec(memory_space=pltpu.SMEM),
            pl.BlockSpec((per, 1, span), lambda p, b: (p, 0, 0)),
            pl.BlockSpec((block, LANES), part),
            pl.BlockSpec((seq_len, LANES), lambda p, b: (0, pairs + p)),
            pl.BlockSpec((seq_len, LANES), lambda p, b: (0, 2 * pairs + p)),
            pl.BlockSpec((block, LANES), part),
            pl.BlockSpec((per, 1, block), lambda p, b: (p, 0, b)),
        ],
        out_specs=[
            pl.BlockSpec((block, LANES), part),
            pl.BlockSpec((seq_len, LANES), whole),
            pl.BlockSpec((seq_len, LANES), whole),
            pl.BlockSpec((per, 1, span), lambda p, b: (p, 0, 0)),
        ],
        out_shape=[flat, flat, flat, jax.ShapeDtypeStruct(diag.shape, jnp.float32)],
        scratch_shapes=[
            pltpu.VMEM((per, span, LANES), jnp.float32),
            pltpu.VMEM((per, seq_len, LANES), jnp.bfloat16),
            pltpu.VMEM((per, span, LANES), jnp.float32),
            pltpu.VMEM((seq_len, LANES), jnp.float32),
            pltpu.VMEM((seq_len, LANES), jnp.float32),
        ],
        compiler_params=pltpu.CompilerParams(vmem_limit_bytes=VMEM_LIMIT),
        cost_estimate=pl.CostEstimate(flops=flops, bytes_accessed=16 * seq_len * cols, transcendentals=0),
        name="attend_back",
    )(length, diag, qkv, qkv, qkv, grad_mixed, lse)


def gated_kernel(width, a_ref, d_ref, g_ref, e_ref):
    gate = dot32(a_ref[...], g_ref[:, :width], NN)
    up = dot32(a_ref[...], g_ref[:, width : 2 * width], NN)
    grad = dot32(d_ref[...], g_ref[:, 2 * width :], NN)
    square = gate * gate
    inner = gelu_scale * gate * (1.0 + gelu_cubic * square)
    turn = jnp.tanh(inner)
    half = 0.5 * (1.0 + turn)
    act = gate * half
    slope = half + 0.5 * gate * (1.0 - turn * turn) * gelu_scale * (1.0 + 3.0 * gelu_cubic * square)
    e_ref[:, :width] = (grad * up * slope).astype(e_ref.dtype)
    e_ref[:, width : 2 * width] = (grad * act).astype(e_ref.dtype)
    e_ref[:, 2 * width :] = (act * up).astype(e_ref.dtype)


def gated_chunk(normed, down_in, weights, tile=256):
    tokens, width = normed.shape[0], weights.shape[1] // 3
    depth = normed.shape[1]
    return pl.pallas_call(
        functools.partial(gated_kernel, width),
        grid=(tokens // tile,),
        in_specs=[
            pl.BlockSpec((tile, depth), lambda t: (t, 0)),
            pl.BlockSpec((tile, depth), lambda t: (t, 0)),
            pl.BlockSpec((depth, 3 * width), lambda t: (0, 0)),
        ],
        out_specs=pl.BlockSpec((tile, 3 * width), lambda t: (t, 0)),
        out_shape=jax.ShapeDtypeStruct((tokens, 3 * width), jnp.bfloat16),
        compiler_params=pltpu.CompilerParams(vmem_limit_bytes=VMEM_LIMIT),
        cost_estimate=pl.CostEstimate(
            flops=6 * tokens * depth * width, bytes_accessed=2 * (2 * tokens * depth + 6 * depth * width), transcendentals=0
        ),
        name="gated_chunk",
    )(normed, down_in, weights)


def back_kernel(count, *refs):
    total = None
    for index in range(count):
        made = dot32(refs[index][...], refs[count + index][...], NT)
        total = made if total is None else total + made
    refs[-1][...] = total.astype(refs[-1].dtype)


def back_sum(pieces, weights, start, width, block_at, half, dtype, tile=256):
    count = len(pieces)
    rows, _, _ = pieces[0].shape
    depth = weights[0].shape[0]
    tile = min(tile, half)
    steps = half // tile

    def body_of(start_ref, *refs):
        back_kernel(count, *refs)

    return pl.pallas_call(
        body_of,
        grid_spec=pltpu.PrefetchScalarGridSpec(
            num_scalar_prefetch=1,
            grid=(rows, steps),
            in_specs=[pl.BlockSpec((None, tile, width), lambda r, t, s: (r, s[0] * steps + t, block_at))] * count
            + [pl.BlockSpec((depth, width), lambda r, t, s: (0, block_at))] * count,
            out_specs=pl.BlockSpec((None, tile, depth), lambda r, t, s: (r, t, 0)),
        ),
        out_shape=jax.ShapeDtypeStruct((rows, half, depth), dtype),
        compiler_params=pltpu.CompilerParams(vmem_limit_bytes=VMEM_LIMIT),
        cost_estimate=pl.CostEstimate(
            flops=2 * rows * half * depth * width * count,
            bytes_accessed=2 * count * width * (rows * half + depth) + 4 * rows * half * depth,
            transcendentals=0,
        ),
        name="back_sum",
    )(start, *pieces, *weights)


def ring_order(count):
    if count % 4 or count < 8:
        return list(range(count))
    long, short = 4, count // 4
    walk = []
    for line in range(long):
        columns = range(1, short) if line % 2 == 0 else range(short - 1, 0, -1)
        walk += [line * short + column for column in columns]
    return walk + [line * short for line in range(long - 1, -1, -1)]


class Ring:
    def __init__(self, count):
        order = ring_order(count)
        place = [0] * count
        for at, index in enumerate(order):
            place[index] = at
        self.count = count
        self.order = jnp.array(order, jnp.int32)
        self.here = jnp.array(place, jnp.int32)[lax.axis_index("dp")]
        self.ahead = [(order[i], order[(i + 1) % count]) for i in range(count)]
        self.behind = [(order[i], order[(i - 1) % count]) for i in range(count)]

    def owner(self, shift):
        return self.order[(self.here + shift) % self.count]

    def send(self, block, forward):
        return lax.ppermute(block, "dp", self.ahead if forward else self.behind)

    def gather(self, shard):
        rows, cols = shard.shape
        cut = cols // 2
        far = self.count // 2
        whole = jnp.zeros((self.count * rows, cols), shard.dtype)

        def put(whole, block, shift, column=0):
            return lax.dynamic_update_slice(whole, block, (self.owner(shift) * rows, column))

        whole = put(whole, shard, 0)
        ahead = behind = shard
        for step in range(1, far):
            ahead, behind = self.send(ahead, True), self.send(behind, False)
            whole = put(put(whole, ahead, -step), behind, step)
        last = (ahead, behind)
        ahead, behind = self.send(ahead[:, :cut], True), self.send(behind[:, cut:], False)
        whole = put(put(whole, ahead, -far), behind, far, cut)
        return whole, last

    def scatter(self, local, cols):
        cut = cols // 2
        far = self.count // 2
        most = local(self.owner(far))
        ahead, behind = self.send(most[:, :cut], True), self.send(most[:, cut:], False)
        for step in range(far - 1, 0, -1):
            mine = local(self.owner(step))
            other = local(self.owner(-step))
            if step == far - 1:
                ahead = jnp.concatenate([add_low(mine[:, :cut], ahead), mine[:, cut:]], axis=1)
                behind = jnp.concatenate([other[:, :cut], add_low(other[:, cut:], behind)], axis=1)
            else:
                ahead, behind = add_low(mine, ahead), add_low(other, behind)
            ahead, behind = self.send(ahead, True), self.send(behind, False)
        return local(self.owner(0)).astype(jnp.float32) + ahead.astype(jnp.float32) + behind.astype(jnp.float32)


def add_low(a, b):
    return (a.astype(jnp.float32) + b.astype(jnp.float32)).astype(jnp.bfloat16)


def body(
    tokens, cotangent, lengths, buckets, gain_one, gain_two, table,
    w_query, w_key, w_value, w_out, w_gate, w_up, w_down,
):
    micro, rows, local, width = tokens.shape
    seq_devices = lax.axis_size("seq")
    dp_devices = lax.axis_size("dp")
    seq_rank = lax.axis_index("seq")
    core = seq_rank % 2
    plane = seq_rank // 2
    planes = seq_devices // 2
    heads = table.shape[1]
    shard_rows, inner = w_query.shape
    head_dim = inner // heads
    half_inner = inner // 2
    hidden_units = w_gate.shape[1]
    pair_local = 2 * local
    seq_len = local * seq_devices
    first = core == 0
    core_pairs = [(i, i ^ 1) for i in range(seq_devices)]
    plane_groups = [[2 * p + c for p in range(planes)] for c in range(2)]
    ring = Ring(dp_devices)

    def swap_core(value):
        return lax.ppermute(value, "seq", core_pairs)

    def both_cores(own, other, axis):
        return jnp.concatenate([jnp.where(first, own, other), jnp.where(first, other, own)], axis=axis)

    def own_half(value, axis):
        return lax.dynamic_slice_in_dim(value, core * local, local, axis)

    def other_half(value, axis):
        return lax.dynamic_slice_in_dim(value, (1 - core) * local, local, axis)

    def core_columns(weight, split):
        low, high = weight[:, :split], weight[:, split:]
        high = jnp.pad(high, ((0, 0), (0, split - high.shape[1])))
        return jnp.where(first, low, high)

    chunk = 512
    chunks = -(-(hidden_units // 2) // chunk)
    split = chunks * chunk
    if split > hidden_units:
        split = hidden_units
    attn_shard = jnp.concatenate(
        [core_columns(w, half_inner) for w in (w_query, w_key, w_value, w_out.T)], axis=1
    )
    up_parts = [core_columns(w, split) for w in (w_gate, w_up, w_down.T)]
    chunk_shards = [
        jnp.concatenate([w[:, n * chunk : (n + 1) * chunk] for w in up_parts], axis=1) for n in range(chunks)
    ]

    small = jnp.concatenate([gain_one, gain_two, table.reshape(-1)])[None]
    small = lax.all_gather(small, "dp", axis=0, tiled=True).astype(jnp.float32)
    gain_first = small[:, :shard_rows].reshape(-1)
    gain_second = small[:, shard_rows : 2 * shard_rows].reshape(-1)
    full_table = small[:, 2 * shard_rows :].reshape(-1, heads)

    attn_weights, last = ring.gather(attn_shard)
    qkv_weights = attn_weights[:, : 3 * half_inner]
    out_own = attn_weights[:, 3 * half_inner :]
    out_other = swap_core(out_own)
    out_pair = jnp.concatenate([out_own, out_other], axis=1)

    chunk_weights = []
    for shard in chunk_shards:
        shard, last = lax.optimization_barrier((shard, last))
        gathered, last = ring.gather(shard)
        chunk_weights.append(gathered)

    tokens_other = swap_core(tokens)
    cotangent_other = swap_core(cotangent)
    tokens_pair = both_cores(tokens, tokens_other, 2)
    down_in = both_cores(cotangent, cotangent_other, 2)

    core_heads = heads // 2
    head_splits = planes // rows
    item_heads = core_heads // head_splits
    item_cols = item_heads * head_dim
    padded_cols = -(-item_cols // LANES) * LANES
    padded_heads = padded_cols // head_dim
    item_row = plane // head_splits
    item_group = plane % head_splits
    head_start = core * core_heads + item_group * item_heads
    item_table = lax.dynamic_slice_in_dim(full_table, head_start, item_heads, 1)
    item_table = jnp.pad(item_table, ((0, 0), (0, padded_heads - item_heads)))
    levels = full_table.shape[0]
    bucket_hot = (buckets[:, None] == jnp.arange(levels)[None, :]).astype(jnp.float32)
    bucket_hot = jnp.pad(bucket_hot, ((0, 1), (0, 0)))
    diag = jnp.dot(item_table.T, bucket_hot.T, precision=highest)[:, None, :]

    def to_items(value, parts):
        if planes == 2 and rows == 2:
            mine = lax.dynamic_index_in_dim(value, plane, 0, keepdims=False)
            sent = lax.dynamic_index_in_dim(value, 1 - plane, 0, keepdims=False)
            got = lax.ppermute(sent, "seq", [(i, i ^ 2) for i in range(4)])
            low = plane == 0
            return jnp.concatenate([jnp.where(low, mine, got), jnp.where(low, got, mine)], axis=0)
        value = value.reshape(rows, pair_local, parts, head_splits, item_cols)
        value = value.transpose(0, 3, 1, 2, 4).reshape(planes, pair_local, parts * item_cols)
        value = lax.all_to_all(value, "seq", 0, 0, tiled=True, axis_index_groups=plane_groups)
        value = value.reshape(seq_len, parts, item_cols)
        value = jnp.pad(value, ((0, 0), (0, 0), (0, padded_cols - item_cols)))
        return value.reshape(seq_len, parts * padded_cols)

    def from_items(values):
        parts = len(values)
        if planes == 2 and rows == 2:
            value = jnp.concatenate(values, axis=1)
            mine = lax.dynamic_slice_in_dim(value, plane * pair_local, pair_local, 0)
            sent = lax.dynamic_slice_in_dim(value, (1 - plane) * pair_local, pair_local, 0)
            got = lax.ppermute(sent, "seq", [(i, i ^ 2) for i in range(4)])
            low = plane == 0
            return jnp.stack([jnp.where(low, mine, got), jnp.where(low, got, mine)])
        value = jnp.concatenate([v[:, :item_cols] for v in values], axis=1)
        value = value.reshape(planes, pair_local, parts * item_cols)
        value = lax.all_to_all(value, "seq", 0, 0, tiled=True, axis_index_groups=plane_groups)
        value = value.reshape(rows, head_splits, pair_local, parts, item_cols).transpose(0, 2, 3, 1, 4)
        return value.reshape(rows, pair_local, parts * half_inner)

    normed, roots, qkvs, lses, mixes, resids, normed_twos, item_lens = [], [], [], [], [], [], [], []
    for step in range(micro):
        rows_in = tokens_pair[step].astype(jnp.float32)
        root = lax.rsqrt(jnp.mean(rows_in * rows_in, axis=-1, keepdims=True) + eps)
        roots.append(root)
        normed.append((rows_in * root * gain_first).astype(jnp.bfloat16))
    for step in range(micro):
        made = jnp.einsum("rld,de->rle", normed[step], qkv_weights, preferred_element_type=jnp.float32)
        qkvs.append(to_items(made.astype(jnp.bfloat16), 3))
    for step in range(micro):
        item_len = lax.dynamic_slice_in_dim(lengths[step], item_row, 1, 0)
        item_lens.append(item_len)
        mixed, lse = attend(qkvs[step], diag, item_len, head_dim)
        lses.append(lse)
        mixed_own = from_items([mixed])
        mixes.append(mixed_own)
        mixed_pair = jnp.concatenate([mixed_own, swap_core(mixed_own)], axis=2)
        resid = tokens_pair[step].astype(jnp.float32) + jnp.einsum(
            "rle,de->rld", mixed_pair, out_pair, preferred_element_type=jnp.float32
        )
        root = lax.rsqrt(jnp.mean(resid * resid, axis=-1, keepdims=True) + eps)
        normed_twos.append((resid * root * gain_second).astype(jnp.bfloat16))
        resids.append(own_half(resid, 1))

    pair_tokens = rows * pair_local
    flat = lambda value: value.reshape(-1, value.shape[-1])
    normed_two_all = jnp.concatenate([flat(v) for v in normed_twos])
    down_all = flat(down_in)
    pieces = [[None] * chunks for _ in range(micro)]
    chunk_totals = []
    for n in range(chunks):
        for step in range(micro):
            rowsl = slice(step * pair_tokens, (step + 1) * pair_tokens)
            pieces[step][n] = gated_chunk(flat(normed_twos[step]), down_all[rowsl], chunk_weights[n])
        joined = jnp.concatenate([pieces[step][n] for step in range(micro)])
        grad_gu = jnp.einsum("td,tf->df", normed_two_all, joined[:, : 2 * chunk], preferred_element_type=jnp.float32)
        grad_dn = jnp.einsum("td,tf->df", down_all, joined[:, 2 * chunk :], preferred_element_type=jnp.float32)
        grad_gu, grad_dn = grad_gu.astype(jnp.bfloat16), grad_dn.astype(jnp.bfloat16)

        def local_term(index, grad_gu=grad_gu, grad_dn=grad_dn):
            return jnp.concatenate(
                [lax.dynamic_slice_in_dim(g, index * shard_rows, shard_rows, 0) for g in (grad_gu, grad_dn)], axis=1
            )

        chunk_totals.append(ring.scatter(local_term, 3 * chunk))

    pieces = [[p.reshape(rows, pair_local, 3 * chunk) for p in per] for per in pieces]
    core_at = core.astype(jnp.int32)[None]
    grad_resids, grads_mixed, attn_ins = [], [], []
    gain_two_sum = jnp.zeros((width,), jnp.float32)
    for step in range(micro):
        sent = back_sum(pieces[step], chunk_weights, 1 - core_at, 2 * chunk, 0, local, jnp.bfloat16)
        got = swap_core(sent)
        kept = back_sum(pieces[step], chunk_weights, core_at, 2 * chunk, 0, local, jnp.float32)
        grad_normed = kept + got.astype(jnp.float32)
        resid = resids[step]
        root = lax.rsqrt(jnp.mean(resid * resid, axis=-1, keepdims=True) + eps)
        gain_two_sum = gain_two_sum + jnp.sum(grad_normed * resid * root, axis=(0, 1))
        scaled = grad_normed * gain_second
        shared = jnp.mean(scaled * resid, axis=-1, keepdims=True) * root * root * root
        grad_resid = cotangent[step].astype(jnp.float32) + scaled * root - resid * shared
        grad_resids.append(grad_resid)
        attn_in = grad_resid.astype(jnp.bfloat16)
        attn_ins.append(attn_in)
        made_own = jnp.einsum("rld,de->rle", attn_in, out_own, preferred_element_type=jnp.float32).astype(jnp.bfloat16)
        made_other = jnp.einsum("rld,de->rle", attn_in, out_other, preferred_element_type=jnp.float32).astype(
            jnp.bfloat16
        )
        grads_mixed.append(both_cores(made_own, swap_core(made_other), 1))

    outputs = []
    for step in range(micro):
        sent = back_sum(pieces[step], chunk_weights, 1 - core_at, chunk, 2, local, jnp.bfloat16)
        got = swap_core(sent)
        kept = back_sum(pieces[step], chunk_weights, core_at, chunk, 2, local, jnp.float32)
        outputs.append((resids[step] + kept + got.astype(jnp.float32)).astype(jnp.bfloat16))

    grads_qkv = []
    diag_sum = 0.0
    for step in range(micro):
        grad_items = to_items(grads_mixed[step], 1)
        grad_q, grad_k, grad_v, grad_diag = attend_back(
            qkvs[step], grad_items, lses[step], diag, item_lens[step], head_dim
        )
        diag_sum = diag_sum + grad_diag[:item_heads, 0]
        grads_qkv.append(from_items([grad_q, grad_k, grad_v]))
    item_grad = jnp.dot(diag_sum, bucket_hot, precision=highest)
    grad_table = lax.dynamic_update_slice(jnp.zeros((heads, levels), jnp.float32), item_grad, (head_start, 0))

    input_grads = []
    gain_one_sum = jnp.zeros((width,), jnp.float32)
    for step in range(micro):
        made = jnp.einsum("rle,de->rld", other_half(grads_qkv[step], 1), qkv_weights, preferred_element_type=jnp.float32)
        got = swap_core(made.astype(jnp.bfloat16))
        kept = jnp.einsum("rle,de->rld", own_half(grads_qkv[step], 1), qkv_weights, preferred_element_type=jnp.float32)
        grad_normed = kept + got.astype(jnp.float32)
        rows_in = tokens[step].astype(jnp.float32)
        root = own_half(roots[step], 1)
        gain_one_sum = gain_one_sum + jnp.sum(grad_normed * rows_in * root, axis=(0, 1))
        scaled = grad_normed * gain_first
        shared = jnp.mean(scaled * rows_in, axis=-1, keepdims=True) * root * root * root
        input_grads.append(grad_resids[step] + scaled * root - rows_in * shared)

    normed_all = jnp.concatenate([flat(v) for v in normed])
    grads_all = jnp.concatenate([flat(v) for v in grads_qkv])
    mixed_all = jnp.concatenate([flat(v) for v in mixes])
    attn_all = jnp.stack(attn_ins)
    attn_all = flat(both_cores(attn_all, swap_core(attn_all), 2))
    grad_attn = jnp.einsum("td,te->de", normed_all, grads_all, preferred_element_type=jnp.float32).astype(jnp.bfloat16)
    grad_o = jnp.einsum("td,te->de", attn_all, mixed_all, preferred_element_type=jnp.float32).astype(jnp.bfloat16)

    def attn_term(index):
        return jnp.concatenate(
            [lax.dynamic_slice_in_dim(g, index * shard_rows, shard_rows, 0) for g in (grad_attn, grad_o)], axis=1
        )

    attn_total = ring.scatter(attn_term, 4 * half_inner)

    def finish(total):
        if planes == 2:
            low = total.astype(jnp.bfloat16)
            got = lax.ppermute(low, "seq", [(i, i ^ 2) for i in range(4)])
            total = low.astype(jnp.float32) + got.astype(jnp.float32)
        else:
            total = lax.psum(total, "seq", axis_index_groups=plane_groups)
        return total, swap_core(total)

    def whole_columns(own, other, size):
        low, high = jnp.where(first, own, other), jnp.where(first, other, own)
        return jnp.concatenate([low, high[:, : size - low.shape[1]]], axis=1)

    own, other = finish(attn_total)
    parts = [slice(i * half_inner, (i + 1) * half_inner) for i in range(4)]
    grad_query, grad_key, grad_value, grad_out = [whole_columns(own[:, p], other[:, p], inner) for p in parts]
    done = [finish(total) for total in chunk_totals]
    parts = [slice(i * chunk, (i + 1) * chunk) for i in range(3)]
    grad_gate, grad_up, grad_down = [
        whole_columns(
            jnp.concatenate([own[:, p] for own, _ in done], axis=1),
            jnp.concatenate([other[:, p] for _, other in done], axis=1),
            hidden_units,
        )
        for p in parts
    ]

    dp_rank = lax.axis_index("dp")
    small = lax.psum(
        jnp.concatenate([gain_one_sum, gain_two_sum, grad_table.T.reshape(-1)]), ("dp", "seq")
    )
    grad_gain_one = lax.dynamic_slice_in_dim(small, dp_rank * shard_rows, shard_rows, 0)
    grad_gain_two = lax.dynamic_slice_in_dim(small, width + dp_rank * shard_rows, shard_rows, 0)
    table_part = levels // dp_devices
    grad_table = lax.dynamic_slice_in_dim(small[2 * width :].reshape(levels, heads), dp_rank * table_part, table_part, 0)

    return (
        jnp.stack(outputs), jnp.stack(input_grads), grad_gain_one, grad_gain_two, grad_table,
        grad_query, grad_key, grad_value, grad_out.T, grad_gate, grad_up, grad_down.T,
    )


def solution(mesh):
    weight, turned = P("dp", None), P(None, "dp")
    return jax.shard_map(
        body,
        mesh=mesh,
        in_specs=(
            P(None, "dp", "seq", None), P(None, "dp", "seq", None), P(None, "dp"), P(), P("dp"), P("dp"),
            weight, weight, weight, weight, turned, weight, weight, turned,
        ),
        out_specs=(
            P(None, "dp", "seq", None), P(None, "dp", "seq", None), P("dp"), P("dp"),
            weight, weight, weight, weight, turned, weight, weight, turned,
        ),
        check_vma=False,
    )
```

time: 3290 us -> 1140 us (0.35)
  waiting for transfers between devices: 1800 us -> 257 us
  matrix products: 839 us -> 134 us
  Pallas kernels: 0 us -> 293 us
  local copies, waits for them, and re-layouts: 328 us -> 130 us
  loops' own time: 55.9 us -> 0 us
  other arithmetic: 82.1 us -> 131 us
  starting transfers between devices: 68.5 us -> 108 us
    reduce_scatter x7 -> x0, waiting for transfers between devices: 1270 us -> none  [the longest x1 396 us: reduce_each(): lax.psum_scatter(grads[7], 'dp', scatter_dimension=0, tiled=True)]
    dot_general x85 -> x24, matrix products: 839 us -> 134 us  [the longest x4 39.6 us: body(): jnp.einsum('td,tf->df', normed_two_all, joined[:, :2 * chunk], preferred_...]
    all_gather x7 -> x0, waiting for transfers between devices: 342 us -> none  [the longest x1 158 us: fetch_each(): lax.all_gather(shards[7], 'dp', axis=0, tiled=True)]
    pallas_call x0 -> x20, Pallas kernels: none -> 293 us  [the longest x8 87 us: back_sum(): pl.pallas_call(body_of, grid_spec=pltpu.PrefetchScalarGridSpec(num_scalar...]
    ppermute x0 -> x112, waiting for transfers between devices: none -> 257 us  [the longest x80 213 us: send(): return lax.ppermute(block, 'dp', self.ahead if forward else self.behind)]
    psum x1 -> x0, waiting for transfers between devices: 134 us -> none  [reduce_each(): lax.psum((summed[0], summed[1], summed[2], summed[3], summed[4], summed[5...]
    ppermute x0 -> x112, starting transfers between devices: none -> 108 us  [the longest x80 87.6 us: send(): return lax.ppermute(block, 'dp', self.ahead if forward else self.behind)]
    all_to_all x16 -> x0, starting transfers between devices: 67.4 us -> none  [the longest x2 8.59 us: body(): lax.all_to_all(project(gathered[4]), 'seq', split_axis=1, concat_axis=0,...]
  transfers between devices with their start and end apart: 31 -> 112, of which waited for: 20 -> 38; matrix products, arithmetic and copies ran while one was open for 33% -> 32% of each run, Pallas kernels for 0% -> 26%
where the time goes in v1:
time: 1140 us; the launch traced here: 1130 us
  Pallas kernels  293 us (26%)
  waiting for transfers between devices  257 us (23%)
  matrix products  134 us (12%)
  other arithmetic  131 us (11%)
  local copies, waits for them, and re-layouts  130 us (11%)
  starting transfers between devices  108 us (9%)
  blocking collectives  61.6 us (5%)
  between operations  17.2 us (2%)
    ppermute x80, waiting for transfers between devices, send(): return lax.ppermute(block, 'dp', self.ahead if forward else self.behind)  213 us
    ppermute x80, starting transfers between devices, send(): return lax.ppermute(block, 'dp', self.ahead if forward else self.behind)  87.6 us
    pallas_call x8, Pallas kernels, back_sum(): pl.pallas_call(body_of, grid_spec=pltpu.PrefetchScalarGridSpec(num_scalar...  87 us
    pallas_call x2, Pallas kernels, attend_back(): pl.pallas_call(functools.partial(attend_back_kernel, head_dim, block), gr...  83.2 us
    pallas_call x8, Pallas kernels, gated_chunk(): pl.pallas_call(functools.partial(gated_kernel, width), grid=(tokens // ti...  81.4 us
    pallas_call x2, Pallas kernels, attend(): pl.pallas_call(functools.partial(attend_kernel, head_dim, block), grid=(p...  41.2 us
    dot_general x4, matrix products, body(): jnp.einsum('td,tf->df', normed_two_all, joined[:, :2 * chunk], preferred_...  39.6 us
    psum x1, blocking collectives, body(): lax.psum(jnp.concatenate([gain_one_sum, gain_two_sum, grad_table.T.reshap...  39.2 us
  transfers between devices with their start and end apart: 112, of which 38 were waited for; matrix products, arithmetic and copies ran while one was open for 32% of the time, Pallas kernels for 26%

profile of v1, /device:TPU:0, one launch (start us, length us, event | category | flops | bytes accessed | tf_op | source)
XLA Modules:
  0.0 1131.1 jit_solution(3358496771489425406)
XLA Ops:
  30.6 22.4 %all-reduce.4 = bf16[3456]{0:T(1024)(128)(2,1)S(1)} all-reduce(bf16[3456]{0:T(1024)(128)(2,1)S(1)} %dynamic-update-slice), channel_id=2, replica_groups=mesh['dp'=8,'seq'=4] {'dp'}, use_global_device_ids=true, to_apply=%add.4 | all-reduce | flops 3456 | bytes 13824
  89.8 5.9 collective-permute-done.5
  102.1 10.4 collective-permute-done.7
  118.6 10.6 collective-permute-done.16
  138.6 7.9 convolution_convert_fusion.1
  148.3 6.5 convolution_convert_fusion.2
  159.4 5.4 fusion.6
  178.7 11.6 %collective-permute-done.20 = bf16[192,768]{1,0:T(8,128)(2,1)S(1)} collective-permute-done((bf16[192,768]{1,0:T(8,128)(2,1)S(1)}, bf16[192,768]{1,0:T(8,128)(2,1)S(1)}, u32[]{:S(2)}, u32[]{:S(2)}) %collective-permute-start.20) | collective-permute-done | bytes 294944 | tf_op jit(solution)/shard_map/ppermute | solution.py:326
  198.1 20.7 %attend.3 = (bf16[1024,384]{1,0:T(8,128)(2,1)}, f32[6,1,1024]{2,1,0:T(1,128)}) custom-call(s32[1]{0:T(128)} %bitcast.30.len_ref, f32[6,1,2048]{2,1,0:T(1,128)} %broadcast_in_dim.9.diag_ref, bf16[1024,1152]{1,0:T(8,128)(2,1)} %pad_maximum_fusion.12.q_ref.k_ref.v_ref, bf16[1024,1152]{1,0:T(8,128)(2,1)} %pad_maximum_fusion.12.q_ref.k_ref.v_ref, ...), custom_call_target="tpu_custom_call" | custom-call | flops 6442450944 | bytes 3145728 | tf_op jit(solution)/shard_map/attend/pallas_call | solution.py:84
  223.9 20.5 %attend.2 = (bf16[1024,384]{1,0:T(8,128)(2,1)}, f32[6,1,1024]{2,1,0:T(1,128)}) custom-call(s32[1]{0:T(128)} %bitcast.1.len_ref, f32[6,1,2048]{2,1,0:T(1,128)} %broadcast_in_dim.9.diag_ref, bf16[1024,1152]{1,0:T(8,128)(2,1)} %pad_maximum_fusion.11.q_ref.k_ref.v_ref, bf16[1024,1152]{1,0:T(8,128)(2,1)} %pad_maximum_fusion.11.q_ref.k_ref.v_ref, ...), custom_call_target="tpu_custom_call" | custom-call | flops 6442450944 | bytes 3145728 | tf_op jit(solution)/shard_map/attend/pallas_call | solution.py:84
  282.2 10.1 gated_chunk.12
  292.3 10.2 gated_chunk.8
  302.5 9.5 fusion.28
  317.6 6.4 convolution_convert_fusion.8
  332.9 10.1 gated_chunk.13
  343.0 10.3 gated_chunk.9
  353.3 9.7 fusion.31
  363.0 6.2 convolution_convert_fusion.7
  384.6 7.0 collective-permute-done.73
  394.9 22.0 %collective-permute-done.82 = bf16[192,1536]{1,0:T(8,128)(2,1)S(1)} collective-permute-done((bf16[192,1536]{1,0:T(8,128)(2,1)S(1)}, bf16[192,1536]{1,0:T(8,128)(2,1)S(1)}, u32[]{:S(2)}, u32[]{:S(2)}) %collective-permute-start.82) | collective-permute-done | bytes 589856 | tf_op jit(solution)/shard_map/ppermute | solution.py:326
  423.1 6.4 collective-permute-done.74
  434.7 20.2 %collective-permute-done.34 = bf16[192,1536]{1,0:T(8,128)(2,1)S(1)} collective-permute-done((bf16[192,1536]{1,0:T(8,128)(2,1)S(1)}, bf16[192,1536]{1,0:T(8,128)(2,1)S(1)}, u32[]{:S(2)}, u32[]{:S(2)}) %collective-permute-start.34) | collective-permute-done | bytes 589856 | tf_op jit(solution)/shard_map/ppermute | solution.py:326
  464.1 19.4 %collective-permute-done.36 = bf16[192,768]{1,0:T(8,128)(2,1)S(1)} collective-permute-done((bf16[192,768]{1,0:T(8,128)(2,1)S(1)}, bf16[192,768]{1,0:T(8,128)(2,1)S(1)}, u32[]{:S(2)}, u32[]{:S(2)}) %collective-permute-start.36) | collective-permute-done | bytes 294944 | tf_op jit(solution)/shard_map/ppermute | solution.py:326
  487.2 10.2 gated_chunk.14
  497.4 10.3 gated_chunk.10
  507.6 9.6 fusion.34
  517.3 6.3 convolution_convert_fusion.6
  536.7 8.5 collective-permute-done.88
  565.1 9.1 collective-permute-done.41
  580.7 6.2 collective-permute-done.96
  591.0 5.5 collective-permute-done.43
  598.7 7.7 collective-permute-done.44
  609.3 10.1 gated_chunk.15
  619.4 10.2 gated_chunk.11
  629.6 10.8 fusion.37
  640.4 7.4 convolution_convert_fusion.5
  647.8 8.2 back_sum.10
  656.0 7.9 back_sum.11
  663.9 13.8 %back_sum.15 = bf16[2,256,1536]{2,1,0:T(8,128)(2,1)} custom-call(s32[1]{0:T(128)S(6)} %sub.39.start_ref, bf16[2,512,1536]{2,1,0:T(8,128)(2,1)} %bitcast.205, bf16[2,512,1536]{2,1,0:T(8,128)(2,1)} %bitcast.213, bf16[2,512,1536]{2,1,0:T(8,128)(2,1)} %bitcast.221, bf16[2,512,1536]{2,1,0:T(8,128)(2,1)} %bitcast.229, bf16[1536,1536]{1,0:T(8,128)(2,1)} %copy-done.1, ...), custom_call_target="tpu_custom_call" | custom-call | flops 6442450944 | bytes 19922944 | tf_op jit(solution)/shard_map/back_sum/pallas_call | solution.py:279
  677.6 13.6 %back_sum.14 = f32[2,256,1536]{2,1,0:T(8,128)} custom-call(s32[1]{0:T(128)} %bitcast.20.start_ref, bf16[2,512,1536]{2,1,0:T(8,128)(2,1)} %bitcast.206, bf16[2,512,1536]{2,1,0:T(8,128)(2,1)} %bitcast.214, bf16[2,512,1536]{2,1,0:T(8,128)(2,1)} %bitcast.222, bf16[2,512,1536]{2,1,0:T(8,128)(2,1)} %bitcast.230, bf16[1536,1536]{1,0:T(8,128)(2,1)} %copy-done.1, ...), custom_call_target="tpu_custom_call" | custom-call | flops 6442450944 | bytes 19922944 | tf_op jit(solution)/shard_map/back_sum/pallas_call | solution.py:279
  691.3 8.2 back_sum.8
  699.4 13.4 %back_sum.13 = bf16[2,256,1536]{2,1,0:T(8,128)(2,1)} custom-call(s32[1]{0:T(128)S(6)} %sub.39.start_ref, bf16[2,512,1536]{2,1,0:T(8,128)(2,1)} %bitcast.200, bf16[2,512,1536]{2,1,0:T(8,128)(2,1)} %bitcast.208, bf16[2,512,1536]{2,1,0:T(8,128)(2,1)} %bitcast.216, bf16[2,512,1536]{2,1,0:T(8,128)(2,1)} %bitcast.224, bf16[1536,1536]{1,0:T(8,128)(2,1)} %copy-done.1, ...), custom_call_target="tpu_custom_call" | custom-call | flops 6442450944 | bytes 19922944 | tf_op jit(solution)/shard_map/back_sum/pallas_call | solution.py:279
  717.8 13.9 %back_sum.12 = f32[2,256,1536]{2,1,0:T(8,128)} custom-call(s32[1]{0:T(128)} %bitcast.20.start_ref, bf16[2,512,1536]{2,1,0:T(8,128)(2,1)} %bitcast.201, bf16[2,512,1536]{2,1,0:T(8,128)(2,1)} %bitcast.209, bf16[2,512,1536]{2,1,0:T(8,128)(2,1)} %bitcast.217, bf16[2,512,1536]{2,1,0:T(8,128)(2,1)} %bitcast.225, bf16[1536,1536]{1,0:T(8,128)(2,1)} %copy-done.1, ...), custom_call_target="tpu_custom_call" | custom-call | flops 6442450944 | bytes 19922944 | tf_op jit(solution)/shard_map/back_sum/pallas_call | solution.py:279
  732.5 8.0 back_sum.9
  754.8 9.2 collective-permute-done.100
  770.0 9.0 collective-permute-done.98
  786.2 6.9 collective-permute-done.105
  800.8 11.7 %convert_bitcast_fusion.1 = (bf16[1,2,256,1536]{3,2,1,0:T(8,128)(2,1)S(1)}, f32[2,256,1536]{2,1,0:T(8,128)S(1)}, bf16[1,2,256,1536]{3,2,1,0:T(8,128)(2,1)}, bf16...) fusion(f32[2,256]{1,0:T(2,128)S(1)} %get-tuple-element.277, ...), kind=kLoop, calls=%fused_computation.512 | loop fusion | flops 20447232 | bytes 40908804 | tf_op jit(solution)/shard_map/stack | solution.py:595
  840.0 41.5 %attend_back.2 = (bf16[1024,384]{1,0:T(8,128)(2,1)}, bf16[1024,384]{1,0:T(8,128)(2,1)}, bf16[1024,384]{1,0:T(8,128)(2,1)}, f32[6,1,2048]{2,1,0:T(1,128)}) custom-call(s32[1]{0:T(128)} %bitcast.1.len_ref, f32[6,1,2048]{2,1,0:T(1,128)} %broadcast_in_dim.9.diag_ref, bf16[1024,1152]{1,0:T(8,128)(2,1)} %pad_maximum_fusion.11.q_ref.k_ref.v_ref, ...), custom_call_target="tpu_custom_call" | custom-call | flops 16106127360 | bytes 6291456 | tf_op jit(solution)/shard_map/attend_back/pallas_call | solution.py:193
  889.8 41.7 %attend_back.3 = (bf16[1024,384]{1,0:T(8,128)(2,1)}, bf16[1024,384]{1,0:T(8,128)(2,1)}, bf16[1024,384]{1,0:T(8,128)(2,1)}, f32[6,1,2048]{2,1,0:T(1,128)}) custom-call(s32[1]{0:T(128)} %bitcast.30.len_ref, f32[6,1,2048]{2,1,0:T(1,128)} %broadcast_in_dim.9.diag_ref, bf16[1024,1152]{1,0:T(8,128)(2,1)} %pad_maximum_fusion.12.q_ref.k_ref.v_ref, ...), custom_call_target="tpu_custom_call" | custom-call | flops 16106127360 | bytes 6291456 | tf_op jit(solution)/shard_map/attend_back/pallas_call | solution.py:193
  944.9 18.4 %collective-permute-done.59 = bf16[512,1152]{1,0:T(8,128)(2,1)} collective-permute-done((bf16[512,1152]{1,0:T(8,128)(2,1)}, bf16[512,1152]{1,0:T(8,128)(2,1)}, u32[]{:S(2)}, u32[]{:S(2)}) %collective-permute-start.59) | collective-permute-done | bytes 1179680 | tf_op jit(solution)/shard_map/ppermute | solution.py:480
  968.1 8.7 convolution_convert_fusion
  978.2 5.4 convolution_convert_fusion.4
  983.6 5.4 convolution_convert_fusion.3
  1006.7 6.7 convolution_convert_fusion.9
  1016.9 6.5 collective-permute-done.66
  1027.3 5.2 collective-permute-done.63
  1033.0 6.0 collective-permute-done.67
  1041.2 4.9 convolution_add_fusion
  1049.0 4.8 collective-permute-done.68
  1056.6 7.2 fusion.44
  1063.8 39.2 %psum.7 = f32[3456]{0:T(1024)S(1)} all-reduce(f32[3456]{0:T(1024)S(1)} %pad_maximum_fusion.54), channel_id=1, replica_groups=mesh['dp'=8,'seq'=4] {'dp','seq'}, use_global_device_ids=true, to_apply=%region_14.15 | all-reduce | flops 3456 | bytes 27648 | tf_op jit(solution)/shard_map/psum | solution.py:635
  1108.6 10.7 collective-permute-done.70
  1119.5 4.5 fusion.42
  (792 shorter events, 392.0 us)
Async XLA Ops:
  20.7 47.7 %collective-permute-start.1 = (bf16[192,1536]{1,0:T(8,128)(2,1)}, bf16[192,1536]{1,0:T(8,128)(2,1)}, u32[]{:S(2)}, u32[]{:S(2)}) collective-permute-start(bf16[192,1536]{1,0:T(8,128)(2,1)} %get-tuple-element.242), channel_id=1, source_target_pairs={{4,12},{12,20},{20,28},{28,24},{24,16},{16,8},{8,0},{0,4},{5,13},{... | collective-permute-start | bytes 1769480 | tf_op jit(solution)/shard_map/ppermute | solution.py:326
  23.6 45.4 %collective-permute-start.2 = (bf16[192,1536]{1,0:T(8,128)(2,1)}, bf16[192,1536]{1,0:T(8,128)(2,1)}, u32[]{:S(2)}, u32[]{:S(2)}) collective-permute-start(bf16[192,1536]{1,0:T(8,128)(2,1)} %get-tuple-element.242), channel_id=1, source_target_pairs={{4,0},{12,4},{20,12},{28,20},{24,28},{16,24},{8,16},{0,8},{5,1},{1... | collective-permute-start | bytes 1769480 | tf_op jit(solution)/shard_map/ppermute | solution.py:326
  23.7 110.2 %collective-permute-start = (bf16[2,2,256,1536]{3,2,1,0:T(8,128)(2,1)S(1)}, bf16[2,2,256,1536]{3,2,1,0:T(8,128)(2,1)}, u32[]{:S(2)}, u32[]{:S(2)}) collective-permute-start(bf16[2,2,256,1536]{3,2,1,0:T(8,128)(2,1)S(1)} %copy-done.22), channel_id=1, source_target_pairs={{0,1},{1,0},{2,3},{3,2},{4,5},{5,4},{6,7},{7,6},{8,9},{9,8},{10,11... | collective-permute-start | bytes 9437192 | tf_op jit(solution)/shard_map/ppermute | solution.py:392
  112.5 42.4 %collective-permute-start.13 = (bf16[2,2,256,1536]{3,2,1,0:T(8,128)(2,1)S(1)}, bf16[2,2,256,1536]{3,2,1,0:T(8,128)(2,1)S(1)}, u32[]{:S(2)}, u32[]{:S(2)}) collective-permute-start(bf16[2,2,256,1536]{3,2,1,0:T(8,128)(2,1)S(1)} %copy-done.21), channel_id=1, source_target_pairs={{0,1},{1,0},{2,3},{3,2},{4,5},{5,4},{6,7},{7,6},{8,9},{9,8},{10,11... | collective-permute-start | bytes 9437192 | tf_op jit(solution)/shard_map/ppermute | solution.py:392
  129.1 40.6 %collective-permute-start.18 = (bf16[192,1536]{1,0:T(8,128)(2,1)}, bf16[192,1536]{1,0:T(8,128)(2,1)}, u32[]{:S(2)}, u32[]{:S(2)}) collective-permute-start(bf16[192,1536]{1,0:T(8,128)(2,1)} %collective-permute-done.16), channel_id=1, source_target_pairs={{4,12},{12,20},{20,28},{28,24},{24,16},{16,8},{8,0},{0,4},{5,13},{... | collective-permute-start | bytes 1769480 | tf_op jit(solution)/shard_map/ppermute | solution.py:326
  129.4 40.3 %collective-permute-start.19 = (bf16[192,1536]{1,0:T(8,128)(2,1)}, bf16[192,1536]{1,0:T(8,128)(2,1)}, u32[]{:S(2)}, u32[]{:S(2)}) collective-permute-start(bf16[192,1536]{1,0:T(8,128)(2,1)} %collective-permute-done.17), channel_id=1, source_target_pairs={{4,0},{12,4},{20,12},{28,20},{24,28},{16,24},{8,16},{0,8},{5,1},{1... | collective-permute-start | bytes 1769480 | tf_op jit(solution)/shard_map/ppermute | solution.py:326
  165.5 28.9 %collective-permute-start.47 = (bf16[512,1152]{1,0:T(8,128)(2,1)S(1)}, bf16[512,1152]{1,0:T(8,128)(2,1)S(1)}, u32[]{:S(2)}, u32[]{:S(2)}) collective-permute-start(bf16[512,1152]{1,0:T(8,128)(2,1)S(1)} %copy-done.105), channel_id=1, source_target_pairs={{0,2},{1,3},{2,0},{3,1},{4,6},{5,7},{6,4},{7,5},{8,10},{9,11},{10,... | collective-permute-start | bytes 3538952 | tf_op jit(solution)/shard_map/ppermute | solution.py:464
  169.8 21.2 %collective-permute-start.22 = (bf16[192,1536]{1,0:T(8,128)(2,1)S(1)}, bf16[192,1536]{1,0:T(8,128)(2,1)}, u32[]{:S(2)}, u32[]{:S(2)}) collective-permute-start(bf16[192,1536]{1,0:T(8,128)(2,1)S(1)} %copy-done.58), channel_id=1, source_target_pairs={{4,12},{12,20},{20,28},{28,24},{24,16},{16,8},{8,0},{0,4},{5,13},{... | collective-permute-start | bytes 1769480 | tf_op jit(solution)/shard_map/ppermute | solution.py:326
  170.1 21.3 %collective-permute-start.23 = (bf16[192,1536]{1,0:T(8,128)(2,1)S(1)}, bf16[192,1536]{1,0:T(8,128)(2,1)S(1)}, u32[]{:S(2)}, u32[]{:S(2)}) collective-permute-start(bf16[192,1536]{1,0:T(8,128)(2,1)S(1)} %copy-done.58), channel_id=1, source_target_pairs={{4,0},{12,4},{20,12},{28,20},{24,28},{16,24},{8,16},{0,8},{5,1},{1... | collective-permute-start | bytes 1769480 | tf_op jit(solution)/shard_map/ppermute | solution.py:326
  190.3 79.3 %collective-permute-start.12 = (bf16[1536,384]{1,0:T(8,128)(2,1)S(1)}, bf16[1536,384]{1,0:T(8,128)(2,1)S(1)}, u32[]{:S(2)}, u32[]{:S(2)}) collective-permute-start(bf16[1536,384]{1,0:T(8,128)(2,1)S(1)} %copy-done.106), channel_id=1, source_target_pairs={{0,1},{1,0},{2,3},{3,2},{4,5},{5,4},{6,7},{7,6},{8,9},{9,8},{10,11... | collective-permute-start | bytes 3538952 | tf_op jit(solution)/shard_map/ppermute | solution.py:392
  190.4 31.8 %collective-permute-start.9 = (bf16[512,1152]{1,0:T(8,128)(2,1)S(1)}, bf16[512,1152]{1,0:T(8,128)(2,1)S(1)}, u32[]{:S(2)}, u32[]{:S(2)}) collective-permute-start(bf16[512,1152]{1,0:T(8,128)(2,1)S(1)} %dynamic-slice_bitcast_fusion.1), channel_id=1, source_target_pairs={{0,2},{1,3},{2,0},{3,1},{4,6},{5,7},{6,4},{7,5},{8,10},{9,11},{10,... | collective-permute-start | bytes 3538952 | tf_op jit(solution)/shard_map/ppermute | solution.py:464
  190.9 55.2 %collective-permute-start.24 = (bf16[192,1536]{1,0:T(8,128)(2,1)}, bf16[192,1536]{1,0:T(8,128)(2,1)}, u32[]{:S(2)}, u32[]{:S(2)}) collective-permute-start(bf16[192,1536]{1,0:T(8,128)(2,1)} %collective-permute-done.22), channel_id=1, source_target_pairs={{4,12},{12,20},{20,28},{28,24},{24,16},{16,8},{8,0},{0,4},{5,13},{... | collective-permute-start | bytes 1769480 | tf_op jit(solution)/shard_map/ppermute | solution.py:326
  191.4 55.2 %collective-permute-start.25 = (bf16[192,1536]{1,0:T(8,128)(2,1)S(1)}, bf16[192,1536]{1,0:T(8,128)(2,1)}, u32[]{:S(2)}, u32[]{:S(2)}) collective-permute-start(bf16[192,1536]{1,0:T(8,128)(2,1)S(1)} %collective-permute-done.23), channel_id=1, source_target_pairs={{4,0},{12,4},{20,12},{28,20},{24,28},{16,24},{8,16},{0,8},{5,1},{1... | collective-permute-start | bytes 1769480 | tf_op jit(solution)/shard_map/ppermute | solution.py:326
  220.6 31.5 %collective-permute-start.48 = (bf16[512,384]{1,0:T(8,128)(2,1)}, bf16[512,384]{1,0:T(8,128)(2,1)}, u32[]{:S(2)}, u32[]{:S(2)}) collective-permute-start(bf16[512,384]{1,0:T(8,128)(2,1)} %constant_dynamic-slice_fusion.95), channel_id=1, source_target_pairs={{0,2},{1,3},{2,0},{3,1},{4,6},{5,7},{6,4},{7,5},{8,10},{9,11},{10,... | collective-permute-start | bytes 1179656 | tf_op jit(solution)/shard_map/ppermute | solution.py:480
  256.4 18.3 %collective-permute-start.11 = (bf16[2,512,384]{2,1,0:T(8,128)(2,1)S(1)}, bf16[2,512,384]{2,1,0:T(8,128)(2,1)S(1)}, u32[]{:S(2)}, u32[]{:S(2)}) collective-permute-start(bf16[2,512,384]{2,1,0:T(8,128)(2,1)S(1)} %pad_maximum_fusion.27), channel_id=1, source_target_pairs={{0,1},{1,0},{2,3},{3,2},{4,5},{5,4},{6,7},{7,6},{8,9},{9,8},{10,11... | collective-permute-start | bytes 2359304 | tf_op jit(solution)/shard_map/ppermute | solution.py:392
  260.8 115.4 %collective-permute-start.30 = (bf16[192,1536]{1,0:T(8,128)(2,1)S(1)}, bf16[192,1536]{1,0:T(8,128)(2,1)}, u32[]{:S(2)}, u32[]{:S(2)}) collective-permute-start(bf16[192,1536]{1,0:T(8,128)(2,1)S(1)} %copy-done.57), channel_id=1, source_target_pairs={{4,12},{12,20},{20,28},{28,24},{24,16},{16,8},{8,0},{0,4},{5,13},{... | collective-permute-start | bytes 1769480 | tf_op jit(solution)/shard_map/ppermute | solution.py:326
  261.2 118.5 %collective-permute-start.31 = (bf16[192,1536]{1,0:T(8,128)(2,1)S(1)}, bf16[192,1536]{1,0:T(8,128)(2,1)}, u32[]{:S(2)}, u32[]{:S(2)}) collective-permute-start(bf16[192,1536]{1,0:T(8,128)(2,1)S(1)} %copy-done.57), channel_id=1, source_target_pairs={{4,0},{12,4},{20,12},{28,20},{24,28},{16,24},{8,16},{0,8},{5,1},{1... | collective-permute-start | bytes 1769480 | tf_op jit(solution)/shard_map/ppermute | solution.py:326
  269.6 58.3 %collective-permute-start.28 = (bf16[192,768]{1,0:T(8,128)(2,1)}, bf16[192,768]{1,0:T(8,128)(2,1)}, u32[]{:S(2)}, u32[]{:S(2)}) collective-permute-start(bf16[192,768]{1,0:T(8,128)(2,1)} %slice.547), channel_id=1, source_target_pairs={{4,12},{12,20},{20,28},{28,24},{24,16},{16,8},{8,0},{0,4},{5,13},{... | collective-permute-start | bytes 884744 | tf_op jit(solution)/shard_map/ppermute | solution.py:326
  270.0 61.2 %collective-permute-start.29 = (bf16[192,768]{1,0:T(8,128)(2,1)}, bf16[192,768]{1,0:T(8,128)(2,1)}, u32[]{:S(2)}, u32[]{:S(2)}) collective-permute-start(bf16[192,768]{1,0:T(8,128)(2,1)} %slice.548), channel_id=1, source_target_pairs={{4,0},{12,4},{20,12},{28,20},{24,28},{16,24},{8,16},{0,8},{5,1},{1... | collective-permute-start | bytes 884744 | tf_op jit(solution)/shard_map/ppermute | solution.py:326
  316.7 55.2 %collective-permute-start.72 = (bf16[192,768]{1,0:T(8,128)(2,1)}, bf16[192,768]{1,0:T(8,128)(2,1)}, u32[]{:S(2)}, u32[]{:S(2)}) collective-permute-start(bf16[192,768]{1,0:T(8,128)(2,1)} %get-tuple-element.105), channel_id=1, source_target_pairs={{4,12},{12,20},{20,28},{28,24},{24,16},{16,8},{8,0},{0,4},{5,13},{... | collective-permute-start | bytes 884744 | tf_op jit(solution)/shard_map/ppermute | solution.py:326
  327.9 46.7 %collective-permute-start.76 = (bf16[192,768]{1,0:T(8,128)(2,1)}, bf16[192,768]{1,0:T(8,128)(2,1)}, u32[]{:S(2)}, u32[]{:S(2)}) collective-permute-start(bf16[192,768]{1,0:T(8,128)(2,1)} %pad_maximum_fusion.50), channel_id=1, source_target_pairs={{4,0},{12,4},{20,12},{28,20},{24,28},{16,24},{8,16},{0,8},{5,1},{1... | collective-permute-start | bytes 884744 | tf_op jit(solution)/shard_map/ppermute | solution.py:326
  379.7 39.6 %collective-permute-start.32 = (bf16[192,1536]{1,0:T(8,128)(2,1)}, bf16[192,1536]{1,0:T(8,128)(2,1)S(1)}, u32[]{:S(2)}, u32[]{:S(2)}) collective-permute-start(bf16[192,1536]{1,0:T(8,128)(2,1)} %collective-permute-done.30), channel_id=1, source_target_pairs={{4,12},{12,20},{20,28},{28,24},{24,16},{16,8},{8,0},{0,4},{5,13},{... | collective-permute-start | bytes 1769480 | tf_op jit(solution)/shard_map/ppermute | solution.py:326
  382.2 39.9 %collective-permute-start.33 = (bf16[192,1536]{1,0:T(8,128)(2,1)}, bf16[192,1536]{1,0:T(8,128)(2,1)S(1)}, u32[]{:S(2)}, u32[]{:S(2)}) collective-permute-start(bf16[192,1536]{1,0:T(8,128)(2,1)} %collective-permute-done.31), channel_id=1, source_target_pairs={{4,0},{12,4},{20,12},{28,20},{24,28},{16,24},{8,16},{0,8},{5,1},{1... | collective-permute-start | bytes 1769480 | tf_op jit(solution)/shard_map/ppermute | solution.py:326
  383.9 33.0 %collective-permute-start.82 = (bf16[192,1536]{1,0:T(8,128)(2,1)S(1)}, bf16[192,1536]{1,0:T(8,128)(2,1)S(1)}, u32[]{:S(2)}, u32[]{:S(2)}) collective-permute-start(bf16[192,1536]{1,0:T(8,128)(2,1)S(1)} %fusion.106), channel_id=1, source_target_pairs={{4,12},{12,20},{20,28},{28,24},{24,16},{16,8},{8,0},{0,4},{5,13},{... | collective-permute-start | bytes 1769480 | tf_op jit(solution)/shard_map/ppermute | solution.py:326
  391.7 27.3 %collective-permute-start.86 = (bf16[192,1536]{1,0:T(8,128)(2,1)S(1)}, bf16[192,1536]{1,0:T(8,128)(2,1)S(1)}, u32[]{:S(2)}, u32[]{:S(2)}) collective-permute-start(bf16[192,1536]{1,0:T(8,128)(2,1)S(1)} %pad_maximum_fusion.41), channel_id=1, source_target_pairs={{4,0},{12,4},{20,12},{28,20},{24,28},{16,24},{8,16},{0,8},{5,1},{1... | collective-permute-start | bytes 1769480 | tf_op jit(solution)/shard_map/ppermute | solution.py:326
  394.4 35.1 %collective-permute-start.74 = (bf16[192,1536]{1,0:T(8,128)(2,1)S(1)}, bf16[192,1536]{1,0:T(8,128)(2,1)S(1)}, u32[]{:S(2)}, u32[]{:S(2)}) collective-permute-start(bf16[192,1536]{1,0:T(8,128)(2,1)S(1)} %add_convert_fusion.21), channel_id=1, source_target_pairs={{4,12},{12,20},{20,28},{28,24},{24,16},{16,8},{8,0},{0,4},{5,13},{... | collective-permute-start | bytes 1769480 | tf_op jit(solution)/shard_map/ppermute | solution.py:326
  419.0 39.4 %collective-permute-start.83 = (bf16[192,1536]{1,0:T(8,128)(2,1)S(1)}, bf16[192,1536]{1,0:T(8,128)(2,1)S(1)}, u32[]{:S(2)}, u32[]{:S(2)}) collective-permute-start(bf16[192,1536]{1,0:T(8,128)(2,1)S(1)} %add_convert_fusion.16), channel_id=1, source_target_pairs={{4,12},{12,20},{20,28},{28,24},{24,16},{16,8},{8,0},{0,4},{5,13},{... | collective-permute-start | bytes 1769480 | tf_op jit(solution)/shard_map/ppermute | solution.py:326
  419.3 40.6 %collective-permute-start.87 = (bf16[192,1536]{1,0:T(8,128)(2,1)S(1)}, bf16[192,1536]{1,0:T(8,128)(2,1)S(1)}, u32[]{:S(2)}, u32[]{:S(2)}) collective-permute-start(bf16[192,1536]{1,0:T(8,128)(2,1)S(1)} %add_convert_fusion.14), channel_id=1, source_target_pairs={{4,0},{12,4},{20,12},{28,20},{24,28},{16,24},{8,16},{0,8},{5,1},{1... | collective-permute-start | bytes 1769480 | tf_op jit(solution)/shard_map/ppermute | solution.py:326
  422.1 32.7 %collective-permute-start.34 = (bf16[192,1536]{1,0:T(8,128)(2,1)S(1)}, bf16[192,1536]{1,0:T(8,128)(2,1)S(1)}, u32[]{:S(2)}, u32[]{:S(2)}) collective-permute-start(bf16[192,1536]{1,0:T(8,128)(2,1)S(1)} %collective-permute-done.32), channel_id=1, source_target_pairs={{4,12},{12,20},{20,28},{28,24},{24,16},{16,8},{8,0},{0,4},{5,13},{... | collective-permute-start | bytes 1769480 | tf_op jit(solution)/shard_map/ppermute | solution.py:326
  429.6 27.2 %collective-permute-start.35 = (bf16[192,1536]{1,0:T(8,128)(2,1)S(1)}, bf16[192,1536]{1,0:T(8,128)(2,1)S(1)}, u32[]{:S(2)}, u32[]{:S(2)}) collective-permute-start(bf16[192,1536]{1,0:T(8,128)(2,1)S(1)} %collective-permute-done.33), channel_id=1, source_target_pairs={{4,0},{12,4},{20,12},{28,20},{24,28},{16,24},{8,16},{0,8},{5,1},{1... | collective-permute-start | bytes 1769480 | tf_op jit(solution)/shard_map/ppermute | solution.py:326
  433.2 91.8 %collective-permute-start.75 = (bf16[192,1536]{1,0:T(8,128)(2,1)}, bf16[192,1536]{1,0:T(8,128)(2,1)}, u32[]{:S(2)}, u32[]{:S(2)}) collective-permute-start(bf16[192,1536]{1,0:T(8,128)(2,1)} %add_convert_fusion.20), channel_id=1, source_target_pairs={{4,12},{12,20},{20,28},{28,24},{24,16},{16,8},{8,0},{0,4},{5,13},{... | collective-permute-start | bytes 1769480 | tf_op jit(solution)/shard_map/ppermute | solution.py:326
  454.9 70.7 %collective-permute-start.79 = (bf16[192,1536]{1,0:T(8,128)(2,1)}, bf16[192,1536]{1,0:T(8,128)(2,1)}, u32[]{:S(2)}, u32[]{:S(2)}) collective-permute-start(bf16[192,1536]{1,0:T(8,128)(2,1)} %add_convert_fusion.18), channel_id=1, source_target_pairs={{4,0},{12,4},{20,12},{28,20},{24,28},{16,24},{8,16},{0,8},{5,1},{1... | collective-permute-start | bytes 1769480 | tf_op jit(solution)/shard_map/ppermute | solution.py:326
  456.7 91.7 %collective-permute-start.38 = (bf16[192,1536]{1,0:T(8,128)(2,1)}, bf16[192,1536]{1,0:T(8,128)(2,1)}, u32[]{:S(2)}, u32[]{:S(2)}) collective-permute-start(bf16[192,1536]{1,0:T(8,128)(2,1)} %pad_maximum_fusion.35), channel_id=1, source_target_pairs={{4,12},{12,20},{20,28},{28,24},{24,16},{16,8},{8,0},{0,4},{5,13},{... | collective-permute-start | bytes 1769480 | tf_op jit(solution)/shard_map/ppermute | solution.py:326
  458.4 25.1 %collective-permute-start.36 = (bf16[192,768]{1,0:T(8,128)(2,1)S(1)}, bf16[192,768]{1,0:T(8,128)(2,1)S(1)}, u32[]{:S(2)}, u32[]{:S(2)}) collective-permute-start(bf16[192,768]{1,0:T(8,128)(2,1)S(1)} %slice.552), channel_id=1, source_target_pairs={{4,12},{12,20},{20,28},{28,24},{24,16},{16,8},{8,0},{0,4},{5,13},{... | collective-permute-start | bytes 884744 | tf_op jit(solution)/shard_map/ppermute | solution.py:326
  459.9 26.0 %collective-permute-start.37 = (bf16[192,768]{1,0:T(8,128)(2,1)S(1)}, bf16[192,768]{1,0:T(8,128)(2,1)S(1)}, u32[]{:S(2)}, u32[]{:S(2)}) collective-permute-start(bf16[192,768]{1,0:T(8,128)(2,1)S(1)} %slice.553), channel_id=1, source_target_pairs={{4,0},{12,4},{20,12},{28,20},{24,28},{16,24},{8,16},{0,8},{5,1},{1... | collective-permute-start | bytes 884744 | tf_op jit(solution)/shard_map/ppermute | solution.py:326
  483.5 68.5 %collective-permute-start.39 = (bf16[192,1536]{1,0:T(8,128)(2,1)}, bf16[192,1536]{1,0:T(8,128)(2,1)}, u32[]{:S(2)}, u32[]{:S(2)}) collective-permute-start(bf16[192,1536]{1,0:T(8,128)(2,1)} %pad_maximum_fusion.35), channel_id=1, source_target_pairs={{4,0},{12,4},{20,12},{28,20},{24,28},{16,24},{8,16},{0,8},{5,1},{1... | collective-permute-start | bytes 1769480 | tf_op jit(solution)/shard_map/ppermute | solution.py:326
  485.9 50.7 %collective-permute-start.84 = (bf16[192,1536]{1,0:T(8,128)(2,1)}, bf16[192,1536]{1,0:T(8,128)(2,1)}, u32[]{:S(2)}, u32[]{:S(2)}) collective-permute-start(bf16[192,1536]{1,0:T(8,128)(2,1)} %add_convert_fusion.15), channel_id=1, source_target_pairs={{4,12},{12,20},{20,28},{28,24},{24,16},{16,8},{8,0},{0,4},{5,13},{... | collective-permute-start | bytes 1769480 | tf_op jit(solution)/shard_map/ppermute | solution.py:326
  534.8 18.3 %collective-permute-start.80 = (bf16[192,1536]{1,0:T(8,128)(2,1)S(1)}, bf16[192,1536]{1,0:T(8,128)(2,1)S(1)}, u32[]{:S(2)}, u32[]{:S(2)}) collective-permute-start(bf16[192,1536]{1,0:T(8,128)(2,1)S(1)} %add_convert_fusion.17), channel_id=1, source_target_pairs={{0,2},{1,3},{2,0},{3,1},{4,6},{5,7},{6,4},{7,5},{8,10},{9,11},{10,... | collective-permute-start | bytes 1769480 | tf_op jit(solution)/shard_map/ppermute | solution.py:610
  536.6 22.2 %collective-permute-start.91 = (bf16[192,1536]{1,0:T(8,128)(2,1)S(1)}, bf16[192,1536]{1,0:T(8,128)(2,1)S(1)}, u32[]{:S(2)}, u32[]{:S(2)}) collective-permute-start(bf16[192,1536]{1,0:T(8,128)(2,1)S(1)} %fusion.108), channel_id=1, source_target_pairs={{4,12},{12,20},{20,28},{28,24},{24,16},{16,8},{8,0},{0,4},{5,13},{... | collective-permute-start | bytes 1769480 | tf_op jit(solution)/shard_map/ppermute | solution.py:326
  553.2 21.0 %collective-permute-start.41 = (bf16[192,1536]{1,0:T(8,128)(2,1)}, bf16[192,1536]{1,0:T(8,128)(2,1)S(1)}, u32[]{:S(2)}, u32[]{:S(2)}) collective-permute-start(bf16[192,1536]{1,0:T(8,128)(2,1)} %collective-permute-done.39), channel_id=1, source_target_pairs={{4,0},{12,4},{20,12},{28,20},{24,28},{16,24},{8,16},{0,8},{5,1},{1... | collective-permute-start | bytes 1769480 | tf_op jit(solution)/shard_map/ppermute | solution.py:326
  558.8 181.7 %collective-permute-start.108 = (f32[192,1536]{1,0:T(8,128)}, f32[192,1536]{1,0:T(8,128)}, u32[]{:S(2)}, u32[]{:S(2)}) collective-permute-start(f32[192,1536]{1,0:T(8,128)} %convert_add_fusion.7), channel_id=1, source_target_pairs={{0,1},{1,0},{2,3},{3,2},{4,5},{5,4},{6,7},{7,6},{8,9},{9,8},{10,11... | collective-permute-start | bytes 3538952 | tf_op jit(solution)/shard_map/ppermute | solution.py:392
  562.2 24.6 %collective-permute-start.96 = (bf16[192,1536]{1,0:T(8,128)(2,1)S(1)}, bf16[192,1536]{1,0:T(8,128)(2,1)S(1)}, u32[]{:S(2)}, u32[]{:S(2)}) collective-permute-start(bf16[192,1536]{1,0:T(8,128)(2,1)S(1)} %add_convert_fusion.9), channel_id=1, source_target_pairs={{4,0},{12,4},{20,12},{28,20},{24,28},{16,24},{8,16},{0,8},{5,1},{1... | collective-permute-start | bytes 1769480 | tf_op jit(solution)/shard_map/ppermute | solution.py:326
  564.0 187.9 %collective-permute-start.109 = (f32[192,1536]{1,0:T(8,128)S(1)}, f32[192,1536]{1,0:T(8,128)}, u32[]{:S(2)}, u32[]{:S(2)}) collective-permute-start(f32[192,1536]{1,0:T(8,128)S(1)} %convert_add_fusion.6), channel_id=1, source_target_pairs={{0,1},{1,0},{2,3},{3,2},{4,5},{5,4},{6,7},{7,6},{8,9},{9,8},{10,11... | collective-permute-start | bytes 3538952 | tf_op jit(solution)/shard_map/ppermute | solution.py:392
  577.8 18.7 %collective-permute-start.43 = (bf16[192,1536]{1,0:T(8,128)(2,1)S(1)}, bf16[192,1536]{1,0:T(8,128)(2,1)S(1)}, u32[]{:S(2)}, u32[]{:S(2)}) collective-permute-start(bf16[192,1536]{1,0:T(8,128)(2,1)S(1)} %collective-permute-done.41), channel_id=1, source_target_pairs={{4,0},{12,4},{20,12},{28,20},{24,28},{16,24},{8,16},{0,8},{5,1},{1... | collective-permute-start | bytes 1769480 | tf_op jit(solution)/shard_map/ppermute | solution.py:326
  586.8 156.7 %collective-permute-start.93 = (bf16[192,1536]{1,0:T(8,128)(2,1)}, bf16[192,1536]{1,0:T(8,128)(2,1)}, u32[]{:S(2)}, u32[]{:S(2)}) collective-permute-start(bf16[192,1536]{1,0:T(8,128)(2,1)} %add_convert_fusion.10), channel_id=1, source_target_pairs={{4,12},{12,20},{20,28},{28,24},{24,16},{16,8},{8,0},{0,4},{5,13},{... | collective-permute-start | bytes 1769480 | tf_op jit(solution)/shard_map/ppermute | solution.py:326
  606.4 137.2 %collective-permute-start.97 = (bf16[192,1536]{1,0:T(8,128)(2,1)}, bf16[192,1536]{1,0:T(8,128)(2,1)}, u32[]{:S(2)}, u32[]{:S(2)}) collective-permute-start(bf16[192,1536]{1,0:T(8,128)(2,1)} %add_convert_fusion.8), channel_id=1, source_target_pairs={{4,0},{12,4},{20,12},{28,20},{24,28},{16,24},{8,16},{0,8},{5,1},{1... | collective-permute-start | bytes 1769480 | tf_op jit(solution)/shard_map/ppermute | solution.py:326
  715.3 30.4 %collective-permute-start.99 = (bf16[192,768]{1,0:T(8,128)(2,1)}, bf16[192,768]{1,0:T(8,128)(2,1)}, u32[]{:S(2)}, u32[]{:S(2)}) collective-permute-start(bf16[192,768]{1,0:T(8,128)(2,1)} %get-tuple-element.135), channel_id=1, source_target_pairs={{4,12},{12,20},{20,28},{28,24},{24,16},{16,8},{8,0},{0,4},{5,13},{... | collective-permute-start | bytes 884744 | tf_op jit(solution)/shard_map/ppermute | solution.py:326
  743.5 55.6 %collective-permute-start.50 = (bf16[2,256,1536]{2,1,0:T(8,128)(2,1)S(1)}, bf16[2,256,1536]{2,1,0:T(8,128)(2,1)S(1)}, u32[]{:S(2)}, u32[]{:S(2)}) collective-permute-start(bf16[2,256,1536]{2,1,0:T(8,128)(2,1)S(1)} %copy-done.69), channel_id=1, source_target_pairs={{0,1},{1,0},{2,3},{3,2},{4,5},{5,4},{6,7},{7,6},{8,9},{9,8},{10,11... | collective-permute-start | bytes 4718600 | tf_op jit(solution)/shard_map/ppermute | solution.py:392
  743.5 51.5 %collective-permute-start.56 = (bf16[2,256,1536]{2,1,0:T(8,128)(2,1)}, bf16[2,256,1536]{2,1,0:T(8,128)(2,1)S(1)}, u32[]{:S(2)}, u32[]{:S(2)}) collective-permute-start(bf16[2,256,1536]{2,1,0:T(8,128)(2,1)} %back_sum.15), channel_id=1, source_target_pairs={{0,1},{1,0},{2,3},{3,2},{4,5},{5,4},{6,7},{7,6},{8,9},{9,8},{10,11... | collective-permute-start | bytes 4718600 | tf_op jit(solution)/shard_map/ppermute | solution.py:392
  745.7 50.6 %collective-permute-start.51 = (bf16[2,256,1536]{2,1,0:T(8,128)(2,1)S(1)}, bf16[2,256,1536]{2,1,0:T(8,128)(2,1)S(1)}, u32[]{:S(2)}, u32[]{:S(2)}) collective-permute-start(bf16[2,256,1536]{2,1,0:T(8,128)(2,1)S(1)} %copy-done.70), channel_id=1, source_target_pairs={{0,1},{1,0},{2,3},{3,2},{4,5},{5,4},{6,7},{7,6},{8,9},{9,8},{10,11... | collective-permute-start | bytes 4718600 | tf_op jit(solution)/shard_map/ppermute | solution.py:392
  793.1 35.8 %collective-permute-start.110 = (f32[192,1536]{1,0:T(8,128)}, f32[192,1536]{1,0:T(8,128)}, u32[]{:S(2)}, u32[]{:S(2)}) collective-permute-start(f32[192,1536]{1,0:T(8,128)} %convert_add_fusion.5), channel_id=1, source_target_pairs={{0,1},{1,0},{2,3},{3,2},{4,5},{5,4},{6,7},{7,6},{8,9},{9,8},{10,11... | collective-permute-start | bytes 3538952 | tf_op jit(solution)/shard_map/ppermute | solution.py:392
  795.0 36.4 %collective-permute-start.102 = (bf16[192,1536]{1,0:T(8,128)(2,1)}, bf16[192,1536]{1,0:T(8,128)(2,1)}, u32[]{:S(2)}, u32[]{:S(2)}) collective-permute-start(bf16[192,1536]{1,0:T(8,128)(2,1)} %add_convert_fusion.5), channel_id=1, source_target_pairs={{4,12},{12,20},{20,28},{28,24},{24,16},{16,8},{8,0},{0,4},{5,13},{... | collective-permute-start | bytes 1769480 | tf_op jit(solution)/shard_map/ppermute | solution.py:326
  796.3 35.2 %collective-permute-start.106 = (bf16[192,1536]{1,0:T(8,128)(2,1)}, bf16[192,1536]{1,0:T(8,128)(2,1)}, u32[]{:S(2)}, u32[]{:S(2)}) collective-permute-start(bf16[192,1536]{1,0:T(8,128)(2,1)} %add_convert_fusion.3), channel_id=1, source_target_pairs={{4,0},{12,4},{20,12},{28,20},{24,28},{16,24},{8,16},{0,8},{5,1},{1... | collective-permute-start | bytes 1769480 | tf_op jit(solution)/shard_map/ppermute | solution.py:326
  826.3 173.4 %collective-permute-start.61 = (bf16[2,2,256,1536]{3,2,1,0:T(8,128)(2,1)}, bf16[2,2,256,1536]{3,2,1,0:T(8,128)(2,1)}, u32[]{:S(2)}, u32[]{:S(2)}) collective-permute-start(bf16[2,2,256,1536]{3,2,1,0:T(8,128)(2,1)} %pad_maximum_fusion.6), channel_id=1, source_target_pairs={{0,1},{1,0},{2,3},{3,2},{4,5},{5,4},{6,7},{7,6},{8,9},{9,8},{10,11... | collective-permute-start | bytes 9437192 | tf_op jit(solution)/shard_map/ppermute | solution.py:392
  828.9 59.8 %collective-permute-start.58 = (bf16[512,384]{1,0:T(8,128)(2,1)S(1)}, bf16[512,384]{1,0:T(8,128)(2,1)S(1)}, u32[]{:S(2)}, u32[]{:S(2)}) collective-permute-start(bf16[512,384]{1,0:T(8,128)(2,1)S(1)} %fusion.112), channel_id=1, source_target_pairs={{0,2},{1,3},{2,0},{3,1},{4,6},{5,7},{6,4},{7,5},{8,10},{9,11},{10,... | collective-permute-start | bytes 1179656 | tf_op jit(solution)/shard_map/ppermute | solution.py:464
  833.7 106.5 %collective-permute-start.107 = (bf16[192,1536]{1,0:T(8,128)(2,1)}, bf16[192,1536]{1,0:T(8,128)(2,1)}, u32[]{:S(2)}, u32[]{:S(2)}) collective-permute-start(bf16[192,1536]{1,0:T(8,128)(2,1)} %add_convert_fusion.2), channel_id=1, source_target_pairs={{0,2},{1,3},{2,0},{3,1},{4,6},{5,7},{6,4},{7,5},{8,10},{9,11},{10,... | collective-permute-start | bytes 1769480 | tf_op jit(solution)/shard_map/ppermute | solution.py:610
  886.8 56.2 %collective-permute-start.54 = (bf16[512,1152]{1,0:T(8,128)(2,1)}, bf16[512,1152]{1,0:T(8,128)(2,1)}, u32[]{:S(2)}, u32[]{:S(2)}) collective-permute-start(bf16[512,1152]{1,0:T(8,128)(2,1)} %constant_dynamic-slice_fusion.94), channel_id=1, source_target_pairs={{0,2},{1,3},{2,0},{3,1},{4,6},{5,7},{6,4},{7,5},{8,10},{9,11},{10,... | collective-permute-start | bytes 3538952 | tf_op jit(solution)/shard_map/ppermute | solution.py:480
  936.9 26.5 %collective-permute-start.59 = (bf16[512,1152]{1,0:T(8,128)(2,1)}, bf16[512,1152]{1,0:T(8,128)(2,1)}, u32[]{:S(2)}, u32[]{:S(2)}) collective-permute-start(bf16[512,1152]{1,0:T(8,128)(2,1)} %constant_dynamic-slice_fusion.92), channel_id=1, source_target_pairs={{0,2},{1,3},{2,0},{3,1},{4,6},{5,7},{6,4},{7,5},{8,10},{9,11},{10,... | collective-permute-start | bytes 3538952 | tf_op jit(solution)/shard_map/ppermute | solution.py:480
  941.8 49.7 %collective-permute-start.111 = (f32[192,1536]{1,0:T(8,128)S(1)}, f32[192,1536]{1,0:T(8,128)S(1)}, u32[]{:S(2)}, u32[]{:S(2)}) collective-permute-start(f32[192,1536]{1,0:T(8,128)S(1)} %convert_add_fusion.4), channel_id=1, source_target_pairs={{0,1},{1,0},{2,3},{3,2},{4,5},{5,4},{6,7},{7,6},{8,9},{9,8},{10,11... | collective-permute-start | bytes 3538952 | tf_op jit(solution)/shard_map/ppermute | solution.py:392
  977.8 37.6 %collective-permute-start.62 = (bf16[192,768]{1,0:T(8,128)(2,1)}, bf16[192,768]{1,0:T(8,128)(2,1)}, u32[]{:S(2)}, u32[]{:S(2)}) collective-permute-start(bf16[192,768]{1,0:T(8,128)(2,1)} %get-tuple-element.82), channel_id=1, source_target_pairs={{4,12},{12,20},{20,28},{28,24},{24,16},{16,8},{8,0},{0,4},{5,13},{... | collective-permute-start | bytes 884744 | tf_op jit(solution)/shard_map/ppermute | solution.py:326
  983.6 73.0 %collective-permute-start.55 = (bf16[2,256,1536]{2,1,0:T(8,128)(2,1)}, bf16[2,256,1536]{2,1,0:T(8,128)(2,1)}, u32[]{:S(2)}, u32[]{:S(2)}) collective-permute-start(bf16[2,256,1536]{2,1,0:T(8,128)(2,1)} %convolution_convert_fusion.4), channel_id=1, source_target_pairs={{0,1},{1,0},{2,3},{3,2},{4,5},{5,4},{6,7},{7,6},{8,9},{9,8},{10,11... | collective-permute-start | bytes 4718600 | tf_op jit(solution)/shard_map/ppermute | solution.py:392
  989.1 52.1 %collective-permute-start.60 = (bf16[2,256,1536]{2,1,0:T(8,128)(2,1)}, bf16[2,256,1536]{2,1,0:T(8,128)(2,1)}, u32[]{:S(2)}, u32[]{:S(2)}) collective-permute-start(bf16[2,256,1536]{2,1,0:T(8,128)(2,1)} %convolution_convert_fusion.3), channel_id=1, source_target_pairs={{0,1},{1,0},{2,3},{3,2},{4,5},{5,4},{6,7},{7,6},{8,9},{9,8},{10,11... | collective-permute-start | bytes 4718600 | tf_op jit(solution)/shard_map/ppermute | solution.py:392
  1048.7 54.5 %collective-permute-start.65 = (bf16[192,1536]{1,0:T(8,128)(2,1)}, bf16[192,1536]{1,0:T(8,128)(2,1)}, u32[]{:S(2)}, u32[]{:S(2)}) collective-permute-start(bf16[192,1536]{1,0:T(8,128)(2,1)} %add_convert_fusion.25), channel_id=1, source_target_pairs={{4,12},{12,20},{20,28},{28,24},{24,16},{16,8},{8,0},{0,4},{5,13},{... | collective-permute-start | bytes 1769480 | tf_op jit(solution)/shard_map/ppermute | solution.py:326
  1054.8 48.4 %collective-permute-start.69 = (bf16[192,1536]{1,0:T(8,128)(2,1)}, bf16[192,1536]{1,0:T(8,128)(2,1)}, u32[]{:S(2)}, u32[]{:S(2)}) collective-permute-start(bf16[192,1536]{1,0:T(8,128)(2,1)} %add_convert_fusion.23), channel_id=1, source_target_pairs={{4,0},{12,4},{20,12},{28,20},{24,28},{16,24},{8,16},{0,8},{5,1},{1... | collective-permute-start | bytes 1769480 | tf_op jit(solution)/shard_map/ppermute | solution.py:326
  (211 other events, 2662.4 us)

commit v2 on v1

--- a/solution.py
+++ b/solution.py
@@ -222,78 +222,14 @@
     )(length, diag, qkv, qkv, qkv, grad_mixed, lse)
 
 
-def gated_kernel(width, a_ref, d_ref, g_ref, e_ref):
-    gate = dot32(a_ref[...], g_ref[:, :width], NN)
-    up = dot32(a_ref[...], g_ref[:, width : 2 * width], NN)
-    grad = dot32(d_ref[...], g_ref[:, 2 * width :], NN)
+def gated_values(gate, up, grad):
     square = gate * gate
-    inner = gelu_scale * gate * (1.0 + gelu_cubic * square)
-    turn = jnp.tanh(inner)
+    turn = jnp.tanh(gelu_scale * gate * (1.0 + gelu_cubic * square))
     half = 0.5 * (1.0 + turn)
     act = gate * half
     slope = half + 0.5 * gate * (1.0 - turn * turn) * gelu_scale * (1.0 + 3.0 * gelu_cubic * square)
-    e_ref[:, :width] = (grad * up * slope).astype(e_ref.dtype)
-    e_ref[:, width : 2 * width] = (grad * act).astype(e_ref.dtype)
-    e_ref[:, 2 * width :] = (act * up).astype(e_ref.dtype)
-
-
-def gated_chunk(normed, down_in, weights, tile=256):
-    tokens, width = normed.shape[0], weights.shape[1] // 3
-    depth = normed.shape[1]
-    return pl.pallas_call(
-        functools.partial(gated_kernel, width),
-        grid=(tokens // tile,),
-        in_specs=[
-            pl.BlockSpec((tile, depth), lambda t: (t, 0)),
-            pl.BlockSpec((tile, depth), lambda t: (t, 0)),
-            pl.BlockSpec((depth, 3 * width), lambda t: (0, 0)),
-        ],
-        out_specs=pl.BlockSpec((tile, 3 * width), lambda t: (t, 0)),
-        out_shape=jax.ShapeDtypeStruct((tokens, 3 * width), jnp.bfloat16),
-        compiler_params=pltpu.CompilerParams(vmem_limit_bytes=VMEM_LIMIT),
-        cost_estimate=pl.CostEstimate(
-            flops=6 * tokens * depth * width, bytes_accessed=2 * (2 * tokens * depth + 6 * depth * width), transcendentals=0
-        ),
-        name="gated_chunk",
-    )(normed, down_in, weights)
-
-
-def back_kernel(count, *refs):
-    total = None
-    for index in range(count):
-        made = dot32(refs[index][...], refs[count + index][...], NT)
-        total = made if total is None else total + made
-    refs[-1][...] = total.astype(refs[-1].dtype)
-
-
-def back_sum(pieces, weights, start, width, block_at, half, dtype, tile=256):
-    count = len(pieces)
-    rows, _, _ = pieces[0].shape
-    depth = weights[0].shape[0]
-    tile = min(tile, half)
-    steps = half // tile
-
-    def body_of(start_ref, *refs):
-        back_kernel(count, *refs)
-
-    return pl.pallas_call(
-        body_of,
-        grid_spec=pltpu.PrefetchScalarGridSpec(
-            num_scalar_prefetch=1,
-            grid=(rows, steps),
-            in_specs=[pl.BlockSpec((None, tile, width), lambda r, t, s: (r, s[0] * steps + t, block_at))] * count
-            + [pl.BlockSpec((depth, width), lambda r, t, s: (0, block_at))] * count,
-            out_specs=pl.BlockSpec((None, tile, depth), lambda r, t, s: (r, t, 0)),
-        ),
-        out_shape=jax.ShapeDtypeStruct((rows, half, depth), dtype),
-        compiler_params=pltpu.CompilerParams(vmem_limit_bytes=VMEM_LIMIT),
-        cost_estimate=pl.CostEstimate(
-            flops=2 * rows * half * depth * width * count,
-            bytes_accessed=2 * count * width * (rows * half + depth) + 4 * rows * half * depth,
-            transcendentals=0,
-        ),
-        name="back_sum",
-    )(start, *pieces, *weights)
+    low = jnp.bfloat16
+    return (grad * up * slope).astype(low), (grad * act).astype(low), (act * up).astype(low)
 
 
 def ring_order(count):
@@ -305,6 +241,589 @@
         columns = range(1, short) if line % 2 == 0 else range(short - 1, 0, -1)
         walk += [line * short + column for column in columns]
     return walk + [line * short for line in range(long - 1, -1, -1)]
+
+
+MESH = pl.DeviceIdType.MESH
+
+
+def pick(options, at):
+    value = jnp.int32(options[0])
+    for index in range(1, len(options)):
+        value = jnp.where(at == index, jnp.int32(options[index]), value)
+    return value
+
+
+class Links:
+    def __init__(self, count, planes):
+        order = ring_order(count)
+        place = [0] * count
+        for at, index in enumerate(order):
+            place[index] = at
+        self.count, self.order, self.planes = count, order, planes
+        self.place = pick(place, lax.axis_index("dp"))
+        seq = lax.axis_index("seq")
+        self.core = seq % 2
+        self.plane = seq // 2
+        self.sibling = {"seq": self.plane * 2 + 1 - self.core}
+        self.across = {"seq": (1 - self.plane) * 2 + self.core}
+        self.ahead = {"dp": self.owner(1)}
+        self.behind = {"dp": self.owner(-1)}
+
+    def owner(self, shift):
+        return pick(self.order, lax.rem(self.place + shift + self.count, self.count))
+
+    def greet(self):
+        barrier = pltpu.get_barrier_semaphore()
+        friends = [self.ahead, self.behind, self.sibling] + ([self.across] if self.planes == 2 else [])
+        for friend in friends:
+            pl.semaphore_signal(barrier, inc=1, device_id=friend, device_id_type=MESH)
+        pl.semaphore_wait(barrier, len(friends))
+
+
+class Gather:
+    def __init__(self, links, shard, whole, sems, rows):
+        self.links, self.shard, self.whole, self.sems, self.rows = links, shard, whole, sems, rows
+        self.far = links.count // 2
+        self.shared = links.planes == 2
+        self.third = rows // 3
+        self.size = 2 * self.third if self.shared else rows
+        self.cut = -(-(self.size // 2) // 16) * 16
+
+    def base(self, shift):
+        start = self.links.owner(shift) * self.rows
+        if self.shared:
+            start = start + self.links.plane * self.third
+        return pl.multiple_of(start, 16)
+
+    def ring_copy(self, step, forward):
+        shift = (1 - step) if forward else (step - 1)
+        offset, size = 0, self.size
+        if step == self.far:
+            offset, size = (0, self.cut) if forward else (self.cut, self.size - self.cut)
+        place = self.whole.at[pl.ds(pl.multiple_of(self.base(shift) + offset, 16), size)]
+        source = place
+        if step == 1:
+            first = self.links.plane * self.third if self.shared else 0
+            source = self.shard.at[pl.ds(pl.multiple_of(first + offset, 16), size)]
+        return pltpu.make_async_remote_copy(
+            src_ref=source,
+            dst_ref=place,
+            send_sem=self.sems.at[0 if forward else 1, step],
+            recv_sem=self.sems.at[2 if forward else 3, step],
+            device_id=self.links.ahead if forward else self.links.behind,
+            device_id_type=MESH,
+        )
+
+    def recv_copy(self, step, forward):
+        shift = -step if forward else step
+        offset, size = 0, self.size
+        if step == self.far:
+            offset, size = (0, self.cut) if forward else (self.cut, self.size - self.cut)
+        place = self.whole.at[pl.ds(pl.multiple_of(self.base(shift) + offset, 16), size)]
+        return pltpu.make_async_remote_copy(
+            src_ref=place,
+            dst_ref=place,
+            send_sem=self.sems.at[0 if forward else 1, step],
+            recv_sem=self.sems.at[2 if forward else 3, step],
+            device_id=self.links.ahead if forward else self.links.behind,
+            device_id_type=MESH,
+        )
+
+    def across_copy(self, slot, shift, receive):
+        plane = 1 - self.links.plane if receive else self.links.plane
+        start = self.links.owner(shift) * self.rows + plane * 2 * self.third
+        place = self.whole.at[pl.ds(pl.multiple_of(start, 16), self.third)]
+        return pltpu.make_async_remote_copy(
+            src_ref=place,
+            dst_ref=place,
+            send_sem=self.sems.at[4, slot],
+            recv_sem=self.sems.at[5, slot],
+            device_id=self.links.across,
+            device_id_type=MESH,
+        )
+
+    def start(self):
+        self.ring_copy(1, True).start()
+        self.ring_copy(1, False).start()
+
+    def advance(self, step):
+        last = step == self.far
+        for forward in (True, False):
+            self.recv_copy(step, forward).wait_recv()
+            if not last:
+                self.ring_copy(step + 1, forward).start()
+            if self.shared and not last:
+                slot = 2 * step - 2 + (0 if forward else 1)
+                self.across_copy(slot, -step if forward else step, False).start()
+        if self.shared and last:
+            self.across_copy(2 * step - 2, step, False).start()
+
+    def slots(self):
+        shifts = []
+        for step in range(1, self.far):
+            shifts += [(2 * step - 2, -step), (2 * step - 1, step)]
+        return shifts + [(2 * self.far - 2, self.far)]
+
+    def finish(self):
+        for step in range(1, self.far + 1):
+            self.ring_copy(step, True).wait_send()
+            self.ring_copy(step, False).wait_send()
+        if self.shared:
+            for slot, shift in self.slots():
+                self.across_copy(slot, shift, False).wait_send()
+                self.across_copy(slot, shift, True).wait_recv()
+
+
+def gather_kernel(count, planes, rows, shard, small, tokens, cotangent, whole, smalls, tokens_there, cotangent_there, sems, sems_small, sems_core, own):
+    links = Links(count, planes)
+    keep = pltpu.make_async_copy(shard, whole.at[pl.ds(pl.multiple_of(links.owner(0) * rows, 16), rows)], own.at[0])
+    keep_small = pltpu.make_async_copy(small, smalls.at[pl.ds(pl.multiple_of(links.owner(0) * 16, 16), 16)], own.at[1])
+    keep.start()
+    keep_small.start()
+    links.greet()
+    large = Gather(links, shard, whole, sems, rows)
+    little = SmallGather(links, small, smalls, sems_small)
+    little.start()
+    large.start()
+    swaps = []
+    for at, (source, target) in enumerate(((tokens, tokens_there), (cotangent, cotangent_there))):
+        swaps.append(
+            pltpu.make_async_remote_copy(
+                src_ref=source, dst_ref=target, send_sem=sems_core.at[at, 0], recv_sem=sems_core.at[at, 1],
+                device_id=links.sibling, device_id_type=MESH,
+            )
+        )
+        swaps[-1].start()
+    for step in range(1, large.far + 1):
+        little.advance(step)
+        large.advance(step)
+    for swap in swaps:
+        swap.wait()
+    little.finish()
+    large.finish()
+    keep.wait()
+    keep_small.wait()
+
+
+class SmallGather(Gather):
+    def __init__(self, links, shard, whole, sems):
+        self.links, self.shard, self.whole, self.sems, self.rows = links, shard, whole, sems, 16
+        self.far, self.shared, self.size, self.cut = links.count // 2, False, 16, 16
+
+    def start(self):
+        self.ring_copy(1, True).start()
+        self.ring_copy(1, False).start()
+
+    def advance(self, step):
+        self.recv_copy(step, True).wait_recv()
+        if step < self.far:
+            self.ring_copy(step + 1, True).start()
+            self.recv_copy(step, False).wait_recv()
+            if step + 1 < self.far:
+                self.ring_copy(step + 1, False).start()
+
+    def finish(self):
+        for step in range(1, self.far + 1):
+            self.ring_copy(step, True).wait_send()
+            if step < self.far:
+                self.ring_copy(step, False).wait_send()
+
+
+def gather_first(shard, small, tokens, cotangent, count, planes):
+    rows, cols = shard.shape
+    anywhere = pl.BlockSpec(memory_space=pl.ANY)
+    return pl.pallas_call(
+        functools.partial(gather_kernel, count, planes, rows),
+        in_specs=[anywhere] * 4,
+        out_specs=[anywhere] * 4,
+        out_shape=[
+            jax.ShapeDtypeStruct((count * rows, cols), shard.dtype),
+            jax.ShapeDtypeStruct((count * 16, small.shape[1]), small.dtype),
+            jax.ShapeDtypeStruct(tokens.shape, tokens.dtype),
+            jax.ShapeDtypeStruct(cotangent.shape, cotangent.dtype),
+        ],
+        scratch_shapes=[
+            pltpu.SemaphoreType.DMA((6, count)),
+            pltpu.SemaphoreType.DMA((4, count)),
+            pltpu.SemaphoreType.DMA((2, 2)),
+            pltpu.SemaphoreType.DMA((2,)),
+        ],
+        compiler_params=pltpu.CompilerParams(collective_id=0, has_side_effects=True),
+        name="gather_first",
+    )(shard, small, tokens, cotangent)
+
+
+class Scatter:
+    def __init__(self, links, grads, inbox, totals, mine, came, made, total, send_sems, recv_sems, near_sems, total_sems, rows):
+        self.links, self.grads, self.inbox, self.totals = links, grads, inbox, totals
+        self.mine, self.came, self.made, self.total = mine, came, made, total
+        self.send_sems, self.recv_sems, self.near_sems, self.total_sems = send_sems, recv_sems, near_sems, total_sems
+        self.rows = rows
+        self.far = links.count // 2
+        self.cut = -(-(rows // 2) // 16) * 16
+        self.spaces = made.shape[0]
+
+    def part(self, step, way):
+        if step > 1:
+            return 0, self.rows
+        return (0, self.cut) if way == 0 else (self.cut, self.rows - self.cut)
+
+    def term(self, chunk, shift, offset, size):
+        start = self.links.owner(shift) * self.rows + offset
+        return self.grads.at[chunk, pl.ds(pl.multiple_of(start, 16), size)]
+
+    def hop(self, chunk, step, way):
+        offset, size = self.part(step, way)
+        if step == 1:
+            source = self.term(chunk, self.far, offset, size)
+        else:
+            source = self.made.at[lax.rem(chunk, self.spaces), way, pl.ds(offset, size)]
+        return pltpu.make_async_remote_copy(
+            src_ref=source,
+            dst_ref=self.inbox.at[chunk, way, step - 1, pl.ds(offset, size)],
+            send_sem=self.send_sems.at[chunk, way, step - 1],
+            recv_sem=self.recv_sems.at[chunk, way, step - 1],
+            device_id=self.links.behind if way else self.links.ahead,
+            device_id_type=MESH,
+        )
+
+    def near(self, chunk, step, way):
+        offset, size = self.part(step, way)
+        space = lax.rem(chunk, self.spaces)
+        shift = (step - self.far) if way else (self.far - step)
+        copies = [
+            pltpu.make_async_copy(
+                self.inbox.at[chunk, way, step - 1, pl.ds(offset, size)],
+                self.came.at[space, way, pl.ds(offset, size)],
+                self.near_sems.at[space, way, 0],
+            )
+        ]
+        if step < self.far or way == 0:
+            copies.append(
+                pltpu.make_async_copy(
+                    self.term(chunk, shift, 0, self.rows), self.mine.at[space, way], self.near_sems.at[space, way, 1]
+                )
+            )
+        return copies
+
+    def start(self, chunk):
+        for way in range(2):
+            self.hop(chunk, 1, way).start()
+
+    def fetch(self, chunk, step):
+        for way in range(2):
+            self.hop(chunk, step, way).wait_recv()
+            for copy in self.near(chunk, step, way):
+                copy.start()
+
+    def pass_on(self, chunk, step):
+        space = lax.rem(chunk, self.spaces)
+        for way in range(2):
+            for copy in self.near(chunk, step, way):
+                copy.wait()
+            self.hop(chunk, step, way).wait_send()
+            offset, size = self.part(step, way)
+            rows = pl.ds(offset, size)
+            if size < self.rows:
+                other = pl.ds(0 if way else size, self.rows - size)
+                self.made[space, way, other] = self.mine[space, way, other]
+            self.made[space, way, rows] = add_low(self.mine[space, way, rows], self.came[space, way, rows])
+            self.hop(chunk, step + 1, way).start()
+
+    def total_copy(self, chunk):
+        return pltpu.make_async_copy(self.total, self.totals.at[chunk], self.total_sems.at[0])
+
+    def close(self, chunk):
+        space = lax.rem(chunk, self.spaces)
+        for way in range(2):
+            for copy in self.near(chunk, self.far, way):
+                copy.wait()
+            self.hop(chunk, self.far, way).wait_send()
+
+        @pl.when(chunk > 0)
+        def _():
+            self.total_copy(chunk - 1).wait()
+
+        total = self.mine[space, 0].astype(jnp.float32) + self.came[space, 0].astype(jnp.float32)
+        self.total[...] = total + self.came[space, 1].astype(jnp.float32)
+        self.total_copy(chunk).start()
+
+
+def feed_kernel(plan, *refs):
+    count, planes, rows, chunks, early, tile, block, groups = plan
+    late = chunks - early
+    (normed, down, *rest) = refs
+    ready, shards = rest[:early], rest[early:chunks]
+    rest = rest[chunks:]
+    back_kept, back_got, out_kept, out_got, totals, pieces, grads, inbox = rest[:8]
+    wholes = rest[8 : 8 + late]
+    (
+        a_all, b_all, weights, piece, stage, mine, came, made, total, out_stage,
+        in_sems, piece_sems, stage_sems, fetch_sems, keep_sems, give_sems, take_sems,
+        send_sems, recv_sems, near_sems, total_sems, own_sems, *gather_sems,
+    ) = rest[8 + late :]
+    tokens, depth = a_all.shape
+    width = weights.shape[2] // 3
+    tiles, blocks = tokens // tile, depth // block
+    per = tiles + blocks
+    front = chunks * per
+    links = Links(count, planes)
+    far = count // 2
+
+    loads = [pltpu.make_async_copy(normed, a_all, in_sems.at[chunks]), pltpu.make_async_copy(down, b_all, in_sems.at[chunks + 1])]
+    loads += [pltpu.make_async_copy(ready[n], weights.at[n], in_sems.at[n]) for n in range(early)]
+    keeps = []
+    for n in range(late):
+        place = wholes[n].at[pl.ds(pl.multiple_of(links.owner(0) * rows, 16), rows)]
+        keeps.append(pltpu.make_async_copy(shards[n], place, own_sems.at[n]))
+    for copy in loads + keeps:
+        copy.start()
+    links.greet()
+    gathers = [Gather(links, shards[n], wholes[n], gather_sems[n], rows) for n in range(late)]
+    scatter = Scatter(
+        links, grads, inbox, totals, mine, came, made, total, send_sems, recv_sems, near_sems, total_sems, rows
+    )
+    loads[0].wait()
+    loads[1].wait()
+
+    gap_gather = max(1, 16 // far)
+    gap = max(2, 20 // far)
+
+    def load_weights(n):
+        source = ready[n] if n < early else wholes[n - early]
+        return pltpu.make_async_copy(source, weights.at[n], in_sems.at[n])
+
+    def piece_copy(n, t):
+        place = pl.ds(pl.multiple_of(t * tile, 16), tile)
+        return pltpu.make_async_copy(piece.at[place], pieces.at[n, place], piece_sems.at[t])
+
+    def stage_copy(n, b):
+        slot = lax.rem(b, 2)
+        place = pl.ds(pl.multiple_of(b * block, 16), block)
+        return pltpu.make_async_copy(stage.at[slot], grads.at[n, place], stage_sems.at[slot])
+
+    def back_rows(g, half):
+        start = (2 * g + half) * tile
+        return pl.ds(pl.multiple_of(start, 16), tile)
+
+    def fetch_copy(n, t):
+        half = jnp.where(lax.rem(t, 2) == 0, 1 - links.core, links.core)
+        slot = lax.rem(t, 2)
+        target = pl.ds(pl.multiple_of((slot * chunks + n) * tile, 16), tile)
+        return pltpu.make_async_copy(pieces.at[n, back_rows(t // 2, half)], piece.at[target], fetch_sems.at[slot, n])
+
+    def give_copy(kind, g):
+        target = (back_got, out_got)[kind]
+        return pltpu.make_async_remote_copy(
+            src_ref=out_stage.at[kind, 0], dst_ref=target.at[g], send_sem=give_sems.at[kind], recv_sem=take_sems.at[kind, g],
+            device_id=links.sibling, device_id_type=MESH,
+        )
+
+    def keep_copy(kind, g):
+        target = (back_kept, out_kept)[kind]
+        return pltpu.make_async_copy(out_stage.at[kind, 1], target.at[g], keep_sems.at[kind])
+
+    items_back = 4 * groups
+    last_event = front + 1 + gap * far
+    total_items = max(front + items_back, last_event + 1)
+
+    def item(i, carry):
+        n, j = i // per, lax.rem(i, per)
+
+        for k in range(late):
+            base = k * per
+            for step in range(far + 2):
+
+                @pl.when(i == base + step * gap_gather)
+                def _(k=k, step=step):
+                    if step == 0:
+                        gathers[k].start()
+                    elif step <= far:
+                        gathers[k].advance(step)
+                    else:
+                        gathers[k].finish()
+                        keeps[k].wait()
+                        load_weights(early + k).start()
+
+        def event(offset, act):
+            past = i - per - offset
+
+            @pl.when((past >= 0) & (past < front) & (lax.rem(past + per * 64, per) == 0))
+            def _():
+                act(past // per)
+
+        def begin(chunk):
+            for b in (blocks - 2, blocks - 1):
+                stage_copy(chunk, b).wait()
+            scatter.start(chunk)
+
+        event(0, begin)
+        for step in range(1, far + 1):
+            event(step * gap - 1, lambda chunk, step=step: scatter.fetch(chunk, step))
+            if step < far:
+                event(step * gap, lambda chunk, step=step: scatter.pass_on(chunk, step))
+            else:
+                event(step * gap, scatter.close)
+
+        @pl.when((i < front) & (j == 0))
+        def _():
+            for m in range(chunks):
+
+                @pl.when(n == m)
+                def _(m=m):
+                    load_weights(m).wait()
+
+        @pl.when((i < front) & (j < tiles))
+        def _():
+            @pl.when(n > 0)
+            def _():
+                piece_copy(n - 1, j).wait()
+
+            place = pl.ds(pl.multiple_of(j * tile, 16), tile)
+            a, d = a_all[place], b_all[place]
+            gate = dot32(a, weights[n, :, :width], NN)
+            up = dot32(a, weights[n, :, width : 2 * width], NN)
+            grad = dot32(d, weights[n, :, 2 * width :], NN)
+            d_gate, d_up, hidden = gated_values(gate, up, grad)
+            piece[place, :width] = d_gate
+            piece[place, width : 2 * width] = d_up
+            piece[place, 2 * width :] = hidden
+            piece_copy(n, j).start()
+
+        @pl.when((i < front) & (j >= tiles))
+        def _():
+            b = j - tiles
+
+            @pl.when(b >= 2)
+            def _():
+                stage_copy(n, b - 2).wait()
+
+            place = pl.ds(pl.multiple_of(b * block, LANES), block)
+            slot = lax.rem(b, 2)
+            first = dot32(a_all[:, place], piece[:, : 2 * width], TN)
+            stage[slot, :, : 2 * width] = first.astype(stage.dtype)
+            second = dot32(b_all[:, place], piece[:, 2 * width :], TN)
+            stage[slot, :, 2 * width :] = second.astype(stage.dtype)
+            stage_copy(n, b).start()
+
+        @pl.when(i == front)
+        def _():
+            for t in range(tiles):
+                piece_copy(chunks - 1, t).wait()
+            for m in range(chunks):
+                fetch_copy(m, 0).start()
+
+        at = i - front
+        t, kind_at = at // 2, lax.rem(at + 2 * per, 2)
+        for kind in range(2):
+
+            @pl.when((at >= 0) & (at < items_back) & (kind_at == kind))
+            def _(kind=kind):
+                slot, g = lax.rem(t, 2), t // 2
+                if kind == 0:
+                    for m in range(chunks):
+                        fetch_copy(m, t).wait()
+
+                    @pl.when(t + 1 < 2 * groups)
+                    def _():
+                        for m in range(chunks):
+                            fetch_copy(m, t + 1).start()
+
+                columns = slice(0, 2 * width) if kind == 0 else slice(2 * width, 3 * width)
+                made_sum = None
+                for m in range(chunks):
+                    place = pl.ds(pl.multiple_of((slot * chunks + m) * tile, 16), tile)
+                    term = dot32(piece[place, columns], weights[m, :, columns], NT)
+                    made_sum = term if made_sum is None else made_sum + term
+
+                @pl.when((t >= 2) & (slot == 0))
+                def _():
+                    give_copy(kind, g - 1).wait_send()
+
+                @pl.when((t >= 2) & (slot == 1))
+                def _():
+                    keep_copy(kind, g - 1).wait()
+
+                out_stage[kind, slot] = made_sum.astype(out_stage.dtype)
+
+                @pl.when(slot == 0)
+                def _():
+                    give_copy(kind, g).start()
+
+                @pl.when(slot == 1)
+                def _():
+                    keep_copy(kind, g).start()
+
+        return carry
+
+    lax.fori_loop(0, total_items, item, 0)
+    scatter.total_copy(chunks - 1).wait()
+    for kind in range(2):
+        give_copy(kind, groups - 1).wait_send()
+        keep_copy(kind, groups - 1).wait()
+        for g in range(groups):
+            give_copy(kind, g).wait_recv()
+
+
+def feed(normed, down, ready, shards, count, planes, tile):
+    tokens, depth = normed.shape
+    rows, cols = shards[0].shape
+    early, chunks = len(ready), len(ready) + len(shards)
+    far = count // 2
+    block = 384
+    groups = tokens // (2 * tile)
+    spaces = 2 if far <= 4 else chunks
+    plan = (count, planes, rows, chunks, early, tile, block, groups)
+    anywhere = pl.BlockSpec(memory_space=pl.ANY)
+    low, wide = jnp.bfloat16, jnp.float32
+    part = jax.ShapeDtypeStruct((groups, tile, depth), low)
+    shapes = [part] * 4 + [
+        jax.ShapeDtypeStruct((chunks, rows, cols), wide),
+        jax.ShapeDtypeStruct((chunks, tokens, cols), low),
+        jax.ShapeDtypeStruct((chunks, depth, cols), low),
+        jax.ShapeDtypeStruct((chunks, 2, far, rows, cols), low),
+    ]
+    shapes += [jax.ShapeDtypeStruct((depth, cols), low)] * len(shards)
+    dma = pltpu.SemaphoreType.DMA
+    made = pl.pallas_call(
+        functools.partial(feed_kernel, plan),
+        in_specs=[anywhere] * (2 + chunks),
+        out_specs=[anywhere] * len(shapes),
+        out_shape=shapes,
+        scratch_shapes=[
+            pltpu.VMEM((tokens, depth), low),
+            pltpu.VMEM((tokens, depth), low),
+            pltpu.VMEM((chunks, depth, cols), low),
+            pltpu.VMEM((tokens, cols), low),
+            pltpu.VMEM((2, block, cols), low),
+            pltpu.VMEM((spaces, 2, rows, cols), low),
+            pltpu.VMEM((spaces, 2, rows, cols), low),
+            pltpu.VMEM((spaces, 2, rows, cols), low),
+            pltpu.VMEM((rows, cols), wide),
+            pltpu.VMEM((2, 2, tile, depth), low),
+            dma((chunks + 2,)),
+            dma((tokens // tile,)),
+            dma((2,)),
+            dma((2, chunks)),
+            dma((2,)),
+            dma((2,)),
+            dma((2, groups)),
+            dma((chunks, 2, far)),
+            dma((chunks, 2, far)),
+            dma((spaces, 2, 2)),
+            dma((1,)),
+            dma((len(shards),)),
+        ]
+        + [dma((6, count))] * len(shards),
+        compiler_params=pltpu.CompilerParams(
+            collective_id=1, has_side_effects=True, vmem_limit_bytes=62 * 1024 * 1024
+        ),
+        cost_estimate=pl.CostEstimate(
+            flops=18 * tokens * depth * cols // 3 * chunks, bytes_accessed=10 * tokens * depth, transcendentals=0
+        ),
+        name="feed",
+    )(normed, down, *ready, *shards)
+    return made[:5]
 
 
 class Ring:
@@ -418,26 +937,28 @@
         jnp.concatenate([w[:, n * chunk : (n + 1) * chunk] for w in up_parts], axis=1) for n in range(chunks)
     ]
 
-    small = jnp.concatenate([gain_one, gain_two, table.reshape(-1)])[None]
-    small = lax.all_gather(small, "dp", axis=0, tiled=True).astype(jnp.float32)
+    small = jnp.concatenate([gain_one, gain_two, table.reshape(-1)])
+    small = jnp.pad(small, (0, -small.shape[0] % LANES))
+    small = jnp.pad(small[None], ((0, 15), (0, 0)))
+    attn_weights, small, tokens_other, cotangent_other = gather_first(
+        attn_shard, small, tokens, cotangent, dp_devices, planes
+    )
+    small = small.reshape(dp_devices, 16, -1)[:, 0].astype(jnp.float32)
     gain_first = small[:, :shard_rows].reshape(-1)
     gain_second = small[:, shard_rows : 2 * shard_rows].reshape(-1)
-    full_table = small[:, 2 * shard_rows :].reshape(-1, heads)
-
-    attn_weights, last = ring.gather(attn_shard)
+    full_table = small[:, 2 * shard_rows : 2 * shard_rows + table.size].reshape(-1, heads)
+    last = attn_weights
     qkv_weights = attn_weights[:, : 3 * half_inner]
     out_own = attn_weights[:, 3 * half_inner :]
     out_other = swap_core(out_own)
     out_pair = jnp.concatenate([out_own, out_other], axis=1)
 
-    chunk_weights = []
-    for shard in chunk_shards:
+    early = min(2, chunks - 1)
+    ready = []
+    for shard in chunk_shards[:early]:
         shard, last = lax.optimization_barrier((shard, last))
-        gathered, last = ring.gather(shard)
-        chunk_weights.append(gathered)
-
-    tokens_other = swap_core(tokens)
-    cotangent_other = swap_core(cotangent)
+        ready.append(lax.all_gather(shard, "dp", axis=0, tiled=True))
+
     tokens_pair = both_cores(tokens, tokens_other, 2)
     down_in = both_cores(cotangent, cotangent_other, 2)
 
@@ -510,37 +1031,20 @@
         normed_twos.append((resid * root * gain_second).astype(jnp.bfloat16))
         resids.append(own_half(resid, 1))
 
-    pair_tokens = rows * pair_local
     flat = lambda value: value.reshape(-1, value.shape[-1])
     normed_two_all = jnp.concatenate([flat(v) for v in normed_twos])
     down_all = flat(down_in)
-    pieces = [[None] * chunks for _ in range(micro)]
-    chunk_totals = []
-    for n in range(chunks):
-        for step in range(micro):
-            rowsl = slice(step * pair_tokens, (step + 1) * pair_tokens)
-            pieces[step][n] = gated_chunk(flat(normed_twos[step]), down_all[rowsl], chunk_weights[n])
-        joined = jnp.concatenate([pieces[step][n] for step in range(micro)])
-        grad_gu = jnp.einsum("td,tf->df", normed_two_all, joined[:, : 2 * chunk], preferred_element_type=jnp.float32)
-        grad_dn = jnp.einsum("td,tf->df", down_all, joined[:, 2 * chunk :], preferred_element_type=jnp.float32)
-        grad_gu, grad_dn = grad_gu.astype(jnp.bfloat16), grad_dn.astype(jnp.bfloat16)
-
-        def local_term(index, grad_gu=grad_gu, grad_dn=grad_dn):
-            return jnp.concatenate(
-                [lax.dynamic_slice_in_dim(g, index * shard_rows, shard_rows, 0) for g in (grad_gu, grad_dn)], axis=1
-            )
-
-        chunk_totals.append(ring.scatter(local_term, 3 * chunk))
-
-    pieces = [[p.reshape(rows, pair_local, 3 * chunk) for p in per] for per in pieces]
-    core_at = core.astype(jnp.int32)[None]
+    back_kept, back_got, out_kept, out_got, chunk_totals = feed(
+        normed_two_all, down_all, ready, chunk_shards[early:], dp_devices, planes, local
+    )
+    back_kept, back_got, out_kept, out_got = [
+        v.reshape(micro, rows, local, width).astype(jnp.float32) for v in (back_kept, back_got, out_kept, out_got)
+    ]
+
     grad_resids, grads_mixed, attn_ins = [], [], []
     gain_two_sum = jnp.zeros((width,), jnp.float32)
     for step in range(micro):
-        sent = back_sum(pieces[step], chunk_weights, 1 - core_at, 2 * chunk, 0, local, jnp.bfloat16)
-        got = swap_core(sent)
-        kept = back_sum(pieces[step], chunk_weights, core_at, 2 * chunk, 0, local, jnp.float32)
-        grad_normed = kept + got.astype(jnp.float32)
+        grad_normed = back_kept[step] + back_got[step]
         resid = resids[step]
         root = lax.rsqrt(jnp.mean(resid * resid, axis=-1, keepdims=True) + eps)
         gain_two_sum = gain_two_sum + jnp.sum(grad_normed * resid * root, axis=(0, 1))
@@ -558,10 +1062,7 @@
 
     outputs = []
     for step in range(micro):
-        sent = back_sum(pieces[step], chunk_weights, 1 - core_at, chunk, 2, local, jnp.bfloat16)
-        got = swap_core(sent)
-        kept = back_sum(pieces[step], chunk_weights, core_at, chunk, 2, local, jnp.float32)
-        outputs.append((resids[step] + kept + got.astype(jnp.float32)).astype(jnp.bfloat16))
+        outputs.append((resids[step] + out_kept[step] + out_got[step]).astype(jnp.bfloat16))
 
     grads_qkv = []
     diag_sum = 0.0
@@ -620,7 +1121,7 @@
     own, other = finish(attn_total)
     parts = [slice(i * half_inner, (i + 1) * half_inner) for i in range(4)]
     grad_query, grad_key, grad_value, grad_out = [whole_columns(own[:, p], other[:, p], inner) for p in parts]
-    done = [finish(total) for total in chunk_totals]
+    done = [finish(chunk_totals[n]) for n in range(chunks)]
     parts = [slice(i * chunk, (i + 1) * chunk) for i in range(3)]
     grad_gate, grad_up, grad_down = [
         whole_columns(

time: 1140 us -> 899 us (0.79)
  waiting for transfers between devices: 257 us -> 102 us
  Pallas kernels: 293 us -> 437 us
  starting transfers between devices: 108 us -> 26.5 us
  matrix products: 134 us -> 63.1 us
  local copies, waits for them, and re-layouts: 130 us -> 71.4 us
  blocking collectives: 61.6 us -> 38.9 us
    ppermute x80 -> x8, waiting for transfers between devices: 213 us -> 19.9 us  [send(): return lax.ppermute(block, 'dp', self.ahead if forward else self.behind)]
    pallas_call x16 -> x2, Pallas kernels: 168 us -> 312 us  [the longest x1 265 us: feed(): pl.pallas_call(functools.partial(feed_kernel, plan), in_specs=[anywhere]...]
    ppermute x80 -> x8, starting transfers between devices: 87.6 us -> 9.64 us  [send(): return lax.ppermute(block, 'dp', self.ahead if forward else self.behind)]
    dot_general x8 -> x0, matrix products: 65.9 us -> none  [the longest x4 39.6 us: body(): jnp.einsum('td,tf->df', normed_two_all, joined[:, :2 * chunk], preferred_...]
    dynamic_update_slice x44 -> x0, local copies, waits for them, and re-layouts: 39.2 us -> none  [put(): lax.dynamic_update_slice(whole, block, (self.owner(shift) * rows, column))]
    unnamed x1 -> x0, blocking collectives: 22.4 us -> none
    ppermute x4, waiting for transfers between devices: 21 us -> 40.7 us  [from_items(): got = lax.ppermute(sent, 'seq', [(i, i ^ 2) for i in range(4)])]
    convert_element_type x30 -> x6, other arithmetic: 20.7 us -> 3.39 us  [add_low(): return (a.astype(jnp.float32) + b.astype(jnp.float32)).astype(jnp.bfloat16)]
  transfers between devices with their start and end apart: 112 -> 36, of which waited for: 38 -> 11; matrix products, arithmetic and copies ran while one was open for 32% -> 24% of each run, Pallas kernels for 26% -> 14%
where the time goes in v2:
time: 899 us; the launch traced here: 887 us
  Pallas kernels  437 us (49%)
  other arithmetic  121 us (13%)
  waiting for transfers between devices  102 us (11%)
  local copies, waits for them, and re-layouts  71.4 us (8%)
  matrix products  63.1 us (7%)
  blocking collectives  38.9 us (4%)
  between operations  27.6 us (3%)
  starting transfers between devices  26.5 us (3%)
    pallas_call x1, Pallas kernels, feed(): pl.pallas_call(functools.partial(feed_kernel, plan), in_specs=[anywhere]...  265 us
    pallas_call x2, Pallas kernels, attend_back(): pl.pallas_call(functools.partial(attend_back_kernel, head_dim, block), gr...  83.3 us
    pallas_call x1, Pallas kernels, gather_first(): pl.pallas_call(functools.partial(gather_kernel, count, planes, rows), in_...  46.9 us
    pallas_call x2, Pallas kernels, attend(): pl.pallas_call(functools.partial(attend_kernel, head_dim, block), grid=(p...  42.2 us
    ppermute x4, waiting for transfers between devices, from_items(): got = lax.ppermute(sent, 'seq', [(i, i ^ 2) for i in range(4)])  40.7 us
    psum x1, blocking collectives, body(): lax.psum(jnp.concatenate([gain_one_sum, gain_two_sum, grad_table.T.reshap...  38.9 us
    unnamed x211, local copies, waits for them, and re-layouts  26.6 us
    ppermute x5, waiting for transfers between devices, finish(): got = lax.ppermute(low, 'seq', [(i, i ^ 2) for i in range(4)])  24.3 us
  transfers between devices with their start and end apart: 36, of which 11 were waited for; matrix products, arithmetic and copies ran while one was open for 24% of the time, Pallas kernels for 14%

profile of v2, /device:TPU:0, one launch (start us, length us, event | category | flops | bytes accessed | tf_op | source)
XLA Modules:
  0.0 887.4 jit_solution(12642299992131940314)
XLA Ops:
  20.9 46.9 %gather_first.1 = (bf16[1536,1536]{1,0:T(8,128)(2,1)}, bf16[128,512]{1,0:T(8,128)(2,1)}, bf16[2,2,256,1536]{3,2,1,0:T(8,128)(2,1)}, bf16[2,2,256,1536]{3,2,1,0:T(8,128)(2,1)}) custom-call(bf16[192,1536]{1,0:T(8,128)(2,1)} %pad_maximum_fusion.23.shard, bf16[16,512]{1,0:T(8,128)(2,1)} %pad.26.small, bf16[2,2,256,1536]{3,2,1,0:T(8,128)(2,1)} %tokens.1, ...), custom_call_target="tpu_custom_call" | custom-call | tf_op jit(solution)/shard_map/gather_first/pallas_call | solution.py:435
  70.2 2.4 broadcast_select_fusion.5
  74.9 4.6 convolution_convert_fusion.1
  83.0 4.6 convolution_convert_fusion.2
  98.6 5.0 broadcast_select_fusion.3
  104.2 2.0 pad_maximum_fusion.26.refs_4_
  106.8 2.0 pad_maximum_fusion.27.refs_5_
  108.7 5.6 fusion.6
  117.4 20.7 %attend.3 = (bf16[1024,384]{1,0:T(8,128)(2,1)}, f32[6,1,1024]{2,1,0:T(1,128)}) custom-call(s32[1]{0:T(128)} %bitcast.13.len_ref, f32[6,1,2048]{2,1,0:T(1,128)} %broadcast_in_dim.7.diag_ref, bf16[1024,1152]{1,0:T(8,128)(2,1)} %pad_maximum_fusion.12.q_ref.k_ref.v_ref, bf16[1024,1152]{1,0:T(8,128)(2,1)} %pad_maximum_fusion.12.q_ref.k_ref.v_ref, ...), custom_call_target="tpu_custom_call" | custom-call | flops 6442450944 | bytes 3145728 | tf_op jit(solution)/shard_map/attend/pallas_call | solution.py:84
  142.8 21.5 %attend.2 = (bf16[1024,384]{1,0:T(8,128)(2,1)}, f32[6,1,1024]{2,1,0:T(1,128)}) custom-call(s32[1]{0:T(128)} %bitcast.2.len_ref, f32[6,1,2048]{2,1,0:T(1,128)} %broadcast_in_dim.7.diag_ref, bf16[1024,1152]{1,0:T(8,128)(2,1)} %pad_maximum_fusion.11.q_ref.k_ref.v_ref, bf16[1024,1152]{1,0:T(8,128)(2,1)} %pad_maximum_fusion.11.q_ref.k_ref.v_ref, ...), custom_call_target="tpu_custom_call" | custom-call | flops 6442450944 | bytes 3145728 | tf_op jit(solution)/shard_map/attend/pallas_call | solution.py:84
  169.1 3.0 pad_maximum_fusion.1
  172.1 5.4 collective-permute-done.1
  191.2 4.8 multiply_reduce_fusion
  196.4 3.8 copy-done.16
  200.2 4.7 multiply_reduce_fusion.1
  207.7 3.1 pad_maximum_fusion.refs_0_
  210.8 16.6 %all-gather.5.cloned.1.call-done.refs_3_ = bf16[1536,1536]{1,0:T(8,128)(2,1)} async-done(((bf16[192,1536]{1,0:T(8,128)(2,1)}), bf16[1536,1536]{1,0:T(8,128)(2,1)}) %all-gather.5.cloned.1.call-update) | async-done | bytes 4718608 | tf_op jit(solution)/shard_map/all_gather | solution.py:960
  227.4 264.6 %feed.1 = (bf16[4,256,1536]{2,1,0:T(8,128)(2,1)}, bf16[4,256,1536]{2,1,0:T(8,128)(2,1)}, bf16[4,256,1536]{2,1,0:T(8,128)(2,1)}, bf16[4,256,1536]{2,1,0:T(8,128)(...) custom-call(bf16[2048,1536]{1,0:T(8,128)(2,1)} %pad_maximum_fusion.r, ...), custom_call_target="tpu_custom_call" | custom-call | flops 115964116992 | bytes 31457280 | tf_op jit(solution)/shard_map/feed/pallas_call | solution.py:788
  492.0 2.6 convert.16
  497.0 2.1 collective-permute-start.26
  499.2 2.0 collective-permute-start.28
  505.1 3.9 convert_element_type.269
  509.0 2.3 copy-done.32
  511.3 3.9 convert_element_type.270
  515.7 2.4 multiply_reduce_fusion.3
  518.1 15.4 %fusion.53 = (bf16[1,2,256,1536]{3,2,1,0:T(8,128)(2,1)}, bf16[1,2,256,1536]{3,2,1,0:T(8,128)(2,1)}, bf16[1,2,256,1536]{3,2,1,0:T(8,128)(2,1)}, f32[2,256,1536]{2...) fusion(f32[4,256,1536]{2,1,0:T(8,128)} %convert_element_type.270, ...), kind=kLoop, calls=%fused_computation.116 | loop fusion | flops 17301504 | bytes 47200260 | tf_op jit(solution)/shard_map/stack | solution.py:1145
  533.5 3.3 convolution_convert_fusion.7
  536.9 2.4 convolution_convert_fusion.6
  539.4 2.2 convolution_convert_fusion.5
  541.7 2.4 convolution_convert_fusion.4
  550.6 2.0 collective-permute-start.8
  552.8 13.6 %collective-permute-done.29 = bf16[192,1536]{1,0:T(8,128)(2,1)S(1)} collective-permute-done((bf16[192,1536]{1,0:T(8,128)(2,1)S(1)}, bf16[192,1536]{1,0:T(8,128)(2,1)S(1)}, u32[]{:S(2)}, u32[]{:S(2)}) %collective-permute-start.29) | collective-permute-done | bytes 589856 | tf_op jit(solution)/shard_map/ppermute | solution.py:1111
  566.4 3.9 convert_add_fusion.7
  570.3 2.2 fusion.143
  573.0 2.3 fusion.144
  575.3 2.3 fusion.145
  577.5 2.3 fusion.146
  581.0 41.7 %attend_back.2 = (bf16[1024,384]{1,0:T(8,128)(2,1)}, bf16[1024,384]{1,0:T(8,128)(2,1)}, bf16[1024,384]{1,0:T(8,128)(2,1)}, f32[6,1,2048]{2,1,0:T(1,128)}) custom-call(s32[1]{0:T(128)} %bitcast.2.len_ref, f32[6,1,2048]{2,1,0:T(1,128)} %broadcast_in_dim.7.diag_ref, bf16[1024,1152]{1,0:T(8,128)(2,1)} %pad_maximum_fusion.11.q_ref.k_ref.v_ref, ...), custom_call_target="tpu_custom_call" | custom-call | flops 16106127360 | bytes 6291456 | tf_op jit(solution)/shard_map/attend_back/pallas_call | solution.py:193
  622.7 2.2 constant_dynamic-update-slice_fusion.2
  626.6 41.5 %attend_back.3 = (bf16[1024,384]{1,0:T(8,128)(2,1)}, bf16[1024,384]{1,0:T(8,128)(2,1)}, bf16[1024,384]{1,0:T(8,128)(2,1)}, f32[6,1,2048]{2,1,0:T(1,128)}) custom-call(s32[1]{0:T(128)} %bitcast.13.len_ref, f32[6,1,2048]{2,1,0:T(1,128)} %broadcast_in_dim.7.diag_ref, bf16[1024,1152]{1,0:T(8,128)(2,1)} %pad_maximum_fusion.12.q_ref.k_ref.v_ref, ...), custom_call_target="tpu_custom_call" | custom-call | flops 16106127360 | bytes 6291456 | tf_op jit(solution)/shard_map/attend_back/pallas_call | solution.py:193
  673.4 2.2 constant_dynamic-update-slice_fusion.1
  680.0 2.1 collective-permute-start.13
  696.0 11.4 %collective-permute-done.9 = bf16[512,1152]{1,0:T(8,128)(2,1)S(1)} collective-permute-done((bf16[512,1152]{1,0:T(8,128)(2,1)S(1)}, bf16[512,1152]{1,0:T(8,128)(2,1)S(1)}, u32[]{:S(2)}, u32[]{:S(2)}) %collective-permute-start.9) | collective-permute-done | bytes 1179680 | tf_op jit(solution)/shard_map/ppermute | solution.py:1001
  707.9 24.0 %collective-permute-done.13 = bf16[512,1152]{1,0:T(8,128)(2,1)S(1)} collective-permute-done((bf16[512,1152]{1,0:T(8,128)(2,1)S(1)}, bf16[512,1152]{1,0:T(8,128)(2,1)S(1)}, u32[]{:S(2)}, u32[]{:S(2)}) %collective-permute-start.13) | collective-permute-done | bytes 1179680 | tf_op jit(solution)/shard_map/ppermute | solution.py:1001
  737.8 11.3 %convolution_convert_fusion = bf16[1536,1152]{1,0:T(8,128)(2,1)S(1)} fusion(bf16[1024,1536]{1,0:T(8,128)(2,1)S(1)} %copy-done.31, bf16[1024,1536]{1,0:T(8,128)(2,1)S(1)} %copy-done.30, bf16[1024,1152]{1,0:T(8,128)(2,1)} %bitcast.230, bf16[1024,1152]{1,0:T(8,128)(2,1)} %bitcast.229), kind=kOutput, calls=%fused_computation | convolution fusion | flops 7271546880 | bytes 14548992 | tf_op jit(solution)/shard_map/td,te->de/dot_general | solution.py:1098
  750.0 2.3 collective-permute-start.16
  752.3 3.4 fusion.50
  758.7 2.1 broadcast_select_fusion.1
  760.8 3.1 pad_maximum_fusion.3
  763.9 6.8 convolution_convert_fusion.3
  773.0 2.1 collective-permute-start.17
  775.1 4.9 collective-permute-done.20
  780.5 2.2 fusion.47
  782.8 4.8 collective-permute-done.17
  789.5 4.3 collective-permute-done.21
  794.5 3.6 convert_add_fusion.2
  798.2 3.1 collective-permute-done.18
  803.7 2.9 collective-permute-done.22
  808.7 4.7 fusion.30
  813.4 38.9 %psum.7 = f32[3456]{0:T(1024)S(1)} all-reduce(f32[3456]{0:T(1024)S(1)} %pad_maximum_fusion.34), channel_id=1, replica_groups=mesh['dp'=8,'seq'=4] {'dp','seq'}, use_global_device_ids=true, to_apply=%region_14.15 | all-reduce | flops 3456 | bytes 27648 | tf_op jit(solution)/shard_map/psum | solution.py:1136
  854.2 2.4 collective-permute-start.24
  857.9 10.7 %collective-permute-done.24 = bf16[192,1536]{1,0:T(8,128)(2,1)S(1)} collective-permute-done((bf16[192,1536]{1,0:T(8,128)(2,1)S(1)}, bf16[192,1536]{1,0:T(8,128)(2,1)S(1)}, u32[]{:S(2)}, u32[]{:S(2)}) %collective-permute-start.24) | collective-permute-done | bytes 589856 | tf_op jit(solution)/shard_map/ppermute | solution.py:1111
  868.8 4.5 fusion.28
  873.3 3.1 pad_maximum_fusion.2
  (396 shorter events, 118.7 us)
Async XLA Ops:
  7.2 203.6 %all-gather.3.cloned.1.call-start = ((), (), s32[]{:S(2)}) async-start(), calls=%async_computation | async-start | bytes 5308416 | tf_op jit(solution)/shard_map/all_gather | solution.py:960
  20.9 49.3 %copy-start.7 = (bf16[2,2,256,1536]{3,2,1,0:T(8,128)(2,1)S(1)}, bf16[2,2,256,1536]{3,2,1,0:T(8,128)(2,1)}, u32[]{:S(2)}) copy-start(bf16[2,2,256,1536]{3,2,1,0:T(8,128)(2,1)} %tokens.1) | copy-start | bytes 9437188
  67.9 159.5 %all-gather.5.cloned.1.call-start = ((), (), s32[]{:S(2)}) async-start(), calls=%async_computation.1 | async-start | bytes 5308416 | tf_op jit(solution)/shard_map/all_gather | solution.py:960
  70.2 38.5 %copy-start.75 = (f32[1536]{0:T(1024)}, f32[1536]{0:T(1024)S(1)}, u32[]{:S(2)}) copy-start(f32[1536]{0:T(1024)S(1)} %mul.402) | copy-start | bytes 18436
  80.8 33.6 %collective-permute-start.4 = (bf16[512,1152]{1,0:T(8,128)(2,1)}, bf16[512,1152]{1,0:T(8,128)(2,1)}, u32[]{:S(2)}, u32[]{:S(2)}) collective-permute-start(bf16[512,1152]{1,0:T(8,128)(2,1)} %dynamic-slice_bitcast_fusion), channel_id=1, source_target_pairs={{0,2},{1,3},{2,0},{3,1},{4,6},{5,7},{6,4},{7,5},{8,10},{9,11},{10,... | collective-permute-start | bytes 3538952 | tf_op jit(solution)/shard_map/ppermute | solution.py:985
  82.4 108.8 %collective-permute-start.3 = (bf16[1536,384]{1,0:T(8,128)(2,1)}, bf16[1536,384]{1,0:T(8,128)(2,1)}, u32[]{:S(2)}, u32[]{:S(2)}) collective-permute-start(bf16[1536,384]{1,0:T(8,128)(2,1)} %slice.318), channel_id=1, source_target_pairs={{0,1},{1,0},{2,3},{3,2},{4,5},{5,4},{6,7},{7,6},{8,9},{9,8},{10,11... | collective-permute-start | bytes 3538952 | tf_op jit(solution)/shard_map/ppermute | solution.py:911
  90.1 49.6 %collective-permute-start = (bf16[512,1152]{1,0:T(8,128)(2,1)}, bf16[512,1152]{1,0:T(8,128)(2,1)}, u32[]{:S(2)}, u32[]{:S(2)}) collective-permute-start(bf16[512,1152]{1,0:T(8,128)(2,1)} %dynamic-slice_bitcast_fusion.1), channel_id=1, source_target_pairs={{0,2},{1,3},{2,0},{3,1},{4,6},{5,7},{6,4},{7,5},{8,10},{9,11},{10,... | collective-permute-start | bytes 3538952 | tf_op jit(solution)/shard_map/ppermute | solution.py:985
  117.4 22.3 %copy-start.39 = (bf16[2,512,1152]{2,1,0:T(8,128)(2,1)S(1)}, bf16[2,512,1152]{2,1,0:T(8,128)(2,1)}, u32[]{:S(2)}) copy-start(bf16[2,512,1152]{2,1,0:T(8,128)(2,1)} %copy-done.38) | copy-start | bytes 7077892
  139.2 28.6 %collective-permute-start.5 = (bf16[512,384]{1,0:T(8,128)(2,1)S(1)}, bf16[512,384]{1,0:T(8,128)(2,1)S(1)}, u32[]{:S(2)}, u32[]{:S(2)}) collective-permute-start(bf16[512,384]{1,0:T(8,128)(2,1)S(1)} %constant_dynamic-slice_fusion.23), channel_id=1, source_target_pairs={{0,2},{1,3},{2,0},{3,1},{4,6},{5,7},{6,4},{7,5},{8,10},{9,11},{10,... | collective-permute-start | bytes 1179656 | tf_op jit(solution)/shard_map/ppermute | solution.py:1001
  142.8 25.0 %copy-start.71 = (bf16[1024,384]{1,0:T(8,128)(2,1)S(1)}, bf16[1024,384]{1,0:T(8,128)(2,1)}, u32[]{:S(2)}) copy-start(bf16[1024,384]{1,0:T(8,128)(2,1)} %get-tuple-element.38) | copy-start | bytes 2359300
  142.8 26.2 %copy-start.20 = (bf16[2,2,256,1536]{3,2,1,0:T(8,128)(2,1)S(1)}, bf16[2,2,256,1536]{3,2,1,0:T(8,128)(2,1)}, u32[]{:S(2)}) copy-start(bf16[2,2,256,1536]{3,2,1,0:T(8,128)(2,1)} %get-tuple-element.87) | copy-start | bytes 9437188
  166.3 11.2 %collective-permute-start.1 = (bf16[512,384]{1,0:T(8,128)(2,1)}, bf16[512,384]{1,0:T(8,128)(2,1)S(1)}, u32[]{:S(2)}, u32[]{:S(2)}) collective-permute-start(bf16[512,384]{1,0:T(8,128)(2,1)} %constant_dynamic-slice_fusion.25), channel_id=1, source_target_pairs={{0,2},{1,3},{2,0},{3,1},{4,6},{5,7},{6,4},{7,5},{8,10},{9,11},{10,... | collective-permute-start | bytes 1179656 | tf_op jit(solution)/shard_map/ppermute | solution.py:1001
  169.0 22.1 %collective-permute-start.6 = (bf16[2,512,384]{2,1,0:T(8,128)(2,1)}, bf16[2,512,384]{2,1,0:T(8,128)(2,1)}, u32[]{:S(2)}, u32[]{:S(2)}) collective-permute-start(bf16[2,512,384]{2,1,0:T(8,128)(2,1)} %pad_maximum_fusion.20), channel_id=1, source_target_pairs={{0,1},{1,0},{2,3},{3,2},{4,5},{5,4},{6,7},{7,6},{8,9},{9,8},{10,11... | collective-permute-start | bytes 2359304 | tf_op jit(solution)/shard_map/ppermute | solution.py:911
  172.1 13.2 %copy-start.79 = (s32[8]{0:T(128)S(1)}, s32[8]{0:T(128)}, u32[]{:S(2)}) copy-start(s32[8]{0:T(128)} %constant.177.clone) | copy-start | bytes 100
  172.1 19.0 %copy-start.80 = (f32[8,192]{1,0:T(8,128)S(1)}, f32[8,192]{1,0:T(8,128)}, u32[]{:S(2)}) copy-start(f32[8,192]{1,0:T(8,128)} %get-tuple-element.199) | copy-start | bytes 18436
  172.1 19.1 %copy-start.18 = (bf16[1,2,512,1536]{3,2,1,0:T(8,128)(2,1)S(1)}, bf16[1,2,512,1536]{3,2,1,0:T(8,128)(2,1)}, u32[]{:S(2)}) copy-start(bf16[1,2,512,1536]{3,2,1,0:T(8,128)(2,1)} %copy-done.17) | copy-start | bytes 9437188
  179.4 16.9 %collective-permute-start.2 = (bf16[2,512,384]{2,1,0:T(8,128)(2,1)}, bf16[2,512,384]{2,1,0:T(8,128)(2,1)}, u32[]{:S(2)}, u32[]{:S(2)}) collective-permute-start(bf16[2,512,384]{2,1,0:T(8,128)(2,1)} %pad_maximum_fusion.19), channel_id=1, source_target_pairs={{0,1},{1,0},{2,3},{3,2},{4,5},{5,4},{6,7},{7,6},{8,9},{9,8},{10,11... | collective-permute-start | bytes 2359304 | tf_op jit(solution)/shard_map/ppermute | solution.py:911
  497.0 53.6 %collective-permute-start.26 = (bf16[192,1536]{1,0:T(8,128)(2,1)}, bf16[192,1536]{1,0:T(8,128)(2,1)}, u32[]{:S(2)}, u32[]{:S(2)}) collective-permute-start(bf16[192,1536]{1,0:T(8,128)(2,1)} %get-tuple-element.116), channel_id=1, source_target_pairs={{0,2},{1,3},{2,0},{3,1},{4,6},{5,7},{6,4},{7,5},{8,10},{9,11},{10,... | collective-permute-start | bytes 1769480 | tf_op jit(solution)/shard_map/ppermute | solution.py:1111
  499.1 53.5 %collective-permute-start.27 = (bf16[192,1536]{1,0:T(8,128)(2,1)}, bf16[192,1536]{1,0:T(8,128)(2,1)}, u32[]{:S(2)}, u32[]{:S(2)}) collective-permute-start(bf16[192,1536]{1,0:T(8,128)(2,1)} %get-tuple-element.119), channel_id=1, source_target_pairs={{0,2},{1,3},{2,0},{3,1},{4,6},{5,7},{6,4},{7,5},{8,10},{9,11},{10,... | collective-permute-start | bytes 1769480 | tf_op jit(solution)/shard_map/ppermute | solution.py:1111
  499.2 53.6 %collective-permute-start.28 = (bf16[192,1536]{1,0:T(8,128)(2,1)}, bf16[192,1536]{1,0:T(8,128)(2,1)}, u32[]{:S(2)}, u32[]{:S(2)}) collective-permute-start(bf16[192,1536]{1,0:T(8,128)(2,1)} %get-tuple-element.118), channel_id=1, source_target_pairs={{0,2},{1,3},{2,0},{3,1},{4,6},{5,7},{6,4},{7,5},{8,10},{9,11},{10,... | collective-permute-start | bytes 1769480 | tf_op jit(solution)/shard_map/ppermute | solution.py:1111
  503.1 12.1 %slice-start.2 = ((s8[6291456]{0:T(1024)(128)(4,1)}), s8[4194304]{0:T(1024)(128)(4,1)S(1)}, s32[]{:S(2)}) async-start(s8[6291456]{0:T(1024)(128)(4,1)} %bitcast.217), calls=%async_computation.4 | async-start | bytes 8388608
  503.9 11.2 %copy-start = (f32[4,256,1536]{2,1,0:T(8,128)}, f32[4,256,1536]{2,1,0:T(8,128)S(1)}, u32[]{:S(2)}) copy-start(f32[4,256,1536]{2,1,0:T(8,128)S(1)} %convert_element_type.276) | copy-start | bytes 18874372
  539.3 10.9 %collective-permute-start.7 = (bf16[2,256,384]{2,1,0:T(8,128)(2,1)S(1)}, bf16[2,256,384]{2,1,0:T(8,128)(2,1)S(1)}, u32[]{:S(2)}, u32[]{:S(2)}) collective-permute-start(bf16[2,256,384]{2,1,0:T(8,128)(2,1)S(1)} %convolution_convert_fusion.6), channel_id=1, source_target_pairs={{0,1},{1,0},{2,3},{3,2},{4,5},{5,4},{6,7},{7,6},{8,9},{9,8},{10,11... | collective-permute-start | bytes 1179656 | tf_op jit(solution)/shard_map/ppermute | solution.py:911
  544.1 6.3 collective-permute-start.11
  550.2 16.2 %collective-permute-start.29 = (bf16[192,1536]{1,0:T(8,128)(2,1)S(1)}, bf16[192,1536]{1,0:T(8,128)(2,1)S(1)}, u32[]{:S(2)}, u32[]{:S(2)}) collective-permute-start(bf16[192,1536]{1,0:T(8,128)(2,1)S(1)} %copy-done.73), channel_id=1, source_target_pairs={{0,2},{1,3},{2,0},{3,1},{4,6},{5,7},{6,4},{7,5},{8,10},{9,11},{10,... | collective-permute-start | bytes 1769480 | tf_op jit(solution)/shard_map/ppermute | solution.py:1111
  550.3 16.1 %copy-start.10 = (bf16[4,192,1536]{2,1,0:T(8,128)(2,1)S(1)}, bf16[4,192,1536]{2,1,0:T(8,128)(2,1)}, u32[]{:S(2)}) copy-start(bf16[4,192,1536]{2,1,0:T(8,128)(2,1)} %copy-done.9) | copy-start | bytes 7077892
  550.4 207.1 %collective-permute-start.15 = (bf16[2,2,256,1536]{3,2,1,0:T(8,128)(2,1)}, bf16[2,2,256,1536]{3,2,1,0:T(8,128)(2,1)}, u32[]{:S(2)}, u32[]{:S(2)}) collective-permute-start(bf16[2,2,256,1536]{3,2,1,0:T(8,128)(2,1)} %pad_maximum_fusion.6), channel_id=1, source_target_pairs={{0,1},{1,0},{2,3},{3,2},{4,5},{5,4},{6,7},{7,6},{8,9},{9,8},{10,11... | collective-permute-start | bytes 9437192 | tf_op jit(solution)/shard_map/ppermute | solution.py:911
  550.6 29.2 %collective-permute-start.8 = (bf16[512,384]{1,0:T(8,128)(2,1)S(1)}, bf16[512,384]{1,0:T(8,128)(2,1)S(1)}, u32[]{:S(2)}, u32[]{:S(2)}) collective-permute-start(bf16[512,384]{1,0:T(8,128)(2,1)S(1)} %fusion.102), channel_id=1, source_target_pairs={{0,2},{1,3},{2,0},{3,1},{4,6},{5,7},{6,4},{7,5},{8,10},{9,11},{10,... | collective-permute-start | bytes 1179656 | tf_op jit(solution)/shard_map/ppermute | solution.py:985
  552.7 72.2 %collective-permute-start.12 = (bf16[512,384]{1,0:T(8,128)(2,1)S(1)}, bf16[512,384]{1,0:T(8,128)(2,1)S(1)}, u32[]{:S(2)}, u32[]{:S(2)}) collective-permute-start(bf16[512,384]{1,0:T(8,128)(2,1)S(1)} %fusion.98), channel_id=1, source_target_pairs={{0,2},{1,3},{2,0},{3,1},{4,6},{5,7},{6,4},{7,5},{8,10},{9,11},{10,... | collective-permute-start | bytes 1179656 | tf_op jit(solution)/shard_map/ppermute | solution.py:985
  570.2 108.3 %collective-permute-start.30 = (f32[192,1536]{1,0:T(8,128)}, f32[192,1536]{1,0:T(8,128)}, u32[]{:S(2)}, u32[]{:S(2)}) collective-permute-start(f32[192,1536]{1,0:T(8,128)} %get-tuple-element.112), channel_id=1, source_target_pairs={{0,1},{1,0},{2,3},{3,2},{4,5},{5,4},{6,7},{7,6},{8,9},{9,8},{10,11... | collective-permute-start | bytes 3538952 | tf_op jit(solution)/shard_map/ppermute | solution.py:911
  572.5 107.5 %collective-permute-start.31 = (f32[192,1536]{1,0:T(8,128)}, f32[192,1536]{1,0:T(8,128)}, u32[]{:S(2)}, u32[]{:S(2)}) collective-permute-start(f32[192,1536]{1,0:T(8,128)} %get-tuple-element.115), channel_id=1, source_target_pairs={{0,1},{1,0},{2,3},{3,2},{4,5},{5,4},{6,7},{7,6},{8,9},{9,8},{10,11... | collective-permute-start | bytes 3538952 | tf_op jit(solution)/shard_map/ppermute | solution.py:911
  579.8 103.6 %collective-permute-start.32 = (f32[192,1536]{1,0:T(8,128)}, f32[192,1536]{1,0:T(8,128)}, u32[]{:S(2)}, u32[]{:S(2)}) collective-permute-start(f32[192,1536]{1,0:T(8,128)} %get-tuple-element.114), channel_id=1, source_target_pairs={{0,1},{1,0},{2,3},{3,2},{4,5},{5,4},{6,7},{7,6},{8,9},{9,8},{10,11... | collective-permute-start | bytes 3538952 | tf_op jit(solution)/shard_map/ppermute | solution.py:911
  624.9 59.9 %collective-permute-start.33 = (f32[192,1536]{1,0:T(8,128)}, f32[192,1536]{1,0:T(8,128)}, u32[]{:S(2)}, u32[]{:S(2)}) collective-permute-start(f32[192,1536]{1,0:T(8,128)} %get-tuple-element.113), channel_id=1, source_target_pairs={{0,1},{1,0},{2,3},{3,2},{4,5},{5,4},{6,7},{7,6},{8,9},{9,8},{10,11... | collective-permute-start | bytes 3538952 | tf_op jit(solution)/shard_map/ppermute | solution.py:911
  626.6 41.6 %copy-start.77 = (f32[6,1,2048]{2,1,0:T(1,128)S(1)}, f32[6,1,2048]{2,1,0:T(1,128)}, u32[]{:S(2)}) copy-start(f32[6,1,2048]{2,1,0:T(1,128)} %get-tuple-element.53) | copy-start | bytes 147460
  626.6 42.4 %copy-start.43 = (pred[2047,32]{1,0:T(8,128)(4,1)S(1)}, pred[2047,32]{1,0:T(8,128)(4,1)}, u32[]{:S(2)}) copy-start(pred[2047,32]{1,0:T(8,128)(4,1)} %copy-done.42) | copy-start | bytes 196516
  678.5 28.9 %collective-permute-start.9 = (bf16[512,1152]{1,0:T(8,128)(2,1)S(1)}, bf16[512,1152]{1,0:T(8,128)(2,1)S(1)}, u32[]{:S(2)}, u32[]{:S(2)}) collective-permute-start(bf16[512,1152]{1,0:T(8,128)(2,1)S(1)} %constant_dynamic-slice_fusion.22), channel_id=1, source_target_pairs={{0,2},{1,3},{2,0},{3,1},{4,6},{5,7},{6,4},{7,5},{8,10},{9,11},{10,... | collective-permute-start | bytes 3538952 | tf_op jit(solution)/shard_map/ppermute | solution.py:1001
  680.0 51.9 %collective-permute-start.13 = (bf16[512,1152]{1,0:T(8,128)(2,1)S(1)}, bf16[512,1152]{1,0:T(8,128)(2,1)S(1)}, u32[]{:S(2)}, u32[]{:S(2)}) collective-permute-start(bf16[512,1152]{1,0:T(8,128)(2,1)S(1)} %constant_dynamic-slice_fusion.20), channel_id=1, source_target_pairs={{0,2},{1,3},{2,0},{3,1},{4,6},{5,7},{6,4},{7,5},{8,10},{9,11},{10,... | collective-permute-start | bytes 3538952 | tf_op jit(solution)/shard_map/ppermute | solution.py:1001
  694.2 13.2 %copy-start.28 = (bf16[1024,1152]{1,0:T(8,128)(2,1)S(1)}, bf16[1024,1152]{1,0:T(8,128)(2,1)}, u32[]{:S(2)}) copy-start(bf16[1024,1152]{1,0:T(8,128)(2,1)} %constant_dynamic-update-slice_fusion) | copy-start | bytes 7077892
  732.4 19.9 %copy-start.24 = (bf16[1,512,1152]{2,1,0:T(8,128)(2,1)}, bf16[1,512,1152]{2,1,0:T(8,128)(2,1)S(1)}, u32[]{:S(2)}) copy-start(bf16[1,512,1152]{2,1,0:T(8,128)(2,1)S(1)} %get-tuple-element.104) | copy-start | bytes 3538948
  732.4 19.9 %copy-start.26 = (bf16[1,512,1152]{2,1,0:T(8,128)(2,1)}, bf16[1,512,1152]{2,1,0:T(8,128)(2,1)S(1)}, u32[]{:S(2)}) copy-start(bf16[1,512,1152]{2,1,0:T(8,128)(2,1)S(1)} %get-tuple-element.105) | copy-start | bytes 3538948
  734.1 18.2 %slice-start.8 = ((s8[4718592]{0:T(1024)(128)(4,1)}), s8[4194304]{0:T(1024)(128)(4,1)S(1)}, s32[]{:S(2)}) async-start(s8[4718592]{0:T(1024)(128)(4,1)} %bitcast.225), calls=%async_computation.10 | async-start | bytes 8388608
  737.8 14.5 %slice-start.9 = ((s8[4718592]{0:T(1024)(128)(4,1)}), s8[524288]{0:T(1024)(128)(4,1)S(1)}, s32[]{:S(2)}) async-start(s8[4718592]{0:T(1024)(128)(4,1)} %bitcast.225), calls=%async_computation.11 | async-start | bytes 1048576
  750.0 21.8 %collective-permute-start.16 = (bf16[192,768]{1,0:T(8,128)(2,1)}, bf16[192,768]{1,0:T(8,128)(2,1)}, u32[]{:S(2)}, u32[]{:S(2)}) collective-permute-start(bf16[192,768]{1,0:T(8,128)(2,1)} %get-tuple-element.100), channel_id=1, source_target_pairs={{4,12},{12,20},{20,28},{28,24},{24,16},{16,8},{8,0},{0,4},{5,13},{... | collective-permute-start | bytes 884744 | tf_op jit(solution)/shard_map/ppermute | solution.py:845
  755.7 38.8 %collective-permute-start.14 = (bf16[2,256,1536]{2,1,0:T(8,128)(2,1)}, bf16[2,256,1536]{2,1,0:T(8,128)(2,1)}, u32[]{:S(2)}, u32[]{:S(2)}) collective-permute-start(bf16[2,256,1536]{2,1,0:T(8,128)(2,1)} %fusion.50), channel_id=1, source_target_pairs={{0,1},{1,0},{2,3},{3,2},{4,5},{5,4},{6,7},{7,6},{8,9},{9,8},{10,11... | collective-permute-start | bytes 4718600 | tf_op jit(solution)/shard_map/ppermute | solution.py:911
  763.9 16.5 %slice-start.10 = ((s8[4718592]{0:T(1024)(128)(4,1)}), s8[4194304]{0:T(1024)(128)(4,1)S(1)}, s32[]{:S(2)}) async-start(s8[4718592]{0:T(1024)(128)(4,1)} %bitcast.227), calls=%async_computation.12 | async-start | bytes 8388608
  763.9 16.5 %slice-start.11 = ((s8[4718592]{0:T(1024)(128)(4,1)}), s8[524288]{0:T(1024)(128)(4,1)S(1)}, s32[]{:S(2)}) async-start(s8[4718592]{0:T(1024)(128)(4,1)} %bitcast.227), calls=%async_computation.13 | async-start | bytes 1048576
  771.8 8.2 collective-permute-start.20
  773.0 14.5 %collective-permute-start.17 = (bf16[192,1536]{1,0:T(8,128)(2,1)S(1)}, bf16[192,1536]{1,0:T(8,128)(2,1)S(1)}, u32[]{:S(2)}, u32[]{:S(2)}) collective-permute-start(bf16[192,1536]{1,0:T(8,128)(2,1)S(1)} %fusion.96), channel_id=1, source_target_pairs={{4,12},{12,20},{20,28},{28,24},{24,16},{16,8},{8,0},{0,4},{5,13},{... | collective-permute-start | bytes 1769480 | tf_op jit(solution)/shard_map/ppermute | solution.py:845
  780.1 13.6 %copy-start.45 = (bf16[192,1152]{1,0:T(8,128)(2,1)S(1)}, bf16[192,1152]{1,0:T(8,128)(2,1)}, u32[]{:S(2)}) copy-start(bf16[192,1152]{1,0:T(8,128)(2,1)} %get-tuple-element.94) | copy-start | bytes 1327108
  780.1 13.6 %collective-permute-start.21 = (bf16[192,1536]{1,0:T(8,128)(2,1)S(1)}, bf16[192,1536]{1,0:T(8,128)(2,1)S(1)}, u32[]{:S(2)}, u32[]{:S(2)}) collective-permute-start(bf16[192,1536]{1,0:T(8,128)(2,1)S(1)} %pad_maximum_fusion.28), channel_id=1, source_target_pairs={{4,0},{12,4},{20,12},{28,20},{24,28},{16,24},{8,16},{0,8},{5,1},{1... | collective-permute-start | bytes 1769480 | tf_op jit(solution)/shard_map/ppermute | solution.py:845
  782.7 11.8 %copy-start.25 = (bf16[1,512,1152]{2,1,0:T(8,128)(2,1)S(1)}, bf16[1,512,1152]{2,1,0:T(8,128)(2,1)}, u32[]{:S(2)}) copy-start(bf16[1,512,1152]{2,1,0:T(8,128)(2,1)} %copy-done.24) | copy-start | bytes 3538948
  782.7 11.8 %copy-start.27 = (bf16[1,512,1152]{2,1,0:T(8,128)(2,1)S(1)}, bf16[1,512,1152]{2,1,0:T(8,128)(2,1)}, u32[]{:S(2)}) copy-start(bf16[1,512,1152]{2,1,0:T(8,128)(2,1)} %copy-done.26) | copy-start | bytes 3538948
  782.7 25.9 %collective-permute-start.10 = (bf16[2,256,1536]{2,1,0:T(8,128)(2,1)S(1)}, bf16[2,256,1536]{2,1,0:T(8,128)(2,1)S(1)}, u32[]{:S(2)}, u32[]{:S(2)}) collective-permute-start(bf16[2,256,1536]{2,1,0:T(8,128)(2,1)S(1)} %fusion.47), channel_id=1, source_target_pairs={{0,1},{1,0},{2,3},{3,2},{4,5},{5,4},{6,7},{7,6},{8,9},{9,8},{10,11... | collective-permute-start | bytes 4718600 | tf_op jit(solution)/shard_map/ppermute | solution.py:911
  787.7 13.6 %collective-permute-start.18 = (bf16[192,1536]{1,0:T(8,128)(2,1)S(1)}, bf16[192,1536]{1,0:T(8,128)(2,1)S(1)}, u32[]{:S(2)}, u32[]{:S(2)}) collective-permute-start(bf16[192,1536]{1,0:T(8,128)(2,1)S(1)} %add_convert_fusion.4), channel_id=1, source_target_pairs={{4,12},{12,20},{20,28},{28,24},{24,16},{16,8},{8,0},{0,4},{5,13},{... | collective-permute-start | bytes 1769480 | tf_op jit(solution)/shard_map/ppermute | solution.py:845
  793.9 12.7 %collective-permute-start.22 = (bf16[192,1536]{1,0:T(8,128)(2,1)S(1)}, bf16[192,1536]{1,0:T(8,128)(2,1)S(1)}, u32[]{:S(2)}, u32[]{:S(2)}) collective-permute-start(bf16[192,1536]{1,0:T(8,128)(2,1)S(1)} %add_convert_fusion.2), channel_id=1, source_target_pairs={{4,0},{12,4},{20,12},{28,20},{24,28},{16,24},{8,16},{0,8},{5,1},{1... | collective-permute-start | bytes 1769480 | tf_op jit(solution)/shard_map/ppermute | solution.py:845
  798.2 15.2 %copy-start.29 = (f32[2,256,1536]{2,1,0:T(8,128)}, f32[2,256,1536]{2,1,0:T(8,128)S(1)}, u32[]{:S(2)}) copy-start(f32[2,256,1536]{2,1,0:T(8,128)S(1)} %convert_add_fusion.2) | copy-start | bytes 9437188
  802.3 50.2 %collective-permute-start.19 = (bf16[192,1536]{1,0:T(8,128)(2,1)}, bf16[192,1536]{1,0:T(8,128)(2,1)}, u32[]{:S(2)}, u32[]{:S(2)}) collective-permute-start(bf16[192,1536]{1,0:T(8,128)(2,1)} %add_convert_fusion.3), channel_id=1, source_target_pairs={{4,12},{12,20},{20,28},{28,24},{24,16},{16,8},{8,0},{0,4},{5,13},{... | collective-permute-start | bytes 1769480 | tf_op jit(solution)/shard_map/ppermute | solution.py:845
  807.5 44.9 %copy-start.74 = (bf16[192,384]{1,0:T(8,128)(2,1)S(1)}, bf16[192,384]{1,0:T(8,128)(2,1)}, u32[]{:S(2)}) copy-start(bf16[192,384]{1,0:T(8,128)(2,1)} %get-tuple-element.161) | copy-start | bytes 442372
  807.5 44.9 %collective-permute-start.23 = (bf16[192,1536]{1,0:T(8,128)(2,1)}, bf16[192,1536]{1,0:T(8,128)(2,1)}, u32[]{:S(2)}, u32[]{:S(2)}) collective-permute-start(bf16[192,1536]{1,0:T(8,128)(2,1)} %add_convert_fusion.1), channel_id=1, source_target_pairs={{4,0},{12,4},{20,12},{28,20},{24,28},{16,24},{8,16},{0,8},{5,1},{1... | collective-permute-start | bytes 1769480 | tf_op jit(solution)/shard_map/ppermute | solution.py:845
  813.3 44.5 %copy-start.83 = (f32[2,512]{1,0:T(2,128)S(1)}, f32[2,512]{1,0:T(2,128)}, u32[]{:S(2)}) copy-start(f32[2,512]{1,0:T(2,128)} %copy-done.81) | copy-start | bytes 12292
  813.3 44.5 %copy-start.86 = (f32[2,512]{1,0:T(2,128)S(1)}, f32[2,512]{1,0:T(2,128)}, u32[]{:S(2)}) copy-start(f32[2,512]{1,0:T(2,128)} %copy-done.84) | copy-start | bytes 12292
  852.5 16.3 %copy-start.3 = (f32[2,256,1536]{2,1,0:T(8,128)S(1)}, f32[2,256,1536]{2,1,0:T(8,128)}, u32[]{:S(2)}) copy-start(f32[2,256,1536]{2,1,0:T(8,128)} %get-tuple-element.83) | copy-start | bytes 9437188
  854.2 14.3 %collective-permute-start.24 = (bf16[192,1536]{1,0:T(8,128)(2,1)S(1)}, bf16[192,1536]{1,0:T(8,128)(2,1)S(1)}, u32[]{:S(2)}, u32[]{:S(2)}) collective-permute-start(bf16[192,1536]{1,0:T(8,128)(2,1)S(1)} %add_convert_fusion), channel_id=1, source_target_pairs={{0,2},{1,3},{2,0},{3,1},{4,6},{5,7},{6,4},{7,5},{8,10},{9,11},{10,... | collective-permute-start | bytes 1769480 | tf_op jit(solution)/shard_map/ppermute | solution.py:1111
  868.7 7.8 collective-permute-start.25
  (76 other events, 343.5 us)
Sparse Core Ops, SparseCore 0:
  68.0 78.4 all-gather.2
  149.3 78.0 all-gather.4

commit v3 on v2

--- a/solution.py
+++ b/solution.py
@@ -75,11 +75,12 @@
     mixed_ref[...] = mixed.astype(mixed_ref.dtype)
 
 
-def attend(qkv, diag, length, head_dim, block=256):
+def attend(qkv, diag, length, head_dim, by_pair=False, block=256):
     seq_len, cols = qkv.shape[0], qkv.shape[1] // 3
     pairs = cols // LANES
     per = LANES // head_dim
     span = diag.shape[-1]
+    at = (lambda part, p: 3 * p + part) if by_pair else (lambda part, p: part * pairs + p)
     flops = 2 * 2 * seq_len * seq_len * LANES * 2 * cols // head_dim
     return pl.pallas_call(
         functools.partial(attend_kernel, head_dim, block),
@@ -87,9 +88,9 @@
         in_specs=[
             pl.BlockSpec(memory_space=pltpu.SMEM),
             pl.BlockSpec((per, 1, span), lambda p, b: (p, 0, 0)),
-            pl.BlockSpec((block, LANES), lambda p, b: (b, p)),
-            pl.BlockSpec((seq_len, LANES), lambda p, b: (0, pairs + p)),
-            pl.BlockSpec((seq_len, LANES), lambda p, b: (0, 2 * pairs + p)),
+            pl.BlockSpec((block, LANES), lambda p, b: (b, at(0, p))),
+            pl.BlockSpec((seq_len, LANES), lambda p, b: (0, at(1, p))),
+            pl.BlockSpec((seq_len, LANES), lambda p, b: (0, at(2, p))),
         ],
         out_specs=[
             pl.BlockSpec((block, LANES), lambda p, b: (b, p)),
@@ -826,6 +827,334 @@
     return made[:5]
 
 
+def mix_back_kernel(plan, len_ref, lse_ref, diag_ref, *refs):
+    count, planes, rows, micro, rows_of, head_dim, block, pairs = plan
+    qkvs, grads_mixed = refs[:micro], refs[micro : 2 * micro]
+    attn_in, mixed, normed = refs[2 * micro : 2 * micro + 3]
+    dqkv, dd_ref, totals, attn_there = refs[2 * micro + 3 : 2 * micro + 7]
+    (
+        qkv_v, do_v, res, sums_v, attn_v, mixed_v, normed_v, grads, inbox,
+        strip, keys, acc_bias, acc_k, acc_v, mine, came, made, total,
+        load_sems, do_sems, res_sems, attn_sems, dqkv_sems, send_sems, recv_sems, near_sems, total_sems,
+    ) = refs[2 * micro + 7 :]
+    seq_len = do_v.shape[1]
+    span = diag_ref.shape[-1]
+    plane_len = seq_len // 2
+    local = attn_in.shape[2]
+    steps = seq_len // block
+    per = LANES // head_dim
+    wide = 3 * LANES
+    units = pairs * micro
+    links = Links(count, planes)
+    far = count // 2
+    plane, core = links.plane, links.core
+    lanes_k = lax.broadcasted_iota(jnp.int32, (seq_len, LANES), 1)
+    lanes_q = lax.broadcasted_iota(jnp.int32, (block, LANES), 1)
+
+    def at_rows(start, size):
+        return pl.ds(pl.multiple_of(start, 16), size)
+
+    def do_far(m):
+        return pltpu.make_async_remote_copy(
+            src_ref=grads_mixed[m].at[1 - plane], dst_ref=do_v.at[m, at_rows(plane * plane_len, plane_len)],
+            send_sem=do_sems.at[m, 0], recv_sem=do_sems.at[m, 1], device_id=links.across, device_id_type=MESH,
+        )
+
+    def do_near(m):
+        return pltpu.make_async_copy(
+            grads_mixed[m].at[plane], do_v.at[m, at_rows(plane * plane_len, plane_len)], do_sems.at[m, 2]
+        )
+
+    def attn_far():
+        return pltpu.make_async_remote_copy(
+            src_ref=attn_in, dst_ref=attn_there, send_sem=attn_sems.at[0], recv_sem=attn_sems.at[1],
+            device_id=links.sibling, device_id_type=MESH,
+        )
+
+    def attn_loads():
+        copies = []
+        for m in range(micro):
+            for r in range(rows_of):
+                for side in range(2):
+                    source = (attn_in, attn_there)[side]
+                    half = core if side == 0 else 1 - core
+                    start = (m * rows_of + r) * 2 * local + half * local
+                    at = (m * rows_of + r) * 2 + side
+                    copies.append(
+                        pltpu.make_async_copy(source.at[m, r], attn_v.at[at_rows(start, local)], attn_sems.at[4 + at])
+                    )
+        return copies
+
+    mixed_load = pltpu.make_async_copy(mixed, mixed_v, attn_sems.at[2])
+    normed_load = pltpu.make_async_copy(normed, normed_v, attn_sems.at[3])
+
+    def unit_loads(m, p, slot):
+        return [
+            pltpu.make_async_copy(
+                qkvs[m].at[:, pl.ds(pl.multiple_of((3 * p + part) * LANES, LANES), LANES)],
+                qkv_v.at[slot, part],
+                load_sems.at[slot, part],
+            )
+            for part in range(3)
+        ]
+
+    def start_unit(u):
+        p, slot = u // micro, lax.rem(u, 2)
+        for m in range(micro):
+
+            @pl.when(lax.rem(u, micro) == m)
+            def _(m=m):
+                for copy in unit_loads(m, p, slot):
+                    copy.start()
+
+    def res_far(u):
+        p, m = u // micro, lax.rem(u, micro)
+        return pltpu.make_async_remote_copy(
+            src_ref=res.at[lax.rem(u, 2), at_rows((1 - plane) * plane_len, plane_len)],
+            dst_ref=sums_v.at[p, m * rows_of + plane],
+            send_sem=res_sems.at[0, lax.rem(u, 2)], recv_sem=res_sems.at[1, u],
+            device_id=links.across, device_id_type=MESH,
+        )
+
+    def dqkv_copy(p, at):
+        return pltpu.make_async_copy(
+            sums_v.at[p, at], dqkv.at[at, :, pl.ds(p * wide, wide)], dqkv_sems.at[p, at]
+        )
+
+    start_unit(jnp.int32(0))
+    mixed_load.start()
+    normed_load.start()
+    for m in range(micro):
+        do_near(m).start()
+    links.greet()
+    for m in range(micro):
+        do_far(m).start()
+    attn_far().start()
+    scatter = Scatter(
+        links, grads, inbox, totals, mine, came, made, total, send_sems, recv_sems, near_sems, total_sems, rows
+    )
+
+    def weight_grads(group, left, right):
+        for at in range(left.shape[1] // 384):
+            place = slice(at * 384, (at + 1) * 384)
+            made_now = dot32(left[:, place], right, TN)
+            grads[group, place] = made_now.astype(grads.dtype)
+        scatter.start(jnp.int32(group))
+
+    def grads_out():
+        for copy in attn_loads():
+            copy.wait()
+        mixed_load.wait()
+        weight_grads(0, attn_v, mixed_v[...])
+
+    def grads_pair(p):
+        if p == 0:
+            normed_load.wait()
+        for m in range(micro):
+            res_far(jnp.int32(p * micro + m)).wait_recv()
+        for at in range(micro * rows_of):
+            dqkv_copy(p, at).start()
+        right = sums_v[p].reshape(micro * rows_of * plane_len, wide)
+        weight_grads(1 + p, normed_v, right)
+
+    per_pair = micro * steps
+    work = pairs * per_pair
+    begins = [4] + [per_pair * (p + 1) + 3 for p in range(pairs - 1)] + [work + 2]
+    gap = max(1, 8 // far)
+    last = begins[-1] + 2 * far * gap
+
+    def item(i, carry):
+        u, b = i // steps, lax.rem(i, steps)
+        p, m = u // micro, lax.rem(u, micro)
+        slot = lax.rem(u, 2)
+
+        @pl.when(i == 3)
+        def _():
+            attn_far().wait_recv()
+            for copy in attn_loads():
+                copy.start()
+
+        for group, begin in enumerate(begins):
+            g = jnp.int32(group)
+
+            @pl.when(i == begin)
+            def _(group=group):
+                grads_out() if group == 0 else grads_pair(group - 1)
+
+            for step in range(1, far + 1):
+
+                @pl.when(i == begin + (2 * step - 1) * gap)
+                def _(g=g, step=step):
+                    scatter.fetch(g, step)
+
+                @pl.when(i == begin + 2 * step * gap)
+                def _(g=g, step=step):
+                    if step < far:
+                        scatter.pass_on(g, step)
+                    else:
+                        scatter.close(g)
+
+        @pl.when((i < work) & (b == 0))
+        def _():
+            for copy in unit_loads(0, p, slot):
+                copy.wait()
+
+            @pl.when(u + 1 < units)
+            def _():
+                start_unit(u + 1)
+
+            for k in range(micro):
+
+                @pl.when(u == k)
+                def _(k=k):
+                    do_near(k).wait()
+                    do_far(k).wait_recv()
+
+            @pl.when(u >= 2)
+            def _():
+                res_far(u - 2).wait_send()
+
+            @pl.when(m == 0)
+            def _():
+                for head in range(per):
+                    strip[head] = toeplitz_strip(diag_ref[p * per + head], span).T
+                acc_bias[...] = jnp.zeros_like(acc_bias)
+
+            length = len_ref[m]
+            for head in range(per):
+                here = lanes_k // head_dim == head
+                spare = ((head + 1) % per) * head_dim
+                keys[head] = with_mask_lane(qkv_v[slot, 1], lanes_k, here, spare, length)
+            acc_k[...] = jnp.zeros_like(acc_k)
+            acc_v[...] = jnp.zeros_like(acc_v)
+
+        @pl.when(i < work)
+        def _():
+            place = at_rows(b * block, block)
+            q_now = qkv_v[slot, 0, place]
+            do_now = do_v[m, place, pl.ds(pl.multiple_of(p * LANES, LANES), LANES)]
+            grad_query = None
+            for head in range(per):
+                here = lanes_q // head_dim == head
+                spare = ((head + 1) % per) * head_dim
+                zero = jnp.zeros_like(q_now)
+                one = (lanes_q == spare).astype(q_now.dtype)
+                query = jnp.where(here, q_now, zero)
+                grad = jnp.where(here, do_now, zero)
+                raw = dot32(keys[head], query + one, NT)
+                grad_probs = dot32(qkv_v[slot, 2], grad, NT)
+                parts, offsets = [], []
+                for sub in range(block // LANES):
+                    offset = pl.multiple_of(seq_len - LANES - (b * block + sub * LANES), LANES)
+                    offsets.append(offset)
+                    parts.append(raw[:, sub * LANES : (sub + 1) * LANES] + strip[head, pl.ds(offset, seq_len), :])
+                scores = jnp.concatenate(parts, axis=1)
+                lse = lse_ref[m * pairs * per + p * per + head, :, pl.ds(pl.multiple_of(b * block, LANES), block)]
+                probs = jnp.exp(scores - lse)
+                product = probs * grad_probs
+                inner = jnp.sum(product, axis=0, keepdims=True)
+                grad_scores = product - probs * inner
+                for sub, offset in enumerate(offsets):
+                    acc_bias[head, pl.ds(offset, seq_len), :] += grad_scores[:, sub * LANES : (sub + 1) * LANES]
+                rounded = grad_scores.astype(jnp.bfloat16)
+                acc_v[...] += dot32(probs.astype(jnp.bfloat16), grad, NN)
+                acc_k[...] += dot32(rounded, query, NN)
+                made_now = dot32(rounded, qkv_v[slot, 1], TN)
+                grad_query = made_now if grad_query is None else jnp.where(here, made_now, grad_query)
+            res[slot, place, :LANES] = grad_query.astype(res.dtype)
+
+        @pl.when((i < work) & (b == steps - 1))
+        def _():
+            res[slot, :, LANES : 2 * LANES] = acc_k[...].astype(res.dtype)
+            res[slot, :, 2 * LANES :] = acc_v[...].astype(res.dtype)
+            res_far(u).start()
+            sums_v[p, m * rows_of + plane] = res[slot, at_rows(plane * plane_len, plane_len)]
+
+            @pl.when(m == micro - 1)
+            def _():
+                row = lax.broadcasted_iota(jnp.int32, (LANES, LANES), 0)
+                col = lax.broadcasted_iota(jnp.int32, (LANES, LANES), 1)
+                flip = (row + col == LANES - 1).astype(jnp.float32)
+                for head in range(per):
+                    turned = lax.dot_general(
+                        flip, acc_bias[head], NT, precision=highest, preferred_element_type=jnp.float32
+                    )
+                    aligned = pltpu.roll(turned, 0, 1, stride=1, stride_axis=0)
+                    dd_ref[p * per + head] = jnp.sum(aligned, axis=0, keepdims=True)
+
+        return carry
+
+    lax.fori_loop(0, last + 1, item, 0)
+    scatter.total_copy(jnp.int32(pairs)).wait()
+    for m in range(micro):
+        do_far(m).wait_send()
+    attn_far().wait_send()
+    for u in range(max(0, units - 2), units):
+        res_far(jnp.int32(u)).wait_send()
+    for p in range(pairs):
+        for at in range(micro * rows_of):
+            dqkv_copy(p, at).wait()
+
+
+def mix_back(qkvs, grads_mixed, attn_in, mixed, normed, lse, diag, lengths, head_dim, count, planes, block=256):
+    micro, rows_of, local, depth = attn_in.shape
+    seq_len, cols = qkvs[0].shape[0], qkvs[0].shape[1] // 3
+    pairs, per, span = cols // LANES, LANES // head_dim, diag.shape[-1]
+    tokens = normed.shape[0]
+    rows, wide, far = depth // count, 3 * LANES, count // 2
+    groups = 1 + pairs
+    plan = (count, planes, rows, micro, rows_of, head_dim, block, pairs)
+    anywhere = pl.BlockSpec(memory_space=pl.ANY)
+    low, f32 = jnp.bfloat16, jnp.float32
+    dma = pltpu.SemaphoreType.DMA
+    return pl.pallas_call(
+        functools.partial(mix_back_kernel, plan),
+        in_specs=[pl.BlockSpec(memory_space=pltpu.SMEM)]
+        + [pl.BlockSpec(memory_space=pltpu.VMEM)] * 2
+        + [anywhere] * (2 * micro + 3),
+        out_specs=[anywhere, pl.BlockSpec(memory_space=pltpu.VMEM), anywhere, anywhere],
+        out_shape=[
+            jax.ShapeDtypeStruct((micro * rows_of, 2 * local, 3 * cols), low),
+            jax.ShapeDtypeStruct(diag.shape, f32),
+            jax.ShapeDtypeStruct((groups, rows, wide), f32),
+            jax.ShapeDtypeStruct(attn_in.shape, low),
+        ],
+        scratch_shapes=[
+            pltpu.VMEM((2, 3, seq_len, LANES), low),
+            pltpu.VMEM((micro, seq_len, cols), low),
+            pltpu.VMEM((2, seq_len, wide), low),
+            pltpu.VMEM((pairs, micro * rows_of, seq_len // 2, wide), low),
+            pltpu.VMEM((tokens, depth), low),
+            pltpu.VMEM((tokens, cols), low),
+            pltpu.VMEM((tokens, depth), low),
+            pltpu.VMEM((groups, depth, wide), low),
+            pltpu.VMEM((groups, 2, far, rows, wide), low),
+            pltpu.VMEM((per, span, LANES), f32),
+            pltpu.VMEM((per, seq_len, LANES), low),
+            pltpu.VMEM((per, span, LANES), f32),
+            pltpu.VMEM((seq_len, LANES), f32),
+            pltpu.VMEM((seq_len, LANES), f32),
+            pltpu.VMEM((2, 2, rows, wide), low),
+            pltpu.VMEM((2, 2, rows, wide), low),
+            pltpu.VMEM((2, 2, rows, wide), low),
+            pltpu.VMEM((rows, wide), f32),
+            dma((2, 3)),
+            dma((micro, 3)),
+            dma((2, pairs * micro)),
+            dma((4 + 2 * micro * rows_of,)),
+            dma((pairs, micro * rows_of)),
+            dma((groups, 2, far)),
+            dma((groups, 2, far)),
+            dma((2, 2, 2)),
+            dma((1,)),
+        ],
+        compiler_params=pltpu.CompilerParams(
+            collective_id=2, has_side_effects=True, vmem_limit_bytes=62 * 1024 * 1024
+        ),
+        name="mix_back",
+    )(lengths, lse, diag, *qkvs, *grads_mixed, attn_in, mixed, normed)
+
+
 class Ring:
     def __init__(self, count):
         order = ring_order(count)
@@ -929,9 +1258,11 @@
     split = chunks * chunk
     if split > hidden_units:
         split = hidden_units
-    attn_shard = jnp.concatenate(
-        [core_columns(w, half_inner) for w in (w_query, w_key, w_value, w_out.T)], axis=1
-    )
+    fused = planes == 2 and rows == 2 and half_inner % LANES == 0
+    attn_parts = [core_columns(w, half_inner) for w in (w_query, w_key, w_value)]
+    if fused:
+        attn_parts = [w[:, p : p + LANES] for p in range(0, half_inner, LANES) for w in attn_parts]
+    attn_shard = jnp.concatenate(attn_parts + [core_columns(w_out.T, half_inner)], axis=1)
     up_parts = [core_columns(w, split) for w in (w_gate, w_up, w_down.T)]
     chunk_shards = [
         jnp.concatenate([w[:, n * chunk : (n + 1) * chunk] for w in up_parts], axis=1) for n in range(chunks)
@@ -1019,7 +1350,7 @@
     for step in range(micro):
         item_len = lax.dynamic_slice_in_dim(lengths[step], item_row, 1, 0)
         item_lens.append(item_len)
-        mixed, lse = attend(qkvs[step], diag, item_len, head_dim)
+        mixed, lse = attend(qkvs[step], diag, item_len, head_dim, fused)
         lses.append(lse)
         mixed_own = from_items([mixed])
         mixes.append(mixed_own)
@@ -1030,6 +1361,24 @@
         root = lax.rsqrt(jnp.mean(resid * resid, axis=-1, keepdims=True) + eps)
         normed_twos.append((resid * root * gain_second).astype(jnp.bfloat16))
         resids.append(own_half(resid, 1))
+
+    def apart(qkvs, grads_items, lses, item_lens, attn_all, mixed_all, normed_all):
+        grads_qkv, diag_sum = [], 0.0
+        for step in range(micro):
+            grad_q, grad_k, grad_v, grad_diag = attend_back(
+                qkvs[step], grads_items[step], lses[step], diag, item_lens[step], head_dim
+            )
+            diag_sum = diag_sum + grad_diag[:item_heads, 0]
+            grads_qkv.append(from_items([grad_q, grad_k, grad_v]))
+        grads_all = jnp.concatenate([flat(v) for v in grads_qkv])
+        attn_all = flat(both_cores(attn_all, swap_core(attn_all), 2))
+        grad_attn = jnp.einsum("td,te->de", normed_all, grads_all, preferred_element_type=jnp.float32)
+        grad_o = jnp.einsum("td,te->de", attn_all, mixed_all, preferred_element_type=jnp.float32)
+        both = jnp.concatenate([grad_o, grad_attn], axis=1).astype(jnp.bfloat16)
+        total = ring.scatter(
+            lambda index: lax.dynamic_slice_in_dim(both, index * shard_rows, shard_rows, 0), 4 * half_inner
+        )
+        return grads_qkv, diag_sum, total
 
     flat = lambda value: value.reshape(-1, value.shape[-1])
     normed_two_all = jnp.concatenate([flat(v) for v in normed_twos])
@@ -1064,15 +1413,20 @@
     for step in range(micro):
         outputs.append((resids[step] + out_kept[step] + out_got[step]).astype(jnp.bfloat16))
 
-    grads_qkv = []
-    diag_sum = 0.0
-    for step in range(micro):
-        grad_items = to_items(grads_mixed[step], 1)
-        grad_q, grad_k, grad_v, grad_diag = attend_back(
-            qkvs[step], grad_items, lses[step], diag, item_lens[step], head_dim
-        )
-        diag_sum = diag_sum + grad_diag[:item_heads, 0]
-        grads_qkv.append(from_items([grad_q, grad_k, grad_v]))
+    normed_all = jnp.concatenate([flat(v) for v in normed])
+    mixed_all = jnp.concatenate([flat(v) for v in mixes])
+    attn_all = jnp.stack(attn_ins)
+    if fused:
+        grads_all, diag_sum, attn_totals, _ = mix_back(
+            qkvs, grads_mixed, attn_all, mixed_all, normed_all, jnp.concatenate(lses), diag,
+            jnp.concatenate(item_lens), head_dim, dp_devices, planes,
+        )
+        grads_qkv = grads_all.reshape(micro, rows, pair_local, 3 * half_inner)
+        diag_sum = diag_sum[:, 0]
+    else:
+        grads_qkv, diag_sum, attn_totals = apart(
+            qkvs, [to_items(g, 1) for g in grads_mixed], lses, item_lens, attn_all, mixed_all, normed_all
+        )
     item_grad = jnp.dot(diag_sum, bucket_hot, precision=highest)
     grad_table = lax.dynamic_update_slice(jnp.zeros((heads, levels), jnp.float32), item_grad, (head_start, 0))
 
@@ -1090,21 +1444,6 @@
         shared = jnp.mean(scaled * rows_in, axis=-1, keepdims=True) * root * root * root
         input_grads.append(grad_resids[step] + scaled * root - rows_in * shared)
 
-    normed_all = jnp.concatenate([flat(v) for v in normed])
-    grads_all = jnp.concatenate([flat(v) for v in grads_qkv])
-    mixed_all = jnp.concatenate([flat(v) for v in mixes])
-    attn_all = jnp.stack(attn_ins)
-    attn_all = flat(both_cores(attn_all, swap_core(attn_all), 2))
-    grad_attn = jnp.einsum("td,te->de", normed_all, grads_all, preferred_element_type=jnp.float32).astype(jnp.bfloat16)
-    grad_o = jnp.einsum("td,te->de", attn_all, mixed_all, preferred_element_type=jnp.float32).astype(jnp.bfloat16)
-
-    def attn_term(index):
-        return jnp.concatenate(
-            [lax.dynamic_slice_in_dim(g, index * shard_rows, shard_rows, 0) for g in (grad_attn, grad_o)], axis=1
-        )
-
-    attn_total = ring.scatter(attn_term, 4 * half_inner)
-
     def finish(total):
         if planes == 2:
             low = total.astype(jnp.bfloat16)
@@ -1118,9 +1457,20 @@
         low, high = jnp.where(first, own, other), jnp.where(first, other, own)
         return jnp.concatenate([low, high[:, : size - low.shape[1]]], axis=1)
 
-    own, other = finish(attn_total)
-    parts = [slice(i * half_inner, (i + 1) * half_inner) for i in range(4)]
-    grad_query, grad_key, grad_value, grad_out = [whole_columns(own[:, p], other[:, p], inner) for p in parts]
+    own, other = finish(attn_totals)
+    if fused:
+        grad_out = whole_columns(own[0], other[0], inner)
+        grad_query, grad_key, grad_value = [
+            whole_columns(
+                jnp.concatenate(list(own[1:, :, part * LANES : (part + 1) * LANES]), axis=1),
+                jnp.concatenate(list(other[1:, :, part * LANES : (part + 1) * LANES]), axis=1),
+                inner,
+            )
+            for part in range(3)
+        ]
+    else:
+        parts = [slice(i * half_inner, (i + 1) * half_inner) for i in range(4)]
+        grad_out, grad_query, grad_key, grad_value = [whole_columns(own[:, p], other[:, p], inner) for p in parts]
     done = [finish(chunk_totals[n]) for n in range(chunks)]
     parts = [slice(i * chunk, (i + 1) * chunk) for i in range(3)]
     grad_gate, grad_up, grad_down = [

time: 899 us -> 807 us (0.90)
  waiting for transfers between devices: 102 us -> 38.7 us
  Pallas kernels: 437 us -> 493 us
  local copies, waits for them, and re-layouts: 71.4 us -> 45 us
  starting transfers between devices: 26.5 us -> 11.9 us
  matrix products: 63.1 us -> 48.8 us
  between operations: 27.6 us -> 15.6 us
  other arithmetic: 121 us -> 109 us
    pallas_call x2 -> x1, Pallas kernels: 83.3 us -> 139 us  [mix_back(): pl.pallas_call(functools.partial(mix_back_kernel, plan), in_specs=[pl.Blo...]
    ppermute x4 -> x2, waiting for transfers between devices: 40.7 us -> 6.91 us  [from_items(): got = lax.ppermute(sent, 'seq', [(i, i ^ 2) for i in range(4)])]
    ppermute x5, waiting for transfers between devices: 24.3 us -> 0.01 us  [finish(): got = lax.ppermute(low, 'seq', [(i, i ^ 2) for i in range(4)])]
    ppermute x8 -> x0, waiting for transfers between devices: 19.9 us -> none  [send(): return lax.ppermute(block, 'dp', self.ahead if forward else self.behind)]
    dot_general x2 -> x0, matrix products: 18.1 us -> none  [the longest x1 11.3 us: body(): jnp.einsum('td,te->de', normed_all, grads_all, preferred_element_type=jnp...]
    unnamed x211 -> x172, local copies, waits for them, and re-layouts: 26.6 us -> 12.7 us
    all_gather x2, waiting for transfers between devices: 16.6 us -> 29.3 us  [body(): ready.append(lax.all_gather(shard, 'dp', axis=0, tiled=True))]
    ppermute x8 -> x0, starting transfers between devices: 9.64 us -> none  [send(): return lax.ppermute(block, 'dp', self.ahead if forward else self.behind)]
  transfers between devices with their start and end apart: 36 -> 23, of which waited for: 11 -> 5; matrix products, arithmetic and copies ran while one was open for 24% -> 21% of each run, Pallas kernels for 14% -> 23%
where the time goes in v3:
time: 807 us; the launch traced here: 803 us
  Pallas kernels  493 us (61%)
  other arithmetic  109 us (14%)
  matrix products  48.8 us (6%)
  local copies, waits for them, and re-layouts  45 us (6%)
  blocking collectives  41.3 us (5%)
  waiting for transfers between devices  38.7 us (5%)
  between operations  15.6 us (2%)
  starting transfers between devices  11.9 us (1%)
    pallas_call x1, Pallas kernels, feed(): pl.pallas_call(functools.partial(feed_kernel, plan), in_specs=[anywhere]...  265 us
    pallas_call x1, Pallas kernels, mix_back(): pl.pallas_call(functools.partial(mix_back_kernel, plan), in_specs=[pl.Blo...  139 us
    pallas_call x1, Pallas kernels, gather_first(): pl.pallas_call(functools.partial(gather_kernel, count, planes, rows), in_...  46.9 us
    pallas_call x2, Pallas kernels, attend(): pl.pallas_call(functools.partial(attend_kernel, head_dim, block), grid=(p...  41.8 us
    psum x1, blocking collectives, body(): lax.psum(jnp.concatenate([gain_one_sum, gain_two_sum, grad_table.T.reshap...  41.3 us
    all_gather x2, waiting for transfers between devices, body(): ready.append(lax.all_gather(shard, 'dp', axis=0, tiled=True))  29.3 us
    another operation x2, other arithmetic, body(): jnp.stack(outputs)  16.8 us
  transfers between devices with their start and end apart: 23, of which 5 were waited for; matrix products, arithmetic and copies ran while one was open for 21% of the time, Pallas kernels for 23%

profile of v3, /device:TPU:0, one launch (start us, length us, event | category | flops | bytes accessed | tf_op | source)
XLA Modules:
  0.0 802.9 jit_solution(16166935525581392990)
XLA Ops:
  12.1 1.3 slice.442
  18.8 46.9 %gather_first.1 = (bf16[1536,1536]{1,0:T(8,128)(2,1)}, bf16[128,512]{1,0:T(8,128)(2,1)}, bf16[2,2,256,1536]{3,2,1,0:T(8,128)(2,1)}, bf16[2,2,256,1536]{3,2,1,0:T(8,128)(2,1)}) custom-call(bf16[192,1536]{1,0:T(8,128)(2,1)} %copy-done.46, bf16[16,512]{1,0:T(8,128)(2,1)} %pad.26.small, bf16[2,2,256,1536]{3,2,1,0:T(8,128)(2,1)} %tokens.1, ...), custom_call_target="tpu_custom_call" | custom-call | tf_op jit(solution)/shard_map/gather_first/pallas_call | solution.py:436
  68.1 2.4 broadcast_select_fusion.3
  70.6 1.7 fusion.7
  73.0 4.6 convolution_convert_fusion
  81.1 4.6 convolution_convert_fusion.1
  85.7 1.4 copy-done.28
  88.3 1.5 collective-permute-start
  94.8 5.0 broadcast_select_fusion.1
  100.5 4.0 fusion.3
  106.8 3.1 pad_maximum_fusion.1
  109.9 3.0 pad_maximum_fusion.2.refs_6_
  112.9 1.5 bitcast_select_fusion.1
  114.4 1.6 pad_maximum_fusion.10.q_ref.k_ref.v_ref.refs_1_
  116.0 20.8 %attend.3 = (bf16[1024,384]{1,0:T(8,128)(2,1)}, f32[6,1,1024]{2,1,0:T(1,128)}) custom-call(s32[1]{0:T(128)} %bitcast.13.len_ref, f32[6,1,2048]{2,1,0:T(1,128)} %broadcast_in_dim.7.diag_ref, bf16[1024,1152]{1,0:T(8,128)(2,1)} %pad_maximum_fusion.10.q_ref.k_ref.v_ref.refs_1_, bf16[1024,1152]{1,0:T(8,128)(2,1)} %pad_maximum_fusion.10.q_ref.k_ref.v_ref.refs_1_, ...), custom_call_target="tpu_custom_call" | custom-call | flops 6442450944 | bytes 3145728 | tf_op jit(solution)/shard_map/attend/pallas_call | solution.py:85
  138.9 1.5 bitcast_select_fusion.3
  140.4 1.6 pad_maximum_fusion.9.q_ref.k_ref.v_ref.refs_0_
  142.0 20.9 %attend.2 = (bf16[1024,384]{1,0:T(8,128)(2,1)}, f32[6,1,1024]{2,1,0:T(1,128)}) custom-call(s32[1]{0:T(128)} %bitcast.2.len_ref, f32[6,1,2048]{2,1,0:T(1,128)} %broadcast_in_dim.7.diag_ref, bf16[1024,1152]{1,0:T(8,128)(2,1)} %pad_maximum_fusion.9.q_ref.k_ref.v_ref.refs_0_, bf16[1024,1152]{1,0:T(8,128)(2,1)} %pad_maximum_fusion.9.q_ref.k_ref.v_ref.refs_0_, ...), custom_call_target="tpu_custom_call" | custom-call | flops 6442450944 | bytes 3145728 | tf_op jit(solution)/shard_map/attend/pallas_call | solution.py:85
  165.6 1.9 pad_add_fusion.len_ref
  168.2 6.9 collective-permute-done.1
  175.5 1.4 pad_maximum_fusion.11.refs_5_
  176.9 4.7 multiply_reduce_fusion
  181.9 3.9 copy-done.12
  185.8 4.5 multiply_reduce_fusion.1
  192.9 3.1 pad_maximum_fusion.refs_0_
  196.0 29.3 %all-gather.5.cloned.1.call-done.refs_3_ = bf16[1536,1536]{1,0:T(8,128)(2,1)} async-done(((bf16[192,1536]{1,0:T(8,128)(2,1)}), bf16[1536,1536]{1,0:T(8,128)(2,1)}) %all-gather.5.cloned.1.call-update) | async-done | bytes 4718608 | tf_op jit(solution)/shard_map/all_gather | solution.py:1291
  225.3 265.1 %feed.1 = (bf16[4,256,1536]{2,1,0:T(8,128)(2,1)}, bf16[4,256,1536]{2,1,0:T(8,128)(2,1)}, bf16[4,256,1536]{2,1,0:T(8,128)(2,1)}, bf16[4,256,1536]{2,1,0:T(8,128)(...) custom-call(bf16[2048,1536]{1,0:T(8,128)(2,1)} %pad_maximum_fusion.r, ...), custom_call_target="tpu_custom_call" | custom-call | flops 115964116992 | bytes 31457280 | tf_op jit(solution)/shard_map/feed/pallas_call | solution.py:789
  490.4 2.6 convert.16
  493.0 1.4 slice_bitcast_fusion.3
  494.5 1.9 collective-permute-start.13
  496.5 1.9 collective-permute-start.15
  502.5 3.9 convert_element_type.200
  506.3 2.3 copy-done.22
  508.7 3.8 convert_element_type.201
  513.1 2.2 multiply_reduce_fusion.3
  515.3 14.8 %fusion.47 = (bf16[1,2,256,1536]{3,2,1,0:T(8,128)(2,1)S(1)}, bf16[1,2,256,1536]{3,2,1,0:T(8,128)(2,1)}, bf16[1,2,256,1536]{3,2,1,0:T(8,128)(2,1)}, f32[2,256,153...) fusion(f32[4,256,1536]{2,1,0:T(8,128)} %convert_element_type.201, ...), kind=kLoop, calls=%fused_computation.96 | loop fusion | flops 17301504 | bytes 47200260 | tf_op jit(solution)/shard_map/stack | solution.py:1495
  530.1 3.3 convolution_convert_fusion.3
  533.5 2.4 convolution_convert_fusion.2
  536.0 2.4 convolution_convert_fusion.5
  538.4 1.9 pad_maximum_fusion.6.refs_4_
  540.4 1.9 pad_maximum_fusion.5
  542.9 2.2 convolution_convert_fusion.4
  548.1 139.1 %mix_back.1 = (bf16[4,512,1152]{2,1,0:T(8,128)(2,1)}, f32[6,1,2048]{2,1,0:T(1,128)}, f32[4,192,384]{2,1,0:T(8,128)}, bf16[2,2,256,1536]{3,2,1,0:T(8,128)(2,1)}) custom-call(s32[2]{0:T(128)} %pad_add_fusion.len_ref, f32[12,1,1024]{2,1,0:T(1,128)} %pad_maximum_fusion.35.lse_ref, f32[6,1,2048]{2,1,0:T(1,128)} %broadcast_in_dim.7.diag_ref, ...), custom_call_target="tpu_custom_call" | custom-call | tf_op jit(solution)/shard_map/mix_back/pallas_call | solution.py:1110
  687.2 1.3 convert_element_type.230
  689.6 2.7 fusion.118
  692.3 6.3 fusion.41
  698.6 1.6 fusion.79
  701.7 4.4 fusion.44
  706.2 2.3 convert_add_fusion.7
  711.6 2.0 slice_bitcast_fusion.9
  715.0 1.6 collective-permute-done.20
  719.2 1.8 maximum_bitcast_fusion
  721.1 1.8 pad_maximum_fusion.8
  722.9 1.8 pad_maximum_fusion.7
  724.8 2.2 convert_add_fusion.2
  727.4 5.3 fusion.24
  733.3 41.3 %psum.7 = f32[3456]{0:T(1024)} all-reduce(f32[3456]{0:T(1024)} %pad_maximum_fusion.36), channel_id=1, replica_groups=mesh['dp'=8,'seq'=4] {'dp','seq'}, use_global_device_ids=true, to_apply=%region_14.15 | all-reduce | flops 3456 | bytes 27648 | tf_op jit(solution)/shard_map/psum | solution.py:1486
  774.5 1.3 slice.461
  775.8 1.4 reshape.275
  778.5 1.3 constant_dynamic-slice_fusion
  779.7 1.4 fusion.130
  781.1 5.4 fusion.22
  786.6 3.1 pad_maximum_fusion.3
  791.7 1.3 slice_bitcast_fusion.6
  (307 shorter events, 59.2 us)
Async XLA Ops:
  7.2 6.3 copy-start.36
  7.2 188.8 %all-gather.3.cloned.1.call-start = ((), (), s32[]{:S(2)}) async-start(), calls=%async_computation | async-start | bytes 5308416 | tf_op jit(solution)/shard_map/all_gather | solution.py:1291
  18.8 49.3 %copy-start.7 = (bf16[2,2,256,1536]{3,2,1,0:T(8,128)(2,1)S(1)}, bf16[2,2,256,1536]{3,2,1,0:T(8,128)(2,1)}, u32[]{:S(2)}) copy-start(bf16[2,2,256,1536]{3,2,1,0:T(8,128)(2,1)} %tokens.1) | copy-start | bytes 9437188
  65.8 159.5 %all-gather.5.cloned.1.call-start = ((), (), s32[]{:S(2)}) async-start(), calls=%async_computation.1 | async-start | bytes 5308416 | tf_op jit(solution)/shard_map/all_gather | solution.py:1291
  68.1 32.3 %copy-start.54 = (f32[1536]{0:T(1024)}, f32[1536]{0:T(1024)S(1)}, u32[]{:S(2)}) copy-start(f32[1536]{0:T(1024)S(1)} %mul.342) | copy-start | bytes 18436
  72.3 5.3 copy-start.13
  72.3 8.8 %copy-start.11 = (bf16[1,2,512,1536]{3,2,1,0:T(8,128)(2,1)}, bf16[1,2,512,1536]{3,2,1,0:T(8,128)(2,1)S(1)}, u32[]{:S(2)}) copy-start(bf16[1,2,512,1536]{3,2,1,0:T(8,128)(2,1)S(1)} %get-tuple-element.63) | copy-start | bytes 9437188
  77.6 8.1 %copy-start.30 = (bf16[2,512,1152]{2,1,0:T(8,128)(2,1)}, bf16[2,512,1152]{2,1,0:T(8,128)(2,1)S(1)}, u32[]{:S(2)}) copy-start(bf16[2,512,1152]{2,1,0:T(8,128)(2,1)S(1)} %convolution_convert_fusion) | copy-start | bytes 7077892
  78.9 34.0 %collective-permute-start.4 = (bf16[512,1152]{1,0:T(8,128)(2,1)}, bf16[512,1152]{1,0:T(8,128)(2,1)}, u32[]{:S(2)}, u32[]{:S(2)}) collective-permute-start(bf16[512,1152]{1,0:T(8,128)(2,1)} %dynamic-slice_bitcast_fusion), channel_id=1, source_target_pairs={{0,2},{1,3},{2,0},{3,1},{4,6},{5,7},{6,4},{7,5},{8,10},{9,11},{10,... | collective-permute-start | bytes 3538952 | tf_op jit(solution)/shard_map/ppermute | solution.py:1316
  80.5 96.3 %collective-permute-start.3 = (bf16[1536,384]{1,0:T(8,128)(2,1)}, bf16[1536,384]{1,0:T(8,128)(2,1)}, u32[]{:S(2)}, u32[]{:S(2)}) collective-permute-start(bf16[1536,384]{1,0:T(8,128)(2,1)} %slice.352), channel_id=1, source_target_pairs={{0,1},{1,0},{2,3},{3,2},{4,5},{5,4},{6,7},{7,6},{8,9},{9,8},{10,11... | collective-permute-start | bytes 3538952 | tf_op jit(solution)/shard_map/ppermute | solution.py:1240
  81.1 8.6 %copy-start.43 = (bf16[192,512]{1,0:T(8,128)(2,1)S(1)}, bf16[192,512]{1,0:T(8,128)(2,1)}, u32[]{:S(2)}) copy-start(bf16[192,512]{1,0:T(8,128)(2,1)} %get-tuple-element.163) | copy-start | bytes 589828
  87.1 7.6 copy-start.6
  88.3 50.7 %collective-permute-start = (bf16[512,1152]{1,0:T(8,128)(2,1)}, bf16[512,1152]{1,0:T(8,128)(2,1)}, u32[]{:S(2)}, u32[]{:S(2)}) collective-permute-start(bf16[512,1152]{1,0:T(8,128)(2,1)} %dynamic-slice_bitcast_fusion.1), channel_id=1, source_target_pairs={{0,2},{1,3},{2,0},{3,1},{4,6},{5,7},{6,4},{7,5},{8,10},{9,11},{10,... | collective-permute-start | bytes 3538952 | tf_op jit(solution)/shard_map/ppermute | solution.py:1316
  91.8 8.0 copy-start.32
  94.8 5.0 copy-start.67
  94.8 5.0 copy-start.66
  94.8 5.1 copy-start.61
  100.4 4.9 copy-start.37
  100.5 4.9 copy-start.39
  100.5 4.9 copy-start.41
  100.5 5.7 copy-start.64
  100.5 6.3 copy-start.15
  100.5 6.3 copy-start.16
  116.0 22.9 %copy-start.29 = (bf16[2,512,1152]{2,1,0:T(8,128)(2,1)S(1)}, bf16[2,512,1152]{2,1,0:T(8,128)(2,1)}, u32[]{:S(2)}) copy-start(bf16[2,512,1152]{2,1,0:T(8,128)(2,1)} %copy-done.28) | copy-start | bytes 7077892
  137.9 27.4 %collective-permute-start.5 = (bf16[512,384]{1,0:T(8,128)(2,1)S(1)}, bf16[512,384]{1,0:T(8,128)(2,1)S(1)}, u32[]{:S(2)}, u32[]{:S(2)}) collective-permute-start(bf16[512,384]{1,0:T(8,128)(2,1)S(1)} %constant_dynamic-slice_fusion.3), channel_id=1, source_target_pairs={{0,2},{1,3},{2,0},{3,1},{4,6},{5,7},{6,4},{7,5},{8,10},{9,11},{10,... | collective-permute-start | bytes 1179656 | tf_op jit(solution)/shard_map/ppermute | solution.py:1332
  142.0 23.2 %copy-start.45 = (bf16[1024,384]{1,0:T(8,128)(2,1)S(1)}, bf16[1024,384]{1,0:T(8,128)(2,1)}, u32[]{:S(2)}) copy-start(bf16[1024,384]{1,0:T(8,128)(2,1)} %get-tuple-element.33) | copy-start | bytes 2359300
  163.0 12.2 %copy-start.44 = (bf16[1024,384]{1,0:T(8,128)(2,1)S(1)}, bf16[1024,384]{1,0:T(8,128)(2,1)}, u32[]{:S(2)}) copy-start(bf16[1024,384]{1,0:T(8,128)(2,1)} %get-tuple-element.32) | copy-start | bytes 2359300
  164.1 11.0 %collective-permute-start.1 = (bf16[512,384]{1,0:T(8,128)(2,1)S(1)}, bf16[512,384]{1,0:T(8,128)(2,1)S(1)}, u32[]{:S(2)}, u32[]{:S(2)}) collective-permute-start(bf16[512,384]{1,0:T(8,128)(2,1)S(1)} %constant_dynamic-slice_fusion.5), channel_id=1, source_target_pairs={{0,2},{1,3},{2,0},{3,1},{4,6},{5,7},{6,4},{7,5},{8,10},{9,11},{10,... | collective-permute-start | bytes 1179656 | tf_op jit(solution)/shard_map/ppermute | solution.py:1332
  165.5 11.3 %collective-permute-start.6 = (bf16[2,512,384]{2,1,0:T(8,128)(2,1)S(1)}, bf16[2,512,384]{2,1,0:T(8,128)(2,1)}, u32[]{:S(2)}, u32[]{:S(2)}) collective-permute-start(bf16[2,512,384]{2,1,0:T(8,128)(2,1)S(1)} %pad_maximum_fusion.19), channel_id=1, source_target_pairs={{0,1},{1,0},{2,3},{3,2},{4,5},{5,4},{6,7},{7,6},{8,9},{9,8},{10,11... | collective-permute-start | bytes 2359304 | tf_op jit(solution)/shard_map/ppermute | solution.py:1240
  168.2 8.7 %copy-start.14 = (bf16[1,2,512,1536]{3,2,1,0:T(8,128)(2,1)S(1)}, bf16[1,2,512,1536]{3,2,1,0:T(8,128)(2,1)}, u32[]{:S(2)}) copy-start(bf16[1,2,512,1536]{3,2,1,0:T(8,128)(2,1)} %copy-done.13) | copy-start | bytes 9437188
  175.4 6.5 collective-permute-start.2
  181.6 9.0 %copy-start.4 = (f32[2,512,1536]{2,1,0:T(8,128)}, f32[2,512,1536]{2,1,0:T(8,128)S(1)}, u32[]{:S(2)}) copy-start(f32[2,512,1536]{2,1,0:T(8,128)S(1)} %get-tuple-element.192) | copy-start | bytes 18874372
  493.0 6.4 copy-start.9
  493.0 5.5 copy-start.25
  494.5 211.6 %collective-permute-start.13 = (bf16[192,1536]{1,0:T(8,128)(2,1)}, bf16[192,1536]{1,0:T(8,128)(2,1)}, u32[]{:S(2)}, u32[]{:S(2)}) collective-permute-start(bf16[192,1536]{1,0:T(8,128)(2,1)} %get-tuple-element.92), channel_id=1, source_target_pairs={{0,2},{1,3},{2,0},{3,1},{4,6},{5,7},{6,4},{7,5},{8,10},{9,11},{10,... | collective-permute-start | bytes 1769480 | tf_op jit(solution)/shard_map/ppermute | solution.py:1450
  496.4 209.8 %collective-permute-start.14 = (bf16[192,1536]{1,0:T(8,128)(2,1)}, bf16[192,1536]{1,0:T(8,128)(2,1)}, u32[]{:S(2)}, u32[]{:S(2)}) collective-permute-start(bf16[192,1536]{1,0:T(8,128)(2,1)} %get-tuple-element.95), channel_id=1, source_target_pairs={{0,2},{1,3},{2,0},{3,1},{4,6},{5,7},{6,4},{7,5},{8,10},{9,11},{10,... | collective-permute-start | bytes 1769480 | tf_op jit(solution)/shard_map/ppermute | solution.py:1450
  496.5 209.7 %collective-permute-start.15 = (bf16[192,1536]{1,0:T(8,128)(2,1)}, bf16[192,1536]{1,0:T(8,128)(2,1)}, u32[]{:S(2)}, u32[]{:S(2)}) collective-permute-start(bf16[192,1536]{1,0:T(8,128)(2,1)} %get-tuple-element.94), channel_id=1, source_target_pairs={{0,2},{1,3},{2,0},{3,1},{4,6},{5,7},{6,4},{7,5},{8,10},{9,11},{10,... | collective-permute-start | bytes 1769480 | tf_op jit(solution)/shard_map/ppermute | solution.py:1450
  498.4 207.8 %collective-permute-start.16 = (bf16[192,1536]{1,0:T(8,128)(2,1)}, bf16[192,1536]{1,0:T(8,128)(2,1)}, u32[]{:S(2)}, u32[]{:S(2)}) collective-permute-start(bf16[192,1536]{1,0:T(8,128)(2,1)} %get-tuple-element.93), channel_id=1, source_target_pairs={{0,2},{1,3},{2,0},{3,1},{4,6},{5,7},{6,4},{7,5},{8,10},{9,11},{10,... | collective-permute-start | bytes 1769480 | tf_op jit(solution)/shard_map/ppermute | solution.py:1450
  500.4 12.1 %slice-start.2 = ((s8[6291456]{0:T(1024)(128)(4,1)}), s8[4194304]{0:T(1024)(128)(4,1)S(1)}, s32[]{:S(2)}) async-start(s8[6291456]{0:T(1024)(128)(4,1)} %bitcast.220), calls=%async_computation.4 | async-start | bytes 8388608
  501.3 11.2 %copy-start = (f32[4,256,1536]{2,1,0:T(8,128)}, f32[4,256,1536]{2,1,0:T(8,128)S(1)}, u32[]{:S(2)}) copy-start(f32[4,256,1536]{2,1,0:T(8,128)S(1)} %convert_element_type.207) | copy-start | bytes 18874372
  502.5 6.2 copy-start.22
  502.5 10.0 %slice-start = ((s8[6291456]{0:T(1024)(128)(4,1)}), s8[4194304]{0:T(1024)(128)(4,1)S(1)}, s32[]{:S(2)}) async-start(s8[6291456]{0:T(1024)(128)(4,1)} %bitcast.218), calls=%async_computation.2 | async-start | bytes 8388608
  502.5 10.0 %slice-start.3 = ((s8[6291456]{0:T(1024)(128)(4,1)}), s8[2097152]{0:T(1024)(128)(4,1)S(1)}, s32[]{:S(2)}) async-start(s8[6291456]{0:T(1024)(128)(4,1)} %bitcast.220), calls=%async_computation.5 | async-start | bytes 4194304
  506.3 6.7 slice-start.1
  535.9 9.3 %collective-permute-start.8 = (bf16[2,256,384]{2,1,0:T(8,128)(2,1)S(1)}, bf16[2,256,384]{2,1,0:T(8,128)(2,1)S(1)}, u32[]{:S(2)}, u32[]{:S(2)}) collective-permute-start(bf16[2,256,384]{2,1,0:T(8,128)(2,1)S(1)} %convolution_convert_fusion.2), channel_id=1, source_target_pairs={{0,1},{1,0},{2,3},{3,2},{4,5},{5,4},{6,7},{7,6},{8,9},{9,8},{10,11... | collective-permute-start | bytes 1179656 | tf_op jit(solution)/shard_map/ppermute | solution.py:1240
  545.2 1.8 collective-permute-start.7
  688.5 21.5 %collective-permute-start.11 = (bf16[4,192,384]{2,1,0:T(8,128)(2,1)S(1)}, bf16[4,192,384]{2,1,0:T(8,128)(2,1)S(1)}, u32[]{:S(2)}, u32[]{:S(2)}) collective-permute-start(bf16[4,192,384]{2,1,0:T(8,128)(2,1)S(1)} %convert_element_type.230), channel_id=1, source_target_pairs={{0,2},{1,3},{2,0},{3,1},{4,6},{5,7},{6,4},{7,5},{8,10},{9,11},{10,... | collective-permute-start | bytes 1769480 | tf_op jit(solution)/shard_map/ppermute | solution.py:1450
  692.3 6.3 copy-start.34
  692.3 6.3 copy-start.33
  692.3 6.3 copy-start.53
  706.1 21.0 %collective-permute-start.9 = (bf16[2,256,1536]{2,1,0:T(8,128)(2,1)S(1)}, bf16[2,256,1536]{2,1,0:T(8,128)(2,1)S(1)}, u32[]{:S(2)}, u32[]{:S(2)}) collective-permute-start(bf16[2,256,1536]{2,1,0:T(8,128)(2,1)S(1)} %copy-done.71), channel_id=1, source_target_pairs={{0,1},{1,0},{2,3},{3,2},{4,5},{5,4},{6,7},{7,6},{8,9},{9,8},{10,11... | collective-permute-start | bytes 4718600 | tf_op jit(solution)/shard_map/ppermute | solution.py:1240
  708.5 5.1 collective-permute-start.17
  709.2 4.8 collective-permute-start.18
  709.3 5.6 collective-permute-start.19
  710.1 6.5 collective-permute-start.20
  713.6 11.2 %collective-permute-start.10 = (bf16[2,256,1536]{2,1,0:T(8,128)(2,1)S(1)}, bf16[2,256,1536]{2,1,0:T(8,128)(2,1)S(1)}, u32[]{:S(2)}, u32[]{:S(2)}) collective-permute-start(bf16[2,256,1536]{2,1,0:T(8,128)(2,1)S(1)} %fusion.44), channel_id=1, source_target_pairs={{0,1},{1,0},{2,3},{3,2},{4,5},{5,4},{6,7},{7,6},{8,9},{9,8},{10,11... | collective-permute-start | bytes 4718600 | tf_op jit(solution)/shard_map/ppermute | solution.py:1240
  714.0 75.8 %collective-permute-start.12 = (f32[4,192,384]{2,1,0:T(8,128)}, f32[4,192,384]{2,1,0:T(8,128)}, u32[]{:S(2)}, u32[]{:S(2)}) collective-permute-start(f32[4,192,384]{2,1,0:T(8,128)} %convert_add_fusion.8), channel_id=1, source_target_pairs={{0,1},{1,0},{2,3},{3,2},{4,5},{5,4},{6,7},{7,6},{8,9},{9,8},{10,11... | collective-permute-start | bytes 3538952 | tf_op jit(solution)/shard_map/ppermute | solution.py:1240
  719.2 5.6 slice-start.8
  727.1 5.6 copy-start.21
  727.1 5.6 copy-start.56
  727.1 5.6 copy-start.70
  727.1 50.0 %copy-start.62 = (f32[2,512]{1,0:T(2,128)S(1)}, f32[2,512]{1,0:T(2,128)}, u32[]{:S(2)}) copy-start(f32[2,512]{1,0:T(2,128)} %copy-done.60) | copy-start | bytes 12292
  727.1 50.7 %copy-start.65 = (f32[2,512]{1,0:T(2,128)S(1)}, f32[2,512]{1,0:T(2,128)}, u32[]{:S(2)}) copy-start(f32[2,512]{1,0:T(2,128)} %copy-done.63) | copy-start | bytes 12292
  727.1 54.0 %copy-start.2 = (f32[2,256,1536]{2,1,0:T(8,128)S(1)}, f32[2,256,1536]{2,1,0:T(8,128)}, u32[]{:S(2)}) copy-start(f32[2,256,1536]{2,1,0:T(8,128)} %get-tuple-element.71) | copy-start | bytes 9437188
  (41 other events, 127.8 us)
Sparse Core Ops, SparseCore 0:
  65.9 78.4 all-gather.2
  147.2 78.0 all-gather.4

commit v4 on v3

--- a/solution.py
+++ b/solution.py
@@ -267,15 +267,18 @@
         self.plane = seq // 2
         self.sibling = {"seq": self.plane * 2 + 1 - self.core}
         self.across = {"seq": (1 - self.plane) * 2 + self.core}
+        self.diagonal = {"seq": (1 - self.plane) * 2 + 1 - self.core}
         self.ahead = {"dp": self.owner(1)}
         self.behind = {"dp": self.owner(-1)}
 
     def owner(self, shift):
         return pick(self.order, lax.rem(self.place + shift + self.count, self.count))
 
-    def greet(self):
+    def greet(self, diagonal=False):
         barrier = pltpu.get_barrier_semaphore()
         friends = [self.ahead, self.behind, self.sibling] + ([self.across] if self.planes == 2 else [])
+        if diagonal:
+            friends.append(self.diagonal)
         for friend in friends:
             pl.semaphore_signal(barrier, inc=1, device_id=friend, device_id_type=MESH)
         pl.semaphore_wait(barrier, len(friends))
@@ -829,18 +832,18 @@
 
 def mix_back_kernel(plan, len_ref, lse_ref, diag_ref, *refs):
     count, planes, rows, micro, rows_of, head_dim, block, pairs = plan
-    qkvs, grads_mixed = refs[:micro], refs[micro : 2 * micro]
-    attn_in, mixed, normed = refs[2 * micro : 2 * micro + 3]
-    dqkv, dd_ref, totals, attn_there = refs[2 * micro + 3 : 2 * micro + 7]
+    qkvs = refs[:micro]
+    made_own, made_other, attn_in, mixed, normed = refs[micro : micro + 5]
+    dqkv_own, dqkv_there, dd_ref, totals, attn_there = refs[micro + 5 : micro + 10]
     (
         qkv_v, do_v, res, sums_v, attn_v, mixed_v, normed_v, grads, inbox,
         strip, keys, acc_bias, acc_k, acc_v, mine, came, made, total,
         load_sems, do_sems, res_sems, attn_sems, dqkv_sems, send_sems, recv_sems, near_sems, total_sems,
-    ) = refs[2 * micro + 7 :]
+    ) = refs[micro + 10 :]
     seq_len = do_v.shape[1]
     span = diag_ref.shape[-1]
     plane_len = seq_len // 2
-    local = attn_in.shape[2]
+    local = attn_in.shape[1]
     steps = seq_len // block
     per = LANES // head_dim
     wide = 3 * LANES
@@ -854,16 +857,23 @@
     def at_rows(start, size):
         return pl.ds(pl.multiple_of(start, 16), size)
 
-    def do_far(m):
-        return pltpu.make_async_remote_copy(
-            src_ref=grads_mixed[m].at[1 - plane], dst_ref=do_v.at[m, at_rows(plane * plane_len, plane_len)],
-            send_sem=do_sems.at[m, 0], recv_sem=do_sems.at[m, 1], device_id=links.across, device_id_type=MESH,
-        )
-
-    def do_near(m):
-        return pltpu.make_async_copy(
-            grads_mixed[m].at[plane], do_v.at[m, at_rows(plane * plane_len, plane_len)], do_sems.at[m, 2]
-        )
+    def do_copies(m):
+        at = lambda p, c: do_v.at[m, at_rows((2 * p + c) * local, local)]
+        far = []
+        for way, (source, row, device) in enumerate(
+            (
+                (made_other, plane, links.sibling),
+                (made_own, 1 - plane, links.across),
+                (made_other, 1 - plane, links.diagonal),
+            )
+        ):
+            far.append(
+                pltpu.make_async_remote_copy(
+                    src_ref=source.at[m * rows_of + row], dst_ref=at(plane, core), send_sem=do_sems.at[m, way],
+                    recv_sem=do_sems.at[m, 3 + way], device_id=device, device_id_type=MESH,
+                )
+            )
+        return far, pltpu.make_async_copy(made_own.at[m * rows_of + plane], at(plane, core), do_sems.at[m, 6])
 
     def attn_far():
         return pltpu.make_async_remote_copy(
@@ -881,7 +891,7 @@
                     start = (m * rows_of + r) * 2 * local + half * local
                     at = (m * rows_of + r) * 2 + side
                     copies.append(
-                        pltpu.make_async_copy(source.at[m, r], attn_v.at[at_rows(start, local)], attn_sems.at[4 + at])
+                        pltpu.make_async_copy(source.at[m * rows_of + r], attn_v.at[at_rows(start, local)], attn_sems.at[4 + at])
                     )
         return copies
 
@@ -916,19 +926,28 @@
             device_id=links.across, device_id_type=MESH,
         )
 
-    def dqkv_copy(p, at):
+    def dqkv_near(p, at):
         return pltpu.make_async_copy(
-            sums_v.at[p, at], dqkv.at[at, :, pl.ds(p * wide, wide)], dqkv_sems.at[p, at]
+            sums_v.at[p, at, at_rows(core * local, local)], dqkv_own.at[at, :, pl.ds(p * wide, wide)], dqkv_sems.at[p, at, 0]
+        )
+
+    def dqkv_far(p, at):
+        return pltpu.make_async_remote_copy(
+            src_ref=sums_v.at[p, at, at_rows((1 - core) * local, local)],
+            dst_ref=dqkv_there.at[at, :, pl.ds(p * wide, wide)],
+            send_sem=dqkv_sems.at[p, at, 1], recv_sem=dqkv_sems.at[p, at, 2],
+            device_id=links.sibling, device_id_type=MESH,
         )
 
     start_unit(jnp.int32(0))
     mixed_load.start()
     normed_load.start()
     for m in range(micro):
-        do_near(m).start()
-    links.greet()
+        do_copies(m)[1].start()
+    links.greet(True)
     for m in range(micro):
-        do_far(m).start()
+        for copy in do_copies(m)[0]:
+            copy.start()
     attn_far().start()
     scatter = Scatter(
         links, grads, inbox, totals, mine, came, made, total, send_sems, recv_sems, near_sems, total_sems, rows
@@ -953,7 +972,8 @@
         for m in range(micro):
             res_far(jnp.int32(p * micro + m)).wait_recv()
         for at in range(micro * rows_of):
-            dqkv_copy(p, at).start()
+            dqkv_near(p, at).start()
+            dqkv_far(p, at).start()
         right = sums_v[p].reshape(micro * rows_of * plane_len, wide)
         weight_grads(1 + p, normed_v, right)
 
@@ -1007,8 +1027,10 @@
 
                 @pl.when(u == k)
                 def _(k=k):
-                    do_near(k).wait()
-                    do_far(k).wait_recv()
+                    far_copies, near_copy = do_copies(k)
+                    near_copy.wait()
+                    for copy in far_copies:
+                        copy.wait_recv()
 
             @pl.when(u >= 2)
             def _():
@@ -1087,17 +1109,21 @@
     lax.fori_loop(0, last + 1, item, 0)
     scatter.total_copy(jnp.int32(pairs)).wait()
     for m in range(micro):
-        do_far(m).wait_send()
+        for copy in do_copies(m)[0]:
+            copy.wait_send()
     attn_far().wait_send()
     for u in range(max(0, units - 2), units):
         res_far(jnp.int32(u)).wait_send()
     for p in range(pairs):
         for at in range(micro * rows_of):
-            dqkv_copy(p, at).wait()
-
-
-def mix_back(qkvs, grads_mixed, attn_in, mixed, normed, lse, diag, lengths, head_dim, count, planes, block=256):
-    micro, rows_of, local, depth = attn_in.shape
+            dqkv_near(p, at).wait()
+            dqkv_far(p, at).wait()
+
+
+def mix_back(qkvs, made_own, made_other, attn_in, mixed, normed, lse, diag, lengths, head_dim, count, planes, block=256):
+    micro = len(qkvs)
+    rows_of = attn_in.shape[0] // micro
+    _, local, depth = attn_in.shape
     seq_len, cols = qkvs[0].shape[0], qkvs[0].shape[1] // 3
     pairs, per, span = cols // LANES, LANES // head_dim, diag.shape[-1]
     tokens = normed.shape[0]
@@ -1111,10 +1137,11 @@
         functools.partial(mix_back_kernel, plan),
         in_specs=[pl.BlockSpec(memory_space=pltpu.SMEM)]
         + [pl.BlockSpec(memory_space=pltpu.VMEM)] * 2
-        + [anywhere] * (2 * micro + 3),
-        out_specs=[anywhere, pl.BlockSpec(memory_space=pltpu.VMEM), anywhere, anywhere],
+        + [anywhere] * (micro + 5),
+        out_specs=[anywhere, anywhere, pl.BlockSpec(memory_space=pltpu.VMEM), anywhere, anywhere],
         out_shape=[
-            jax.ShapeDtypeStruct((micro * rows_of, 2 * local, 3 * cols), low),
+            jax.ShapeDtypeStruct((micro * rows_of, local, 3 * cols), low),
+            jax.ShapeDtypeStruct((micro * rows_of, local, 3 * cols), low),
             jax.ShapeDtypeStruct(diag.shape, f32),
             jax.ShapeDtypeStruct((groups, rows, wide), f32),
             jax.ShapeDtypeStruct(attn_in.shape, low),
@@ -1139,10 +1166,10 @@
             pltpu.VMEM((2, 2, rows, wide), low),
             pltpu.VMEM((rows, wide), f32),
             dma((2, 3)),
-            dma((micro, 3)),
+            dma((micro, 7)),
             dma((2, pairs * micro)),
             dma((4 + 2 * micro * rows_of,)),
-            dma((pairs, micro * rows_of)),
+            dma((pairs, micro * rows_of, 3)),
             dma((groups, 2, far)),
             dma((groups, 2, far)),
             dma((2, 2, 2)),
@@ -1152,7 +1179,122 @@
             collective_id=2, has_side_effects=True, vmem_limit_bytes=62 * 1024 * 1024
         ),
         name="mix_back",
-    )(lengths, lse, diag, *qkvs, *grads_mixed, attn_in, mixed, normed)
+    )(lengths, lse, diag, *qkvs, made_own, made_other, attn_in, mixed, normed)
+
+
+def resid_back_kernel(kept, got, out_kept, out_got, resid_ref, cot, gain, w_own, w_other, grad_ref, attn_ref, own_ref, other_ref, out_ref, sum_ref):
+    @pl.when(pl.program_id(0) == 0)
+    def _():
+        sum_ref[...] = jnp.zeros_like(sum_ref)
+
+    wide = jnp.float32
+    resid = resid_ref[...]
+    out_ref[...] = (resid + (out_kept[...].astype(wide) + out_got[...].astype(wide))).astype(out_ref.dtype)
+    grad = kept[...].astype(wide) + got[...].astype(wide)
+    root = lax.rsqrt(jnp.mean(resid * resid, axis=-1, keepdims=True) + eps)
+    sum_ref[...] += jnp.sum(grad * resid * root, axis=0, keepdims=True)
+    scaled = grad * gain[...]
+    shared = jnp.mean(scaled * resid, axis=-1, keepdims=True) * root * root * root
+    total = cot[...].astype(wide) + scaled * root - resid * shared
+    grad_ref[...] = total
+    low = total.astype(attn_ref.dtype)
+    attn_ref[...] = low
+    own_ref[...] = dot32(low, w_own[...], NN).astype(own_ref.dtype)
+    other_ref[...] = dot32(low, w_other[...], NN).astype(other_ref.dtype)
+
+
+def resid_back(kept, got, out_kept, out_got, resid, cotangent, gain, w_own, w_other):
+    groups, tile, depth = kept.shape
+    cols = w_own.shape[1]
+    tall = lambda width: pl.BlockSpec((None, tile, width), lambda g: (g, 0, 0))
+    flat = lambda shape: pl.BlockSpec(shape, lambda g: (0, 0))
+    low, wide = jnp.bfloat16, jnp.float32
+    shape = lambda width, kind: jax.ShapeDtypeStruct((groups, tile, width), kind)
+    return pl.pallas_call(
+        resid_back_kernel,
+        grid=(groups,),
+        in_specs=[tall(depth)] * 6 + [flat((1, depth)), flat((depth, cols)), flat((depth, cols))],
+        out_specs=[tall(depth), tall(depth), tall(cols), tall(cols), tall(depth), flat((1, depth))],
+        out_shape=[
+            shape(depth, wide), shape(depth, low), shape(cols, low), shape(cols, low), shape(depth, low),
+            jax.ShapeDtypeStruct((1, depth), wide),
+        ],
+        compiler_params=pltpu.CompilerParams(vmem_limit_bytes=VMEM_LIMIT),
+        name="resid_back",
+    )(kept, got, out_kept, out_got, resid, cotangent, gain, w_own, w_other)
+
+
+def input_back_kernel(own, there, w_own, w_other, tokens, grad_resid, gain, out_ref, sum_ref):
+    @pl.when(pl.program_id(0) == 0)
+    def _():
+        sum_ref[...] = jnp.zeros_like(sum_ref)
+
+    grad = dot32(own[...], w_own[...], NT) + dot32(there[...], w_other[...], NT)
+    values = tokens[...].astype(jnp.float32)
+    root = lax.rsqrt(jnp.mean(values * values, axis=-1, keepdims=True) + eps)
+    sum_ref[...] += jnp.sum(grad * values * root, axis=0, keepdims=True)
+    scaled = grad * gain[...]
+    shared = jnp.mean(scaled * values, axis=-1, keepdims=True) * root * root * root
+    out_ref[...] = grad_resid[...] + scaled * root - values * shared
+
+
+def input_back(own, there, w_own, w_other, tokens, grad_resid, gain):
+    groups, tile, depth = tokens.shape
+    cols = own.shape[2]
+    tall = lambda width: pl.BlockSpec((None, tile, width), lambda g: (g, 0, 0))
+    flat = lambda shape: pl.BlockSpec(shape, lambda g: (0, 0))
+    return pl.pallas_call(
+        input_back_kernel,
+        grid=(groups,),
+        in_specs=[tall(cols), tall(cols), flat((depth, cols)), flat((depth, cols)), tall(depth), tall(depth), flat((1, depth))],
+        out_specs=[tall(depth), flat((1, depth))],
+        out_shape=[
+            jax.ShapeDtypeStruct((groups, tile, depth), jnp.float32), jax.ShapeDtypeStruct((1, depth), jnp.float32)
+        ],
+        compiler_params=pltpu.CompilerParams(vmem_limit_bytes=VMEM_LIMIT),
+        name="input_back",
+    )(own, there, w_own, w_other, tokens, grad_resid, gain)
+
+
+def small_sum_kernel(sizes, x_ref, o_ref, outbox, inbox, send_sems, recv_sems):
+    partners = []
+    for name, size in sizes:
+        at, bit = lax.axis_index(name), 1
+        while bit < size:
+            partners.append({name: jnp.where(lax.rem(at // bit, 2) == 0, at + bit, at - bit)})
+            bit *= 2
+    barrier = pltpu.get_barrier_semaphore()
+    for partner in partners:
+        pl.semaphore_signal(barrier, inc=1, device_id=partner, device_id_type=MESH)
+    pl.semaphore_wait(barrier, len(partners))
+    o_ref[...] = x_ref[...]
+    for at, partner in enumerate(partners):
+        outbox[at] = o_ref[...]
+        copy = pltpu.make_async_remote_copy(
+            src_ref=outbox.at[at], dst_ref=inbox.at[at], send_sem=send_sems.at[at], recv_sem=recv_sems.at[at],
+            device_id=partner, device_id_type=MESH,
+        )
+        copy.start()
+        copy.wait()
+        o_ref[...] += inbox[at]
+
+
+def small_sum(values, sizes):
+    rounds = sum(size.bit_length() - 1 for _, size in sizes)
+    return pl.pallas_call(
+        functools.partial(small_sum_kernel, sizes),
+        in_specs=[pl.BlockSpec(memory_space=pltpu.VMEM)],
+        out_specs=pl.BlockSpec(memory_space=pltpu.VMEM),
+        out_shape=jax.ShapeDtypeStruct(values.shape, values.dtype),
+        scratch_shapes=[
+            pltpu.VMEM((rounds,) + values.shape, values.dtype),
+            pltpu.VMEM((rounds,) + values.shape, values.dtype),
+            pltpu.SemaphoreType.DMA((rounds,)),
+            pltpu.SemaphoreType.DMA((rounds,)),
+        ],
+        compiler_params=pltpu.CompilerParams(collective_id=3, has_side_effects=True),
+        name="small_sum",
+    )(values)
 
 
 class Ring:
@@ -1279,9 +1421,10 @@
     gain_second = small[:, shard_rows : 2 * shard_rows].reshape(-1)
     full_table = small[:, 2 * shard_rows : 2 * shard_rows + table.size].reshape(-1, heads)
     last = attn_weights
-    qkv_weights = attn_weights[:, : 3 * half_inner]
-    out_own = attn_weights[:, 3 * half_inner :]
-    out_other = swap_core(out_own)
+    qkv_cols = 3 * half_inner
+    there_weights = swap_core(attn_weights)
+    qkv_weights = attn_weights[:, :qkv_cols]
+    out_own, out_other = attn_weights[:, qkv_cols:], there_weights[:, qkv_cols:]
     out_pair = jnp.concatenate([out_own, out_other], axis=1)
 
     early = min(2, chunks - 1)
@@ -1386,63 +1529,37 @@
     back_kept, back_got, out_kept, out_got, chunk_totals = feed(
         normed_two_all, down_all, ready, chunk_shards[early:], dp_devices, planes, local
     )
-    back_kept, back_got, out_kept, out_got = [
-        v.reshape(micro, rows, local, width).astype(jnp.float32) for v in (back_kept, back_got, out_kept, out_got)
-    ]
-
-    grad_resids, grads_mixed, attn_ins = [], [], []
-    gain_two_sum = jnp.zeros((width,), jnp.float32)
-    for step in range(micro):
-        grad_normed = back_kept[step] + back_got[step]
-        resid = resids[step]
-        root = lax.rsqrt(jnp.mean(resid * resid, axis=-1, keepdims=True) + eps)
-        gain_two_sum = gain_two_sum + jnp.sum(grad_normed * resid * root, axis=(0, 1))
-        scaled = grad_normed * gain_second
-        shared = jnp.mean(scaled * resid, axis=-1, keepdims=True) * root * root * root
-        grad_resid = cotangent[step].astype(jnp.float32) + scaled * root - resid * shared
-        grad_resids.append(grad_resid)
-        attn_in = grad_resid.astype(jnp.bfloat16)
-        attn_ins.append(attn_in)
-        made_own = jnp.einsum("rld,de->rle", attn_in, out_own, preferred_element_type=jnp.float32).astype(jnp.bfloat16)
-        made_other = jnp.einsum("rld,de->rle", attn_in, out_other, preferred_element_type=jnp.float32).astype(
-            jnp.bfloat16
-        )
-        grads_mixed.append(both_cores(made_own, swap_core(made_other), 1))
-
-    outputs = []
-    for step in range(micro):
-        outputs.append((resids[step] + out_kept[step] + out_got[step]).astype(jnp.bfloat16))
+    by_row = lambda value: value.reshape(micro * rows, local, value.shape[-1])
+    grad_resid, attn_in, made_own, made_other, output, gain_two_sum = resid_back(
+        back_kept, back_got, out_kept, out_got, jnp.concatenate(resids), by_row(cotangent), gain_second[None],
+        out_own, out_other,
+    )
 
     normed_all = jnp.concatenate([flat(v) for v in normed])
     mixed_all = jnp.concatenate([flat(v) for v in mixes])
-    attn_all = jnp.stack(attn_ins)
     if fused:
-        grads_all, diag_sum, attn_totals, _ = mix_back(
-            qkvs, grads_mixed, attn_all, mixed_all, normed_all, jnp.concatenate(lses), diag,
+        own, there, diag_sum, attn_totals, _ = mix_back(
+            qkvs, made_own, made_other, attn_in, mixed_all, normed_all, jnp.concatenate(lses), diag,
             jnp.concatenate(item_lens), head_dim, dp_devices, planes,
         )
-        grads_qkv = grads_all.reshape(micro, rows, pair_local, 3 * half_inner)
+        input_grad, gain_one_sum = input_back(
+            own, there, attn_weights, there_weights, by_row(tokens), grad_resid, gain_first[None]
+        )
         diag_sum = diag_sum[:, 0]
     else:
+        split_micro = lambda value: value.reshape(micro, rows, local, -1)
+        grads_mixed = both_cores(split_micro(made_own), swap_core(split_micro(made_other)), 2)
         grads_qkv, diag_sum, attn_totals = apart(
-            qkvs, [to_items(g, 1) for g in grads_mixed], lses, item_lens, attn_all, mixed_all, normed_all
+            qkvs, [to_items(g, 1) for g in grads_mixed], lses, item_lens, split_micro(attn_in), mixed_all, normed_all
+        )
+        grads_qkv = jnp.stack(grads_qkv)
+        own = by_row(own_half(grads_qkv, 2))
+        there = swap_core(by_row(other_half(grads_qkv, 2)))
+        input_grad, gain_one_sum = input_back(
+            own, there, attn_weights, there_weights, by_row(tokens), grad_resid, gain_first[None]
         )
     item_grad = jnp.dot(diag_sum, bucket_hot, precision=highest)
     grad_table = lax.dynamic_update_slice(jnp.zeros((heads, levels), jnp.float32), item_grad, (head_start, 0))
-
-    input_grads = []
-    gain_one_sum = jnp.zeros((width,), jnp.float32)
-    for step in range(micro):
-        made = jnp.einsum("rle,de->rld", other_half(grads_qkv[step], 1), qkv_weights, preferred_element_type=jnp.float32)
-        got = swap_core(made.astype(jnp.bfloat16))
-        kept = jnp.einsum("rle,de->rld", own_half(grads_qkv[step], 1), qkv_weights, preferred_element_type=jnp.float32)
-        grad_normed = kept + got.astype(jnp.float32)
-        rows_in = tokens[step].astype(jnp.float32)
-        root = own_half(roots[step], 1)
-        gain_one_sum = gain_one_sum + jnp.sum(grad_normed * rows_in * root, axis=(0, 1))
-        scaled = grad_normed * gain_first
-        shared = jnp.mean(scaled * rows_in, axis=-1, keepdims=True) * root * root * root
-        input_grads.append(grad_resids[step] + scaled * root - rows_in * shared)
 
     def finish(total):
         if planes == 2:
@@ -1471,7 +1588,8 @@
     else:
         parts = [slice(i * half_inner, (i + 1) * half_inner) for i in range(4)]
         grad_out, grad_query, grad_key, grad_value = [whole_columns(own[:, p], other[:, p], inner) for p in parts]
-    done = [finish(chunk_totals[n]) for n in range(chunks)]
+    own, other = finish(chunk_totals)
+    done = [(own[n], other[n]) for n in range(chunks)]
     parts = [slice(i * chunk, (i + 1) * chunk) for i in range(3)]
     grad_gate, grad_up, grad_down = [
         whole_columns(
@@ -1483,16 +1601,16 @@
     ]
 
     dp_rank = lax.axis_index("dp")
-    small = lax.psum(
-        jnp.concatenate([gain_one_sum, gain_two_sum, grad_table.T.reshape(-1)]), ("dp", "seq")
-    )
+    small = jnp.concatenate([gain_one_sum[0], gain_two_sum[0], grad_table.T.reshape(-1)])
+    small = jnp.pad(small, (0, -small.shape[0] % (8 * LANES))).reshape(-1, LANES)
+    small = small_sum(small, (("seq", seq_devices), ("dp", dp_devices))).reshape(-1)
     grad_gain_one = lax.dynamic_slice_in_dim(small, dp_rank * shard_rows, shard_rows, 0)
     grad_gain_two = lax.dynamic_slice_in_dim(small, width + dp_rank * shard_rows, shard_rows, 0)
     table_part = levels // dp_devices
-    grad_table = lax.dynamic_slice_in_dim(small[2 * width :].reshape(levels, heads), dp_rank * table_part, table_part, 0)
+    grad_table = lax.dynamic_slice_in_dim(small[2 * width : 2 * width + levels * heads].reshape(levels, heads), dp_rank * table_part, table_part, 0)
 
     return (
-        jnp.stack(outputs), jnp.stack(input_grads), grad_gain_one, grad_gain_two, grad_table,
+        output.reshape(tokens.shape), input_grad.reshape(tokens.shape), grad_gain_one, grad_gain_two, grad_table,
         grad_query, grad_key, grad_value, grad_out.T, grad_gate, grad_up, grad_down.T,
     )
 

time: 807 us -> 767 us (0.950)
  Pallas kernels: 493 us -> 586 us
  blocking collectives: 41.3 us -> 0 us
  other arithmetic: 109 us -> 76.8 us
  matrix products: 48.8 us -> 17.1 us
  waiting for transfers between devices: 38.7 us -> 13.4 us
    pallas_call x0 -> x3, Pallas kernels: none -> 46.4 us  [the longest x1 16 us: small_sum(): pl.pallas_call(functools.partial(small_sum_kernel, sizes), in_specs=[pl.B...]
    psum x1 -> x0, blocking collectives: 41.3 us -> none  [body(): lax.psum(jnp.concatenate([gain_one_sum, gain_two_sum, grad_table.T.reshap...]
    another operation x6 -> x0, other arithmetic: 29.9 us -> none  [the longest x2 16.8 us: body(): jnp.stack(outputs)]
    all_gather x2, waiting for transfers between devices: 29.3 us -> 0.01 us  [body(): ready.append(lax.all_gather(shard, 'dp', axis=0, tiled=True))]
    pallas_call x1, Pallas kernels: 46.9 us -> 76.2 us  [gather_first(): pl.pallas_call(functools.partial(gather_kernel, count, planes, rows), in_...]
    dot_general x8 -> x0, matrix products: 28.5 us -> none  [the longest x2 10.6 us: body(): jnp.einsum('rle,de->rld', other_half(grads_qkv[step], 1), qkv_weights, pr...]
    pallas_call x1, Pallas kernels: 139 us -> 152 us  [mix_back(): pl.pallas_call(functools.partial(mix_back_kernel, plan), in_specs=[pl.Blo...]
    convert_element_type x4 -> x0, other arithmetic: 9.43 us -> none  [body(): v.reshape(micro, rows, local, width).astype(jnp.float32)]
  transfers between devices with their start and end apart: 23 -> 13, of which waited for: 5 -> 2; matrix products, arithmetic and copies ran while one was open for 21% -> 15% of each run, Pallas kernels for 23% -> 42%
where the time goes in v4:
time: 767 us; the launch traced here: 758 us
  Pallas kernels  586 us (76%)
  other arithmetic  76.8 us (10%)
  local copies, waits for them, and re-layouts  42.3 us (6%)
  matrix products  17.1 us (2%)
  between operations  15.4 us (2%)
  waiting for transfers between devices  13.4 us (2%)
    pallas_call x1, Pallas kernels, feed(): pl.pallas_call(functools.partial(feed_kernel, plan), in_specs=[anywhere]...  269 us
    pallas_call x1, Pallas kernels, mix_back(): pl.pallas_call(functools.partial(mix_back_kernel, plan), in_specs=[pl.Blo...  152 us
    pallas_call x1, Pallas kernels, gather_first(): pl.pallas_call(functools.partial(gather_kernel, count, planes, rows), in_...  76.2 us
    pallas_call x2, Pallas kernels, attend(): pl.pallas_call(functools.partial(attend_kernel, head_dim, block), grid=(p...  42.2 us
    pallas_call x1, Pallas kernels, small_sum(): pl.pallas_call(functools.partial(small_sum_kernel, sizes), in_specs=[pl.B...  16 us
    pallas_call x1, Pallas kernels, input_back(): pl.pallas_call(input_back_kernel, grid=(groups,), in_specs=[tall(cols), t...  15.6 us
  transfers between devices with their start and end apart: 13, of which 2 were waited for; matrix products, arithmetic and copies ran while one was open for 15% of the time, Pallas kernels for 42%

profile of v4, /device:TPU:0, one launch (start us, length us, event | category | flops | bytes accessed | tf_op | source)
XLA Modules:
  0.0 757.6 jit_solution(17582635167745348763)
XLA Ops:
  7.2 1.2 slice.384
  8.4 1.5 slice_select_fusion.3
  21.7 76.2 %gather_first.1 = (bf16[1536,1536]{1,0:T(8,128)(2,1)}, bf16[128,512]{1,0:T(8,128)(2,1)}, bf16[2,2,256,1536]{3,2,1,0:T(8,128)(2,1)}, bf16[2,2,256,1536]{3,2,1,0:T(8,128)(2,1)}) custom-call(bf16[192,1536]{1,0:T(8,128)(2,1)} %fusion.41.shard, bf16[16,512]{1,0:T(8,128)(2,1)} %pad.30.small, bf16[2,2,256,1536]{3,2,1,0:T(8,128)(2,1)} %tokens.1, ...), custom_call_target="tpu_custom_call" | custom-call | tf_op jit(solution)/shard_map/gather_first/pallas_call | solution.py:439
  100.1 2.4 broadcast_select_fusion.3
  102.6 1.5 fusion.7
  104.8 4.6 convolution_convert_fusion
  109.4 1.3 dynamic-slice_bitcast_fusion
  110.7 1.0 collective-permute-start.4
  112.3 4.6 convolution_convert_fusion.1
  116.9 1.4 copy-done.19
  118.3 1.1 dynamic-slice_bitcast_fusion.1
  119.4 1.0 collective-permute-start
  121.3 1.1 iota_compare_fusion
  122.4 1.9 pad_maximum_fusion.21.refs_5_
  124.3 1.9 pad_maximum_fusion.20.refs_4_
  126.1 5.0 broadcast_select_fusion.1
  132.3 1.4 slice.302.w_own
  133.7 1.3 constant_dynamic-slice_fusion.4
  136.4 1.3 fusion.31
  138.3 1.3 copy.32
  139.6 1.3 copy.33
  140.9 1.5 bitcast_select_fusion.1
  142.4 1.6 pad_maximum_fusion.8.q_ref.k_ref.v_ref.refs_1_
  144.0 20.8 %attend.3 = (bf16[1024,384]{1,0:T(8,128)(2,1)}, f32[6,1,1024]{2,1,0:T(1,128)}) custom-call(s32[1]{0:T(128)} %bitcast.13.len_ref, f32[6,1,2048]{2,1,0:T(1,128)} %broadcast_in_dim.7.diag_ref, bf16[1024,1152]{1,0:T(8,128)(2,1)} %pad_maximum_fusion.8.q_ref.k_ref.v_ref.refs_1_, bf16[1024,1152]{1,0:T(8,128)(2,1)} %pad_maximum_fusion.8.q_ref.k_ref.v_ref.refs_1_, ...), custom_call_target="tpu_custom_call" | custom-call | flops 6442450944 | bytes 3145728 | tf_op jit(solution)/shard_map/attend/pallas_call | solution.py:85
  164.8 1.0 constant_dynamic-slice_fusion.3
  165.8 1.1 collective-permute-start.5
  166.9 1.5 bitcast_select_fusion.3
  168.4 1.6 pad_maximum_fusion.7.q_ref.k_ref.v_ref.refs_0_
  170.0 21.4 %attend.2 = (bf16[1024,384]{1,0:T(8,128)(2,1)}, f32[6,1,1024]{2,1,0:T(1,128)}) custom-call(s32[1]{0:T(128)} %bitcast.2.len_ref, f32[6,1,2048]{2,1,0:T(1,128)} %broadcast_in_dim.7.diag_ref, bf16[1024,1152]{1,0:T(8,128)(2,1)} %pad_maximum_fusion.7.q_ref.k_ref.v_ref.refs_0_, bf16[1024,1152]{1,0:T(8,128)(2,1)} %pad_maximum_fusion.7.q_ref.k_ref.v_ref.refs_0_, ...), custom_call_target="tpu_custom_call" | custom-call | flops 6442450944 | bytes 3145728 | tf_op jit(solution)/shard_map/attend/pallas_call | solution.py:85
  191.4 1.2 constant_dynamic-slice_fusion.5
  192.6 1.1 collective-permute-start.1
  194.1 3.1 pad_maximum_fusion.1
  197.2 6.1 collective-permute-done.1
  203.7 1.8 slice.379.w_other
  206.0 2.9 multiply_reduce_fusion
  209.0 2.9 multiply_reduce_fusion.1
  211.9 1.2 multiply_convert_fusion.1
  213.1 1.4 copy-done.3
  214.5 3.1 pad_maximum_fusion.refs_0_
  217.6 269.4 %feed.1 = (bf16[4,256,1536]{2,1,0:T(8,128)(2,1)}, bf16[4,256,1536]{2,1,0:T(8,128)(2,1)}, bf16[4,256,1536]{2,1,0:T(8,128)(2,1)}, bf16[4,256,1536]{2,1,0:T(8,128)(...) custom-call(bf16[2048,1536]{1,0:T(8,128)(2,1)} %pad_maximum_fusion.r, ...), custom_call_target="tpu_custom_call" | custom-call | flops 115964116992 | bytes 31457280 | tf_op jit(solution)/shard_map/feed/pallas_call | solution.py:792
  487.0 4.2 convert_element_type.104
  492.1 3.6 fusion.3
  496.3 1.9 pad_add_fusion.len_ref
  498.3 6.6 pad_maximum_fusion.3.refs_6_
  505.5 2.7 pad_maximum_fusion.9.refs_5_
  508.7 3.1 pad_maximum_fusion.2.resid_ref
  511.9 14.8 %resid_back.1 = (f32[4,256,1536]{2,1,0:T(8,128)}, bf16[4,256,1536]{2,1,0:T(8,128)(2,1)}, bf16[4,256,384]{2,1,0:T(8,128)(2,1)}, bf16[4,256,384]{2,1,0:T(8,128)(2,...) custom-call(bf16[4,256,1536]{2,1,0:T(8,128)(2,1)} %get-tuple-element.45.kept, ...), custom_call_target="tpu_custom_call" | custom-call | tf_op jit(solution)/shard_map/resid_back/pallas_call | solution.py:1213
  526.6 151.8 %mix_back.1 = (bf16[4,256,1152]{2,1,0:T(8,128)(2,1)}, bf16[4,256,1152]{2,1,0:T(8,128)(2,1)}, f32[6,1,2048]{2,1,0:T(1,128)}, f32[4,192,384]{2,1,0:T(8,128)}, bf16[4,256,1536]{2,1,0:T(8,128)(2,1)}) custom-call(s32[2]{0:T(128)} %pad_add_fusion.len_ref, f32[12,1,1024]{2,1,0:T(1,128)} %pad_maximum_fusion.31.lse_ref, f32[6,1,2048]{2,1,0:T(1,128)} %broadcast_in_dim.7.diag_ref, ...), custom_call_target="tpu_custom_call" | custom-call | tf_op jit(solution)/shard_map/mix_back/pallas_call | solution.py:1136
  678.4 1.3 convert_element_type.101
  679.7 1.4 collective-permute-start.7
  681.1 6.1 convert_add_fusion
  687.2 7.2 collective-permute-done.7
  695.3 1.0 fusion.33
  696.6 15.6 %input_back.1 = (f32[4,256,1536]{2,1,0:T(8,128)}, f32[1,1536]{1,0:T(1,128)}) custom-call(bf16[4,256,1152]{2,1,0:T(8,128)(2,1)} %get-tuple-element.55.own, bf16[4,256,1152]{2,1,0:T(8,128)(2,1)} %get-tuple-element.56.there, bf16[1536,1536]{1,0:T(8,128)(2,1)} %get-tuple-element.40.w_own, bf16[1536,1536]{1,0:T(8,128)(2,1)} %collective-permute-done.3.w_other, ...), custom_call_target="tpu_custom_call" | custom-call | tf_op jit(solution)/shard_map/input_back/pallas_call | solution.py:1246
  713.7 16.0 %small_sum.1 = f32[32,128]{1,0:T(8,128)} custom-call(f32[32,128]{1,0:T(8,128)} %fusion.44.x_ref), custom_call_target="tpu_custom_call" | custom-call | tf_op jit(solution)/shard_map/small_sum/pallas_call | solution.py:1284
  731.1 1.4 fusion.70
  732.6 0.9 maximum_bitcast_fusion.4
  733.6 0.9 pad_maximum_fusion.24
  735.4 0.9 pad_maximum_fusion.22
  736.2 2.7 slice_bitcast_fusion.7
  739.3 2.7 slice_bitcast_fusion.3
  744.0 1.8 maximum_bitcast_fusion
  745.9 1.8 pad_maximum_fusion.6
  748.5 1.8 pad_maximum_fusion.5
  (218 shorter events, 31.5 us)
Async XLA Ops:
  7.2 210.4 %all-gather.5.cloned.1.call-start = ((), (), s32[]{:S(2)}) async-start(), calls=%async_computation.1 | async-start | bytes 5308416 | tf_op jit(solution)/shard_map/all_gather | solution.py:1434
  8.4 2.2 copy-start.17
  8.4 2.2 slice-start.6
  12.5 2.8 copy-start.29
  12.7 3.2 copy-start.30
  12.7 3.9 copy-start.31
  13.5 7.4 copy-start.32
  14.4 203.2 %all-gather.3.cloned.1.call-start = ((), (), s32[]{:S(2)}) async-start(), calls=%async_computation | async-start | bytes 5308416 | tf_op jit(solution)/shard_map/all_gather | solution.py:1434
  21.7 78.5 %copy-start = (bf16[2,2,256,1536]{3,2,1,0:T(8,128)(2,1)S(1)}, bf16[2,2,256,1536]{3,2,1,0:T(8,128)(2,1)}, u32[]{:S(2)}) copy-start(bf16[2,2,256,1536]{3,2,1,0:T(8,128)(2,1)} %tokens.1) | copy-start | bytes 9437188
  97.8 105.9 %collective-permute-start.3 = (bf16[1536,1536]{1,0:T(8,128)(2,1)}, bf16[1536,1536]{1,0:T(8,128)(2,1)}, u32[]{:S(2)}, u32[]{:S(2)}) collective-permute-start(bf16[1536,1536]{1,0:T(8,128)(2,1)} %get-tuple-element.40.w_own), channel_id=1, source_target_pairs={{0,1},{1,0},{2,3},{3,2},{4,5},{5,4},{6,7},{7,6},{8,9},{9,8},{10,11... | collective-permute-start | bytes 14155784 | tf_op jit(solution)/shard_map/ppermute | solution.py:1382
  99.5 3.1 copy-start.34
  100.1 4.7 slice-start.4
  102.6 2.2 slice-start.5
  102.6 2.2 copy-start.38
  104.1 5.3 copy-start.7
  104.1 8.1 %copy-start.4 = (bf16[1,2,512,1536]{3,2,1,0:T(8,128)(2,1)}, bf16[1,2,512,1536]{3,2,1,0:T(8,128)(2,1)S(1)}, u32[]{:S(2)}) copy-start(bf16[1,2,512,1536]{3,2,1,0:T(8,128)(2,1)S(1)} %get-tuple-element.65) | copy-start | bytes 9437188
  109.4 7.4 copy-start.21
  110.7 30.2 %collective-permute-start.4 = (bf16[512,1152]{1,0:T(8,128)(2,1)}, bf16[512,1152]{1,0:T(8,128)(2,1)}, u32[]{:S(2)}, u32[]{:S(2)}) collective-permute-start(bf16[512,1152]{1,0:T(8,128)(2,1)} %dynamic-slice_bitcast_fusion), channel_id=1, source_target_pairs={{0,2},{1,3},{2,0},{3,1},{4,6},{5,7},{6,4},{7,5},{8,10},{9,11},{10,... | collective-permute-start | bytes 3538952 | tf_op jit(solution)/shard_map/ppermute | solution.py:1459
  118.3 3.0 copy-start.44
  119.4 6.8 copy-start.1
  119.4 47.5 %collective-permute-start = (bf16[512,1152]{1,0:T(8,128)(2,1)}, bf16[512,1152]{1,0:T(8,128)(2,1)}, u32[]{:S(2)}, u32[]{:S(2)}) collective-permute-start(bf16[512,1152]{1,0:T(8,128)(2,1)} %dynamic-slice_bitcast_fusion.1), channel_id=1, source_target_pairs={{0,2},{1,3},{2,0},{3,1},{4,6},{5,7},{6,4},{7,5},{8,10},{9,11},{10,... | collective-permute-start | bytes 3538952 | tf_op jit(solution)/shard_map/ppermute | solution.py:1459
  126.1 5.0 copy-start.47
  131.1 5.1 copy-start.36
  131.1 9.7 %copy-start.22 = (bf16[2,512,1152]{2,1,0:T(8,128)(2,1)S(1)}, bf16[2,512,1152]{2,1,0:T(8,128)(2,1)}, u32[]{:S(2)}) copy-start(bf16[2,512,1152]{2,1,0:T(8,128)(2,1)} %copy-done.21) | copy-start | bytes 7077892
  132.2 2.8 copy-start.50
  132.2 3.4 copy-start.45
  133.7 75.3 %copy-start.13 = (bf16[1536,384]{1,0:T(8,128)(2,1)}, bf16[1536,384]{1,0:T(8,128)(2,1)S(1)}, u32[]{:S(2)}) copy-start(bf16[1536,384]{1,0:T(8,128)(2,1)S(1)} %slice.302.w_own) | copy-start | bytes 3538948
  144.0 22.9 %copy-start.20 = (bf16[2,512,1152]{2,1,0:T(8,128)(2,1)S(1)}, bf16[2,512,1152]{2,1,0:T(8,128)(2,1)}, u32[]{:S(2)}) copy-start(bf16[2,512,1152]{2,1,0:T(8,128)(2,1)} %copy-done.19) | copy-start | bytes 7077892
  165.8 27.8 %collective-permute-start.5 = (bf16[512,384]{1,0:T(8,128)(2,1)S(1)}, bf16[512,384]{1,0:T(8,128)(2,1)S(1)}, u32[]{:S(2)}, u32[]{:S(2)}) collective-permute-start(bf16[512,384]{1,0:T(8,128)(2,1)S(1)} %constant_dynamic-slice_fusion.3), channel_id=1, source_target_pairs={{0,2},{1,3},{2,0},{3,1},{4,6},{5,7},{6,4},{7,5},{8,10},{9,11},{10,... | collective-permute-start | bytes 1179656 | tf_op jit(solution)/shard_map/ppermute | solution.py:1475
  170.0 23.7 %copy-start.27 = (bf16[1024,384]{1,0:T(8,128)(2,1)S(1)}, bf16[1024,384]{1,0:T(8,128)(2,1)}, u32[]{:S(2)}) copy-start(bf16[1024,384]{1,0:T(8,128)(2,1)} %get-tuple-element.42) | copy-start | bytes 2359300
  170.0 24.1 %copy-start.11 = (bf16[2,2,256,1536]{3,2,1,0:T(8,128)(2,1)S(1)}, bf16[2,2,256,1536]{3,2,1,0:T(8,128)(2,1)}, u32[]{:S(2)}) copy-start(bf16[2,2,256,1536]{3,2,1,0:T(8,128)(2,1)} %get-tuple-element.69) | copy-start | bytes 9437188
  191.4 2.7 copy-start.10
  192.6 10.7 %collective-permute-start.1 = (bf16[512,384]{1,0:T(8,128)(2,1)S(1)}, bf16[512,384]{1,0:T(8,128)(2,1)S(1)}, u32[]{:S(2)}, u32[]{:S(2)}) collective-permute-start(bf16[512,384]{1,0:T(8,128)(2,1)S(1)} %constant_dynamic-slice_fusion.5), channel_id=1, source_target_pairs={{0,2},{1,3},{2,0},{3,1},{4,6},{5,7},{6,4},{7,5},{8,10},{9,11},{10,... | collective-permute-start | bytes 1179656 | tf_op jit(solution)/shard_map/ppermute | solution.py:1475
  194.0 3.2 copy-start.15
  194.0 11.5 %collective-permute-start.6 = (bf16[2,512,384]{2,1,0:T(8,128)(2,1)S(1)}, bf16[2,512,384]{2,1,0:T(8,128)(2,1)S(1)}, u32[]{:S(2)}, u32[]{:S(2)}) collective-permute-start(bf16[2,512,384]{2,1,0:T(8,128)(2,1)S(1)} %pad_maximum_fusion.17), channel_id=1, source_target_pairs={{0,1},{1,0},{2,3},{3,2},{4,5},{5,4},{6,7},{7,6},{8,9},{9,8},{10,11... | collective-permute-start | bytes 2359304 | tf_op jit(solution)/shard_map/ppermute | solution.py:1382
  194.1 9.2 %copy-start.28 = (bf16[1024,384]{1,0:T(8,128)(2,1)S(1)}, bf16[1024,384]{1,0:T(8,128)(2,1)}, u32[]{:S(2)}) copy-start(bf16[1024,384]{1,0:T(8,128)(2,1)} %get-tuple-element.41) | copy-start | bytes 2359300
  203.5 2.5 copy-start.8
  203.6 5.3 copy-start.16
  203.6 5.3 collective-permute-start.2
  205.5 3.5 copy-start.14
  205.5 3.5 copy-start.5
  208.9 3.0 copy-start.2
  211.8 2.7 copy-start.3
  487.0 5.0 copy-start.6
  487.0 5.1 copy-start.9
  487.0 5.1 copy-start.39
  487.0 5.1 copy-start.42
  487.0 5.1 copy-start.43
  491.2 189.9 %collective-permute-start.9 = (bf16[4,192,1536]{2,1,0:T(8,128)(2,1)}, bf16[4,192,1536]{2,1,0:T(8,128)(2,1)}, u32[]{:S(2)}, u32[]{:S(2)}) collective-permute-start(bf16[4,192,1536]{2,1,0:T(8,128)(2,1)} %convert_element_type.104), channel_id=1, source_target_pairs={{0,2},{1,3},{2,0},{3,1},{4,6},{5,7},{6,4},{7,5},{8,10},{9,11},{10,... | collective-permute-start | bytes 7077896 | tf_op jit(solution)/shard_map/ppermute | solution.py:1567
  492.1 3.6 copy-start.37
  492.1 16.1 %slice-start.2 = ((s8[6291456]{0:T(1024)(128)(4,1)}), s8[2097152]{0:T(1024)(128)(4,1)S(1)}, s32[]{:S(2)}) async-start(s8[6291456]{0:T(1024)(128)(4,1)} %bitcast.159), calls=%async_computation.4 | async-start | bytes 4194304
  498.2 10.0 %slice-start = ((s8[6291456]{0:T(1024)(128)(4,1)}), s8[4194304]{0:T(1024)(128)(4,1)S(1)}, s32[]{:S(2)}) async-start(s8[6291456]{0:T(1024)(128)(4,1)} %bitcast.157), calls=%async_computation.2 | async-start | bytes 8388608
  498.3 6.6 copy-start.40
  498.3 6.6 copy-start.41
  498.3 10.0 %slice-start.1 = ((s8[6291456]{0:T(1024)(128)(4,1)}), s8[2097152]{0:T(1024)(128)(4,1)S(1)}, s32[]{:S(2)}) async-start(s8[6291456]{0:T(1024)(128)(4,1)} %bitcast.157), calls=%async_computation.3 | async-start | bytes 4194304
  498.3 10.0 %slice-start.3 = ((s8[6291456]{0:T(1024)(128)(4,1)}), s8[4194304]{0:T(1024)(128)(4,1)S(1)}, s32[]{:S(2)}) async-start(s8[6291456]{0:T(1024)(128)(4,1)} %bitcast.159), calls=%async_computation.5 | async-start | bytes 8388608
  679.7 14.7 %copy-start.12 = (f32[4,192,384]{2,1,0:T(8,128)S(1)}, f32[4,192,384]{2,1,0:T(8,128)}, u32[]{:S(2)}) copy-start(f32[4,192,384]{2,1,0:T(8,128)} %get-tuple-element.62) | copy-start | bytes 3538948
  679.7 14.7 %collective-permute-start.7 = (bf16[4,192,384]{2,1,0:T(8,128)(2,1)S(1)}, bf16[4,192,384]{2,1,0:T(8,128)(2,1)S(1)}, u32[]{:S(2)}, u32[]{:S(2)}) collective-permute-start(bf16[4,192,384]{2,1,0:T(8,128)(2,1)S(1)} %convert_element_type.101), channel_id=1, source_target_pairs={{0,2},{1,3},{2,0},{3,1},{4,6},{5,7},{6,4},{7,5},{8,10},{9,11},{10,... | collective-permute-start | bytes 1769480 | tf_op jit(solution)/shard_map/ppermute | solution.py:1567
  687.2 7.4 copy-start.35
  687.2 8.1 %copy-start.23 = (pred[2047,32]{1,0:T(8,128)(4,1)S(1)}, pred[2047,32]{1,0:T(8,128)(4,1)}, u32[]{:S(2)}) copy-start(pred[2047,32]{1,0:T(8,128)(4,1)} %iota_compare_fusion) | copy-start | bytes 196516
  687.2 8.1 %copy-start.33 = (f32[6,1,2048]{2,1,0:T(1,128)S(1)}, f32[6,1,2048]{2,1,0:T(1,128)}, u32[]{:S(2)}) copy-start(f32[6,1,2048]{2,1,0:T(1,128)} %get-tuple-element.61) | copy-start | bytes 147460
  687.2 52.0 %collective-permute-start.10 = (f32[4,192,1536]{2,1,0:T(8,128)}, f32[4,192,1536]{2,1,0:T(8,128)}, u32[]{:S(2)}, u32[]{:S(2)}) collective-permute-start(f32[4,192,1536]{2,1,0:T(8,128)} %convert_add_fusion), channel_id=1, source_target_pairs={{0,1},{1,0},{2,3},{3,2},{4,5},{5,4},{6,7},{7,6},{8,9},{9,8},{10,11... | collective-permute-start | bytes 14155784 | tf_op jit(solution)/shard_map/ppermute | solution.py:1382
  694.6 38.0 %collective-permute-start.8 = (f32[4,192,384]{2,1,0:T(8,128)S(1)}, f32[4,192,384]{2,1,0:T(8,128)S(1)}, u32[]{:S(2)}, u32[]{:S(2)}) collective-permute-start(f32[4,192,384]{2,1,0:T(8,128)S(1)} %convert_add_fusion.1), channel_id=1, source_target_pairs={{0,1},{1,0},{2,3},{3,2},{4,5},{5,4},{6,7},{7,6},{8,9},{9,8},{10,11... | collective-permute-start | bytes 3538952 | tf_op jit(solution)/shard_map/ppermute | solution.py:1382
  696.6 16.4 %copy-start.46 = (f32[1,1536]{1,0:T(1,128)S(1)}, f32[1,1536]{1,0:T(1,128)}, u32[]{:S(2)}) copy-start(f32[1,1536]{1,0:T(1,128)} %get-tuple-element.60) | copy-start | bytes 18436
  (9 other events, 17.5 us)
Sparse Core Ops, SparseCore 0:
  14.5 102.0 all-gather.4
  121.4 80.5 all-gather.2

commit v5 on v4

--- a/solution.py
+++ b/solution.py
@@ -285,18 +285,18 @@
 
 
 class Gather:
-    def __init__(self, links, shard, whole, sems, rows):
+    def __init__(self, links, shard, whole, sems, rows, share):
         self.links, self.shard, self.whole, self.sems, self.rows = links, shard, whole, sems, rows
         self.far = links.count // 2
         self.shared = links.planes == 2
-        self.third = rows // 3
-        self.size = 2 * self.third if self.shared else rows
+        self.share = share
+        self.size = rows - share if self.shared else rows
         self.cut = -(-(self.size // 2) // 16) * 16
 
     def base(self, shift):
         start = self.links.owner(shift) * self.rows
         if self.shared:
-            start = start + self.links.plane * self.third
+            start = start + self.links.plane * self.share
         return pl.multiple_of(start, 16)
 
     def ring_copy(self, step, forward):
@@ -307,7 +307,7 @@
         place = self.whole.at[pl.ds(pl.multiple_of(self.base(shift) + offset, 16), size)]
         source = place
         if step == 1:
-            first = self.links.plane * self.third if self.shared else 0
+            first = self.links.plane * self.share if self.shared else 0
             source = self.shard.at[pl.ds(pl.multiple_of(first + offset, 16), size)]
         return pltpu.make_async_remote_copy(
             src_ref=source,
@@ -335,8 +335,8 @@
 
     def across_copy(self, slot, shift, receive):
         plane = 1 - self.links.plane if receive else self.links.plane
-        start = self.links.owner(shift) * self.rows + plane * 2 * self.third
-        place = self.whole.at[pl.ds(pl.multiple_of(start, 16), self.third)]
+        start = self.links.owner(shift) * self.rows + plane * (self.rows - self.share)
+        place = self.whole.at[pl.ds(pl.multiple_of(start, 16), self.share)]
         return pltpu.make_async_remote_copy(
             src_ref=place,
             dst_ref=place,
@@ -378,17 +378,44 @@
                 self.across_copy(slot, shift, True).wait_recv()
 
 
-def gather_kernel(count, planes, rows, shard, small, tokens, cotangent, whole, smalls, tokens_there, cotangent_there, sems, sems_small, sems_core, own):
+def gather_kernel(
+    count, planes, rows, shard, small, tokens, cotangent,
+    whole, smalls, tokens_there, cotangent_there, items,
+    sems, sems_small, sems_core, own, item_sems,
+):
     links = Links(count, planes)
+    micro = tokens.shape[0]
+    split = planes == 2 and tokens.shape[1] == 2
+    plane, rank = links.plane, 2 * links.plane + links.core
     keep = pltpu.make_async_copy(shard, whole.at[pl.ds(pl.multiple_of(links.owner(0) * rows, 16), rows)], own.at[0])
     keep_small = pltpu.make_async_copy(small, smalls.at[pl.ds(pl.multiple_of(links.owner(0) * 16, 16), 16)], own.at[1])
-    keep.start()
-    keep_small.start()
+    starts = [keep, keep_small]
+    if split:
+        starts += [pltpu.make_async_copy(tokens.at[m, plane], items.at[m, rank], own.at[2 + m]) for m in range(micro)]
+    for copy in starts:
+        copy.start()
     links.greet()
-    large = Gather(links, shard, whole, sems, rows)
+    large = Gather(links, shard, whole, sems, rows, 16)
     little = SmallGather(links, small, smalls, sems_small)
     little.start()
     large.start()
+
+    def item_copy(kind, m):
+        source, place, device = (
+            (tokens.at[m, 1 - plane], rank, links.across),
+            (tokens.at[m, plane], rank, links.sibling),
+            (items.at[m, rank_across], rank_across, links.sibling),
+        )[kind]
+        return pltpu.make_async_remote_copy(
+            src_ref=source, dst_ref=items.at[m, place], send_sem=item_sems.at[kind, m, 0],
+            recv_sem=item_sems.at[kind, m, 1], device_id=device, device_id_type=MESH,
+        )
+
+    rank_across = 2 * (1 - plane) + links.core
+    if split:
+        for kind in range(2):
+            for m in range(micro):
+                item_copy(kind, m).start()
     swaps = []
     for at, (source, target) in enumerate(((tokens, tokens_there), (cotangent, cotangent_there))):
         swaps.append(
@@ -401,12 +428,21 @@
     for step in range(1, large.far + 1):
         little.advance(step)
         large.advance(step)
+    if split:
+        for m in range(micro):
+            item_copy(0, m).wait_recv()
+            item_copy(2, m).start()
     for swap in swaps:
         swap.wait()
     little.finish()
     large.finish()
-    keep.wait()
-    keep_small.wait()
+    if split:
+        for m in range(micro):
+            item_copy(0, m).wait_send()
+            for kind in range(1, 3):
+                item_copy(kind, m).wait()
+    for copy in starts:
+        copy.wait()
 
 
 class SmallGather(Gather):
@@ -435,23 +471,21 @@
 
 def gather_first(shard, small, tokens, cotangent, count, planes):
     rows, cols = shard.shape
+    micro, _, local, depth = tokens.shape
     anywhere = pl.BlockSpec(memory_space=pl.ANY)
+    dma = pltpu.SemaphoreType.DMA
     return pl.pallas_call(
         functools.partial(gather_kernel, count, planes, rows),
         in_specs=[anywhere] * 4,
-        out_specs=[anywhere] * 4,
+        out_specs=[anywhere] * 5,
         out_shape=[
             jax.ShapeDtypeStruct((count * rows, cols), shard.dtype),
             jax.ShapeDtypeStruct((count * 16, small.shape[1]), small.dtype),
             jax.ShapeDtypeStruct(tokens.shape, tokens.dtype),
             jax.ShapeDtypeStruct(cotangent.shape, cotangent.dtype),
+            jax.ShapeDtypeStruct((micro, 2 * planes, local, depth), tokens.dtype),
         ],
-        scratch_shapes=[
-            pltpu.SemaphoreType.DMA((6, count)),
-            pltpu.SemaphoreType.DMA((4, count)),
-            pltpu.SemaphoreType.DMA((2, 2)),
-            pltpu.SemaphoreType.DMA((2,)),
-        ],
+        scratch_shapes=[dma((6, count)), dma((4, count)), dma((2, 2)), dma((2 + micro,)), dma((3, micro, 2))],
         compiler_params=pltpu.CompilerParams(collective_id=0, has_side_effects=True),
         name="gather_first",
     )(shard, small, tokens, cotangent)
@@ -463,6 +497,7 @@
         self.mine, self.came, self.made, self.total = mine, came, made, total
         self.send_sems, self.recv_sems, self.near_sems, self.total_sems = send_sems, recv_sems, near_sems, total_sems
         self.rows = rows
+        self.base = 0
         self.far = links.count // 2
         self.cut = -(-(rows // 2) // 16) * 16
         self.spaces = made.shape[0]
@@ -474,7 +509,7 @@
 
     def term(self, chunk, shift, offset, size):
         start = self.links.owner(shift) * self.rows + offset
-        return self.grads.at[chunk, pl.ds(pl.multiple_of(start, 16), size)]
+        return self.grads.at[chunk + self.base, pl.ds(pl.multiple_of(start, 16), size)]
 
     def hop(self, chunk, step, way):
         offset, size = self.part(step, way)
@@ -549,14 +584,15 @@
             self.total_copy(chunk - 1).wait()
 
         total = self.mine[space, 0].astype(jnp.float32) + self.came[space, 0].astype(jnp.float32)
-        self.total[...] = total + self.came[space, 1].astype(jnp.float32)
+        self.total[...] = (total + self.came[space, 1].astype(jnp.float32)).astype(self.total.dtype)
         self.total_copy(chunk).start()
 
 
 def feed_kernel(plan, *refs):
-    count, planes, rows, chunks, early, tile, block, groups = plan
+    count, planes, rows, chunks, early, inside, micro, tile, block, groups = plan
     late = chunks - early
-    (normed, down, *rest) = refs
+    normed = refs[:micro]
+    (down, *rest) = refs[micro:]
     ready, shards = rest[:early], rest[early:chunks]
     rest = rest[chunks:]
     back_kept, back_got, out_kept, out_got, totals, pieces, grads, inbox = rest[:8]
@@ -574,7 +610,10 @@
     links = Links(count, planes)
     far = count // 2
 
-    loads = [pltpu.make_async_copy(normed, a_all, in_sems.at[chunks]), pltpu.make_async_copy(down, b_all, in_sems.at[chunks + 1])]
+    loads = [pltpu.make_async_copy(down, b_all, in_sems.at[chunks])]
+    for m in range(micro):
+        share = tokens // micro
+        loads.append(pltpu.make_async_copy(normed[m], a_all.at[pl.ds(m * share, share)], in_sems.at[chunks + 1 + m]))
     loads += [pltpu.make_async_copy(ready[n], weights.at[n], in_sems.at[n]) for n in range(early)]
     keeps = []
     for n in range(late):
@@ -583,12 +622,12 @@
     for copy in loads + keeps:
         copy.start()
     links.greet()
-    gathers = [Gather(links, shards[n], wholes[n], gather_sems[n], rows) for n in range(late)]
+    gathers = [Gather(links, shards[n], wholes[n], gather_sems[n], rows, rows // 3) for n in range(late)]
     scatter = Scatter(
         links, grads, inbox, totals, mine, came, made, total, send_sems, recv_sems, near_sems, total_sems, rows
     )
-    loads[0].wait()
-    loads[1].wait()
+    for copy in loads[: 1 + micro]:
+        copy.wait()
 
     gap_gather = max(1, 16 // far)
     gap = max(2, 20 // far)
@@ -628,7 +667,7 @@
         return pltpu.make_async_copy(out_stage.at[kind, 1], target.at[g], keep_sems.at[kind])
 
     items_back = 4 * groups
-    last_event = front + 1 + gap * far
+    last_event = per * inside + 1 + gap * far
     total_items = max(front + items_back, last_event + 1)
 
     def item(i, carry):
@@ -652,7 +691,7 @@
         def event(offset, act):
             past = i - per - offset
 
-            @pl.when((past >= 0) & (past < front) & (lax.rem(past + per * 64, per) == 0))
+            @pl.when((past >= 0) & (past < inside * per) & (lax.rem(past + per * 64, per) == 0))
             def _():
                 act(past // per)
 
@@ -712,6 +751,9 @@
 
         @pl.when(i == front)
         def _():
+            if inside < chunks:
+                for b in (blocks - 2, blocks - 1):
+                    stage_copy(chunks - 1, b).wait()
             for t in range(tiles):
                 piece_copy(chunks - 1, t).wait()
             for m in range(chunks):
@@ -761,7 +803,7 @@
         return carry
 
     lax.fori_loop(0, total_items, item, 0)
-    scatter.total_copy(chunks - 1).wait()
+    scatter.total_copy(inside - 1).wait()
     for kind in range(2):
         give_copy(kind, groups - 1).wait_send()
         keep_copy(kind, groups - 1).wait()
@@ -769,20 +811,21 @@
             give_copy(kind, g).wait_recv()
 
 
-def feed(normed, down, ready, shards, count, planes, tile):
-    tokens, depth = normed.shape
+def feed(normed, down, ready, shards, count, planes, tile, inside):
+    tokens, depth = down.shape
+    micro = len(normed)
     rows, cols = shards[0].shape
     early, chunks = len(ready), len(ready) + len(shards)
     far = count // 2
     block = 384
     groups = tokens // (2 * tile)
     spaces = 2 if far <= 4 else chunks
-    plan = (count, planes, rows, chunks, early, tile, block, groups)
+    plan = (count, planes, rows, chunks, early, inside, micro, tile, block, groups)
     anywhere = pl.BlockSpec(memory_space=pl.ANY)
-    low, wide = jnp.bfloat16, jnp.float32
+    low = jnp.bfloat16
     part = jax.ShapeDtypeStruct((groups, tile, depth), low)
     shapes = [part] * 4 + [
-        jax.ShapeDtypeStruct((chunks, rows, cols), wide),
+        jax.ShapeDtypeStruct((inside, rows, cols), low),
         jax.ShapeDtypeStruct((chunks, tokens, cols), low),
         jax.ShapeDtypeStruct((chunks, depth, cols), low),
         jax.ShapeDtypeStruct((chunks, 2, far, rows, cols), low),
@@ -791,7 +834,7 @@
     dma = pltpu.SemaphoreType.DMA
     made = pl.pallas_call(
         functools.partial(feed_kernel, plan),
-        in_specs=[anywhere] * (2 + chunks),
+        in_specs=[anywhere] * (1 + micro + chunks),
         out_specs=[anywhere] * len(shapes),
         out_shape=shapes,
         scratch_shapes=[
@@ -803,9 +846,9 @@
             pltpu.VMEM((spaces, 2, rows, cols), low),
             pltpu.VMEM((spaces, 2, rows, cols), low),
             pltpu.VMEM((spaces, 2, rows, cols), low),
-            pltpu.VMEM((rows, cols), wide),
+            pltpu.VMEM((rows, cols), low),
             pltpu.VMEM((2, 2, tile, depth), low),
-            dma((chunks + 2,)),
+            dma((chunks + 1 + micro,)),
             dma((tokens // tile,)),
             dma((2,)),
             dma((2, chunks)),
@@ -826,20 +869,251 @@
             flops=18 * tokens * depth * cols // 3 * chunks, bytes_accessed=10 * tokens * depth, transcendentals=0
         ),
         name="feed",
-    )(normed, down, *ready, *shards)
-    return made[:5]
+    )(*normed, down, *ready, *shards)
+    return (*made[:5], made[6])
+
+
+def mix_ahead_kernel(
+    plan, len_ref, diag_ref, made, shard, shard_2, mixes, there, lse_ref, whole, whole_2,
+    qkv_v, mix_v, strip, keys, in_sems, mix_sems, own_sems, gather_sems, gather_sems_2,
+):
+    count, planes, rows, head_dim, block = plan
+    micro, seq_len, cols = made.shape
+    pairs = cols // (3 * LANES)
+    plane_len = seq_len // 2
+    span = diag_ref.shape[-1]
+    per, wide, steps = LANES // head_dim, 3 * LANES, seq_len // block
+    units = micro * pairs
+    links = Links(count, planes)
+    plane = links.plane
+    far = count // 2
+    lanes_k = lax.broadcasted_iota(jnp.int32, (seq_len, LANES), 1)
+    lanes_q = lax.broadcasted_iota(jnp.int32, (block, LANES), 1)
+
+    def at_rows(start, size):
+        return pl.ds(pl.multiple_of(start, 16), size)
+
+    def unit_load(u):
+        p, m = u // micro, lax.rem(u, micro)
+        source = made.at[m, :, pl.ds(pl.multiple_of(p * wide, LANES), wide)]
+        return pltpu.make_async_copy(source, qkv_v.at[lax.rem(u, 2)], in_sems.at[lax.rem(u, 2)])
+
+    def columns(p):
+        return pl.ds(pl.multiple_of(p * LANES, LANES), LANES)
+
+    def mix_copies(u):
+        p, m, slot = u // micro, lax.rem(u, micro), lax.rem(u, 2)
+        mine = mix_v.at[slot, at_rows(plane * plane_len, plane_len)]
+        near = pltpu.make_async_copy(mine, mixes.at[m, plane, :, columns(p)], mix_sems.at[0, slot])
+        beside = pltpu.make_async_remote_copy(
+            src_ref=mine, dst_ref=there.at[m, plane, :, columns(p)], send_sem=mix_sems.at[1, slot],
+            recv_sem=mix_sems.at[2, u], device_id=links.sibling, device_id_type=MESH,
+        )
+        far_away = pltpu.make_async_remote_copy(
+            src_ref=mix_v.at[slot, at_rows((1 - plane) * plane_len, plane_len)],
+            dst_ref=mixes.at[m, plane, :, columns(p)], send_sem=mix_sems.at[3, slot],
+            recv_sem=mix_sems.at[4, u], device_id=links.across, device_id_type=MESH,
+        )
+        return near, beside, far_away
+
+    def forward_copy(u):
+        p, m = u // micro, lax.rem(u, micro)
+        return pltpu.make_async_remote_copy(
+            src_ref=mixes.at[m, 1 - plane, :, columns(p)], dst_ref=there.at[m, 1 - plane, :, columns(p)],
+            send_sem=mix_sems.at[5, u], recv_sem=mix_sems.at[6, u], device_id=links.sibling, device_id_type=MESH,
+        )
+
+    def forward(u):
+        p, m = u // micro, lax.rem(u, micro)
+        arrived = pltpu.make_async_remote_copy(
+            src_ref=mixes.at[m, 1 - plane, :, columns(p)], dst_ref=mixes.at[m, 1 - plane, :, columns(p)],
+            send_sem=mix_sems.at[3, 0], recv_sem=mix_sems.at[4, u], device_id=links.across, device_id_type=MESH,
+        )
+        arrived.wait_recv()
+        forward_copy(u).start()
+
+    pairs_of = ((shard, whole, gather_sems), (shard_2, whole_2, gather_sems_2))
+    keeps = [
+        pltpu.make_async_copy(source, target.at[at_rows(links.owner(0) * rows, rows)], own_sems.at[k])
+        for k, (source, target, _) in enumerate(pairs_of)
+    ]
+    for keep in keeps:
+        keep.start()
+    unit_load(jnp.int32(0)).start()
+    links.greet()
+    gathers = [Gather(links, source, target, sems, rows, rows // 4) for source, target, sems in pairs_of]
+    gathers[0].start()
+    spacing = units * steps // (2 * far)
+
+    def item(i, carry):
+        u, b = i // steps, lax.rem(i, steps)
+        p, m, slot = u // micro, lax.rem(u, micro), lax.rem(u, 2)
+
+        for step in range(1, 2 * far):
+
+            @pl.when(i == step * spacing)
+            def _(step=step):
+                if step <= far:
+                    gathers[0].advance(step)
+                if step == far - 1:
+                    gathers[1].start()
+                if step > far:
+                    gathers[1].advance(step - far)
+
+        @pl.when(b == 0)
+        def _():
+            unit_load(u).wait()
+
+            @pl.when(u + 1 < units)
+            def _():
+                unit_load(u + 1).start()
+
+            @pl.when(u >= 2)
+            def _():
+                near, beside, far_away = mix_copies(u - 2)
+                near.wait()
+                beside.wait_send()
+                far_away.wait_send()
+                forward(u - 2)
+
+            @pl.when(m == 0)
+            def _():
+                for head in range(per):
+                    strip[head] = toeplitz_strip(diag_ref[p * per + head], span)
+
+            length = len_ref[m]
+            for head in range(per):
+                here = lanes_k // head_dim == head
+                spare = ((head + 1) % per) * head_dim
+                keys[head] = with_mask_lane(qkv_v[slot, :, LANES : 2 * LANES], lanes_k, here, spare, length)
+
+        place = at_rows(b * block, block)
+        q_now = qkv_v[slot, place, :LANES]
+        mixed = None
+        for head in range(per):
+            here = lanes_q // head_dim == head
+            spare = ((head + 1) % per) * head_dim
+            query = jnp.where(here, q_now, (lanes_q == spare).astype(q_now.dtype))
+            raw = dot32(query, keys[head], NT)
+            parts = []
+            for sub in range(block // LANES):
+                offset = pl.multiple_of(seq_len - LANES - (b * block + sub * LANES), LANES)
+                parts.append(raw[sub * LANES : (sub + 1) * LANES] + strip[head, :, pl.ds(offset, seq_len)])
+            scores = jnp.concatenate(parts, axis=0)
+            top = jnp.max(scores, axis=1, keepdims=True)
+            expo = jnp.exp(scores - top)
+            total = jnp.sum(expo, axis=1, keepdims=True)
+            now = dot32(expo.astype(jnp.bfloat16), qkv_v[slot, :, 2 * LANES :], NN) / total
+            mixed = now if mixed is None else jnp.where(here, now, mixed)
+            lse = jnp.broadcast_to(top + jnp.log(total), (block, LANES))
+            at = m * pairs * per + p * per + head
+            lse_ref[at, :, pl.ds(pl.multiple_of(b * block, LANES), block)] = lse.T[:1]
+        mix_v[slot, place] = mixed.astype(mix_v.dtype)
+
+        @pl.when(b == steps - 1)
+        def _():
+            for copy in mix_copies(u):
+                copy.start()
+
+        return carry
+
+    lax.fori_loop(0, units * steps, item, 0)
+    for u in range(max(0, units - 2), units):
+        near, beside, far_away = mix_copies(jnp.int32(u))
+        near.wait()
+        beside.wait_send()
+        far_away.wait_send()
+        forward(jnp.int32(u))
+    gathers[1].advance(far)
+    for gather, keep in zip(gathers, keeps):
+        gather.finish()
+        keep.wait()
+    for u in range(units):
+        at = jnp.int32(u)
+        mix_copies(at)[1].wait_recv()
+        forward_copy(at).wait()
+
+
+def mix_ahead(made, diag, lengths, shards, rows_of, head_dim, count, planes, block=256):
+    micro, seq_len, cols = made.shape
+    pairs, per, span = cols // (3 * LANES), LANES // head_dim, diag.shape[-1]
+    plane_len, units = seq_len // 2, micro * pairs
+    rows, width = shards[0].shape
+    plan = (count, planes, rows, head_dim, block)
+    anywhere = pl.BlockSpec(memory_space=pl.ANY)
+    near = pl.BlockSpec(memory_space=pltpu.VMEM)
+    low, f32 = jnp.bfloat16, jnp.float32
+    dma = pltpu.SemaphoreType.DMA
+    return pl.pallas_call(
+        functools.partial(mix_ahead_kernel, plan),
+        in_specs=[pl.BlockSpec(memory_space=pltpu.SMEM), near, anywhere, anywhere, anywhere],
+        out_specs=[anywhere, anywhere, near, anywhere, anywhere],
+        out_shape=[
+            jax.ShapeDtypeStruct((micro, rows_of, plane_len, cols // 3), low),
+            jax.ShapeDtypeStruct((micro, rows_of, plane_len, cols // 3), low),
+            jax.ShapeDtypeStruct((units * per, 1, seq_len), f32),
+        ]
+        + [jax.ShapeDtypeStruct((count * rows, width), low)] * 2,
+        scratch_shapes=[
+            pltpu.VMEM((2, seq_len, 3 * LANES), low),
+            pltpu.VMEM((2, seq_len, LANES), low),
+            pltpu.VMEM((per, LANES, span), f32),
+            pltpu.VMEM((per, seq_len, LANES), low),
+            dma((2,)),
+            dma((7, units)),
+            dma((2,)),
+            dma((6, count)),
+            dma((6, count)),
+        ],
+        compiler_params=pltpu.CompilerParams(
+            collective_id=4, has_side_effects=True, vmem_limit_bytes=VMEM_LIMIT
+        ),
+        name="mix_ahead",
+    )(lengths, diag, made, *shards)
+
+
+def resid_ahead_kernel(core_ref, own, there, w_own, w_other, tokens, tokens_there, gain, resid_ref, normed_ref):
+    resid = jnp.where(pl.program_id(1) == 1, tokens[...], tokens_there[...]).astype(jnp.float32)
+    resid = resid + (dot32(own[...], w_own[...], NT) + dot32(there[...], w_other[...], NT))
+    root = lax.rsqrt(jnp.mean(resid * resid, axis=-1, keepdims=True) + eps)
+    resid_ref[...] = resid
+    normed_ref[...] = (resid * root * gain[...]).astype(normed_ref.dtype)
+
+
+def resid_ahead(mixes, there, w_own, w_other, tokens, tokens_there, gain, core_at):
+    groups, tile, depth = tokens.shape
+    cols, pair_len = mixes.shape[2], 2 * tile
+    mine = pl.BlockSpec((None, tile, depth), lambda g, h, s: (g, 0, 0))
+    tall = lambda width: pl.BlockSpec((None, tile, width), lambda g, h, s: (g, lax.rem(s[0] + 1 + h, 2), 0))
+    flat = lambda shape: pl.BlockSpec(shape, lambda g, h, s: (0, 0))
+    last = pl.BlockSpec((depth, cols), lambda g, h, s: (0, 3))
+    return pl.pallas_call(
+        resid_ahead_kernel,
+        grid_spec=pltpu.PrefetchScalarGridSpec(
+            num_scalar_prefetch=1,
+            grid=(groups, 2),
+            in_specs=[tall(cols), tall(cols), last, last, mine, mine, flat((1, depth))],
+            out_specs=[mine, tall(depth)],
+        ),
+        out_shape=[
+            jax.ShapeDtypeStruct((groups, tile, depth), jnp.float32),
+            jax.ShapeDtypeStruct((groups, pair_len, depth), jnp.bfloat16),
+        ],
+        compiler_params=pltpu.CompilerParams(vmem_limit_bytes=VMEM_LIMIT),
+        name="resid_ahead",
+    )(core_at, mixes, there, w_own, w_other, tokens, tokens_there, gain)
 
 
 def mix_back_kernel(plan, len_ref, lse_ref, diag_ref, *refs):
     count, planes, rows, micro, rows_of, head_dim, block, pairs = plan
-    qkvs = refs[:micro]
-    made_own, made_other, attn_in, mixed, normed = refs[micro : micro + 5]
-    dqkv_own, dqkv_there, dd_ref, totals, attn_there = refs[micro + 5 : micro + 10]
+    qkvs, mixed, normed, made_own, made_other, attn_in, last_grads = refs[:7]
+    dqkv_own, dqkv_there, dd_ref, totals, attn_there, last_totals, last_inbox = refs[7:14]
     (
-        qkv_v, do_v, res, sums_v, attn_v, mixed_v, normed_v, grads, inbox,
+        qkv_v, do_v, sums_v, attn_v, mixed_v, normed_v, grads, inbox,
         strip, keys, acc_bias, acc_k, acc_v, mine, came, made, total,
-        load_sems, do_sems, res_sems, attn_sems, dqkv_sems, send_sems, recv_sems, near_sems, total_sems,
-    ) = refs[micro + 10 :]
+        load_sems, do_sems, attn_sems, dqkv_sems, send_sems, recv_sems, near_sems, total_sems,
+        mine_2, came_2, made_2, total_2, send_2, recv_2, near_2, total_sems_2,
+    ) = refs[14:]
     seq_len = do_v.shape[1]
     span = diag_ref.shape[-1]
     plane_len = seq_len // 2
@@ -901,7 +1175,7 @@
     def unit_loads(m, p, slot):
         return [
             pltpu.make_async_copy(
-                qkvs[m].at[:, pl.ds(pl.multiple_of((3 * p + part) * LANES, LANES), LANES)],
+                qkvs.at[m, :, pl.ds(pl.multiple_of((3 * p + part) * LANES, LANES), LANES)],
                 qkv_v.at[slot, part],
                 load_sems.at[slot, part],
             )
@@ -909,35 +1183,29 @@
         ]
 
     def start_unit(u):
-        p, slot = u // micro, lax.rem(u, 2)
-        for m in range(micro):
-
-            @pl.when(lax.rem(u, micro) == m)
-            def _(m=m):
-                for copy in unit_loads(m, p, slot):
-                    copy.start()
-
-    def res_far(u):
+        for copy in unit_loads(lax.rem(u, micro), u // micro, lax.rem(u, 2)):
+            copy.start()
+
+    def give_copies(u):
         p, m = u // micro, lax.rem(u, micro)
-        return pltpu.make_async_remote_copy(
-            src_ref=res.at[lax.rem(u, 2), at_rows((1 - plane) * plane_len, plane_len)],
-            dst_ref=sums_v.at[p, m * rows_of + plane],
-            send_sem=res_sems.at[0, lax.rem(u, 2)], recv_sem=res_sems.at[1, u],
-            device_id=links.across, device_id_type=MESH,
-        )
-
-    def dqkv_near(p, at):
-        return pltpu.make_async_copy(
-            sums_v.at[p, at, at_rows(core * local, local)], dqkv_own.at[at, :, pl.ds(p * wide, wide)], dqkv_sems.at[p, at, 0]
-        )
-
-    def dqkv_far(p, at):
-        return pltpu.make_async_remote_copy(
-            src_ref=sums_v.at[p, at, at_rows((1 - core) * local, local)],
-            dst_ref=dqkv_there.at[at, :, pl.ds(p * wide, wide)],
-            send_sem=dqkv_sems.at[p, at, 1], recv_sem=dqkv_sems.at[p, at, 2],
-            device_id=links.sibling, device_id_type=MESH,
-        )
+        at = m * rows_of + plane
+        target = lambda ref: ref.at[at, :, pl.ds(pl.multiple_of(p * wide, LANES), wide)]
+        source = lambda q, c: sums_v.at[p, m, at_rows((2 * q + c) * local, local)]
+        far = []
+        for way, (q, c, ref, device) in enumerate(
+            (
+                (plane, 1 - core, dqkv_there, links.sibling),
+                (1 - plane, core, dqkv_own, links.across),
+                (1 - plane, 1 - core, dqkv_there, links.diagonal),
+            )
+        ):
+            far.append(
+                pltpu.make_async_remote_copy(
+                    src_ref=source(q, c), dst_ref=target(ref), send_sem=dqkv_sems.at[u, way],
+                    recv_sem=dqkv_sems.at[u, 3 + way], device_id=device, device_id_type=MESH,
+                )
+            )
+        return far, pltpu.make_async_copy(source(plane, core), target(dqkv_own), dqkv_sems.at[u, 6])
 
     start_unit(jnp.int32(0))
     mixed_load.start()
@@ -953,6 +1221,15 @@
         links, grads, inbox, totals, mine, came, made, total, send_sems, recv_sems, near_sems, total_sems, rows
     )
 
+    last_scatter = Scatter(
+        links, last_grads, last_inbox, last_totals, mine_2, came_2, made_2, total_2, send_2, recv_2, near_2,
+        total_sems_2, last_totals.shape[1],
+    )
+    last_scatter.base = last_grads.shape[0] - 1
+    last_gap = max(2, 20 // far)
+    zero = jnp.int32(0)
+    last_scatter.start(zero)
+
     def weight_grads(group, left, right):
         for at in range(left.shape[1] // 384):
             place = slice(at * 384, (at + 1) * 384)
@@ -969,18 +1246,13 @@
     def grads_pair(p):
         if p == 0:
             normed_load.wait()
-        for m in range(micro):
-            res_far(jnp.int32(p * micro + m)).wait_recv()
-        for at in range(micro * rows_of):
-            dqkv_near(p, at).start()
-            dqkv_far(p, at).start()
-        right = sums_v[p].reshape(micro * rows_of * plane_len, wide)
+        right = sums_v[p].reshape(micro * seq_len, wide)
         weight_grads(1 + p, normed_v, right)
 
     per_pair = micro * steps
     work = pairs * per_pair
-    begins = [4] + [per_pair * (p + 1) + 3 for p in range(pairs - 1)] + [work + 2]
-    gap = max(1, 8 // far)
+    begins = [4] + [per_pair * (p + 1) for p in range(pairs)]
+    gap = 1
     last = begins[-1] + 2 * far * gap
 
     def item(i, carry):
@@ -993,6 +1265,19 @@
             attn_far().wait_recv()
             for copy in attn_loads():
                 copy.start()
+
+        for step in range(1, far + 1):
+
+            @pl.when(i == step * last_gap - 1)
+            def _(step=step):
+                last_scatter.fetch(zero, step)
+
+            @pl.when(i == step * last_gap)
+            def _(step=step):
+                if step < far:
+                    last_scatter.pass_on(zero, step)
+                else:
+                    last_scatter.close(zero)
 
         for group, begin in enumerate(begins):
             g = jnp.int32(group)
@@ -1016,7 +1301,7 @@
 
         @pl.when((i < work) & (b == 0))
         def _():
-            for copy in unit_loads(0, p, slot):
+            for copy in unit_loads(m, p, slot):
                 copy.wait()
 
             @pl.when(u + 1 < units)
@@ -1031,10 +1316,6 @@
                     near_copy.wait()
                     for copy in far_copies:
                         copy.wait_recv()
-
-            @pl.when(u >= 2)
-            def _():
-                res_far(u - 2).wait_send()
 
             @pl.when(m == 0)
             def _():
@@ -1059,10 +1340,10 @@
             for head in range(per):
                 here = lanes_q // head_dim == head
                 spare = ((head + 1) % per) * head_dim
-                zero = jnp.zeros_like(q_now)
+                blank = jnp.zeros_like(q_now)
                 one = (lanes_q == spare).astype(q_now.dtype)
-                query = jnp.where(here, q_now, zero)
-                grad = jnp.where(here, do_now, zero)
+                query = jnp.where(here, q_now, blank)
+                grad = jnp.where(here, do_now, blank)
                 raw = dot32(keys[head], query + one, NT)
                 grad_probs = dot32(qkv_v[slot, 2], grad, NT)
                 parts, offsets = [], []
@@ -1083,14 +1364,16 @@
                 acc_k[...] += dot32(rounded, query, NN)
                 made_now = dot32(rounded, qkv_v[slot, 1], TN)
                 grad_query = made_now if grad_query is None else jnp.where(here, made_now, grad_query)
-            res[slot, place, :LANES] = grad_query.astype(res.dtype)
+            sums_v[p, m, place, :LANES] = grad_query.astype(sums_v.dtype)
 
         @pl.when((i < work) & (b == steps - 1))
         def _():
-            res[slot, :, LANES : 2 * LANES] = acc_k[...].astype(res.dtype)
-            res[slot, :, 2 * LANES :] = acc_v[...].astype(res.dtype)
-            res_far(u).start()
-            sums_v[p, m * rows_of + plane] = res[slot, at_rows(plane * plane_len, plane_len)]
+            sums_v[p, m, :, LANES : 2 * LANES] = acc_k[...].astype(sums_v.dtype)
+            sums_v[p, m, :, 2 * LANES :] = acc_v[...].astype(sums_v.dtype)
+            far_copies, near_copy = give_copies(u)
+            near_copy.start()
+            for copy in far_copies:
+                copy.start()
 
             @pl.when(m == micro - 1)
             def _():
@@ -1108,27 +1391,29 @@
 
     lax.fori_loop(0, last + 1, item, 0)
     scatter.total_copy(jnp.int32(pairs)).wait()
+    last_scatter.total_copy(zero).wait()
     for m in range(micro):
         for copy in do_copies(m)[0]:
             copy.wait_send()
     attn_far().wait_send()
-    for u in range(max(0, units - 2), units):
-        res_far(jnp.int32(u)).wait_send()
-    for p in range(pairs):
-        for at in range(micro * rows_of):
-            dqkv_near(p, at).wait()
-            dqkv_far(p, at).wait()
-
-
-def mix_back(qkvs, made_own, made_other, attn_in, mixed, normed, lse, diag, lengths, head_dim, count, planes, block=256):
-    micro = len(qkvs)
+    for u in range(units):
+        far_copies, near_copy = give_copies(jnp.int32(u))
+        near_copy.wait()
+        for copy in far_copies:
+            copy.wait()
+
+
+def mix_back(qkvs, made_own, made_other, attn_in, mixed, normed, last_grads, lse, diag, lengths, head_dim, count, planes, block=256):
+    micro, seq_len, cols = qkvs.shape
+    cols = cols // 3
     rows_of = attn_in.shape[0] // micro
     _, local, depth = attn_in.shape
-    seq_len, cols = qkvs[0].shape[0], qkvs[0].shape[1] // 3
     pairs, per, span = cols // LANES, LANES // head_dim, diag.shape[-1]
     tokens = normed.shape[0]
+    chunk_cols = last_grads.shape[2]
     rows, wide, far = depth // count, 3 * LANES, count // 2
     groups = 1 + pairs
+    spaces = 2 if far <= 4 else groups
     plan = (count, planes, rows, micro, rows_of, head_dim, block, pairs)
     anywhere = pl.BlockSpec(memory_space=pl.ANY)
     low, f32 = jnp.bfloat16, jnp.float32
@@ -1137,20 +1422,21 @@
         functools.partial(mix_back_kernel, plan),
         in_specs=[pl.BlockSpec(memory_space=pltpu.SMEM)]
         + [pl.BlockSpec(memory_space=pltpu.VMEM)] * 2
-        + [anywhere] * (micro + 5),
-        out_specs=[anywhere, anywhere, pl.BlockSpec(memory_space=pltpu.VMEM), anywhere, anywhere],
+        + [anywhere] * 7,
+        out_specs=[anywhere, anywhere, pl.BlockSpec(memory_space=pltpu.VMEM)] + [anywhere] * 4,
         out_shape=[
             jax.ShapeDtypeStruct((micro * rows_of, local, 3 * cols), low),
             jax.ShapeDtypeStruct((micro * rows_of, local, 3 * cols), low),
             jax.ShapeDtypeStruct(diag.shape, f32),
-            jax.ShapeDtypeStruct((groups, rows, wide), f32),
+            jax.ShapeDtypeStruct((groups, rows, wide), low),
             jax.ShapeDtypeStruct(attn_in.shape, low),
+            jax.ShapeDtypeStruct((1, rows, chunk_cols), low),
+            jax.ShapeDtypeStruct((1, 2, far, rows, chunk_cols), low),
         ],
         scratch_shapes=[
             pltpu.VMEM((2, 3, seq_len, LANES), low),
             pltpu.VMEM((micro, seq_len, cols), low),
-            pltpu.VMEM((2, seq_len, wide), low),
-            pltpu.VMEM((pairs, micro * rows_of, seq_len // 2, wide), low),
+            pltpu.VMEM((pairs, micro, seq_len, wide), low),
             pltpu.VMEM((tokens, depth), low),
             pltpu.VMEM((tokens, cols), low),
             pltpu.VMEM((tokens, depth), low),
@@ -1161,25 +1447,32 @@
             pltpu.VMEM((per, span, LANES), f32),
             pltpu.VMEM((seq_len, LANES), f32),
             pltpu.VMEM((seq_len, LANES), f32),
-            pltpu.VMEM((2, 2, rows, wide), low),
-            pltpu.VMEM((2, 2, rows, wide), low),
-            pltpu.VMEM((2, 2, rows, wide), low),
-            pltpu.VMEM((rows, wide), f32),
+            pltpu.VMEM((spaces, 2, rows, wide), low),
+            pltpu.VMEM((spaces, 2, rows, wide), low),
+            pltpu.VMEM((spaces, 2, rows, wide), low),
+            pltpu.VMEM((rows, wide), low),
             dma((2, 3)),
             dma((micro, 7)),
-            dma((2, pairs * micro)),
             dma((4 + 2 * micro * rows_of,)),
-            dma((pairs, micro * rows_of, 3)),
+            dma((pairs * micro, 7)),
             dma((groups, 2, far)),
             dma((groups, 2, far)),
-            dma((2, 2, 2)),
+            dma((spaces, 2, 2)),
+            dma((1,)),
+            pltpu.VMEM((1, 2, rows, chunk_cols), low),
+            pltpu.VMEM((1, 2, rows, chunk_cols), low),
+            pltpu.VMEM((1, 2, rows, chunk_cols), low),
+            pltpu.VMEM((rows, chunk_cols), low),
+            dma((1, 2, far)),
+            dma((1, 2, far)),
+            dma((1, 2, 2)),
             dma((1,)),
         ],
         compiler_params=pltpu.CompilerParams(
             collective_id=2, has_side_effects=True, vmem_limit_bytes=62 * 1024 * 1024
         ),
         name="mix_back",
-    )(lengths, lse, diag, *qkvs, made_own, made_other, attn_in, mixed, normed)
+    )(lengths, lse, diag, qkvs, mixed, normed, made_own, made_other, attn_in, last_grads)
 
 
 def resid_back_kernel(kept, got, out_kept, out_got, resid_ref, cot, gain, w_own, w_other, grad_ref, attn_ref, own_ref, other_ref, out_ref, sum_ref):
@@ -1205,7 +1498,7 @@
 
 def resid_back(kept, got, out_kept, out_got, resid, cotangent, gain, w_own, w_other):
     groups, tile, depth = kept.shape
-    cols = w_own.shape[1]
+    cols = w_own.shape[1] // 4
     tall = lambda width: pl.BlockSpec((None, tile, width), lambda g: (g, 0, 0))
     flat = lambda shape: pl.BlockSpec(shape, lambda g: (0, 0))
     low, wide = jnp.bfloat16, jnp.float32
@@ -1213,7 +1506,7 @@
     return pl.pallas_call(
         resid_back_kernel,
         grid=(groups,),
-        in_specs=[tall(depth)] * 6 + [flat((1, depth)), flat((depth, cols)), flat((depth, cols))],
+        in_specs=[tall(depth)] * 6 + [flat((1, depth))] + [pl.BlockSpec((depth, cols), lambda g: (0, 3))] * 2,
         out_specs=[tall(depth), tall(depth), tall(cols), tall(cols), tall(depth), flat((1, depth))],
         out_shape=[
             shape(depth, wide), shape(depth, low), shape(cols, low), shape(cols, low), shape(depth, low),
@@ -1413,27 +1706,16 @@
     small = jnp.concatenate([gain_one, gain_two, table.reshape(-1)])
     small = jnp.pad(small, (0, -small.shape[0] % LANES))
     small = jnp.pad(small[None], ((0, 15), (0, 0)))
-    attn_weights, small, tokens_other, cotangent_other = gather_first(
+    attn_weights, small, tokens_other, cotangent_other, items = gather_first(
         attn_shard, small, tokens, cotangent, dp_devices, planes
     )
     small = small.reshape(dp_devices, 16, -1)[:, 0].astype(jnp.float32)
     gain_first = small[:, :shard_rows].reshape(-1)
     gain_second = small[:, shard_rows : 2 * shard_rows].reshape(-1)
     full_table = small[:, 2 * shard_rows : 2 * shard_rows + table.size].reshape(-1, heads)
-    last = attn_weights
     qkv_cols = 3 * half_inner
     there_weights = swap_core(attn_weights)
     qkv_weights = attn_weights[:, :qkv_cols]
-    out_own, out_other = attn_weights[:, qkv_cols:], there_weights[:, qkv_cols:]
-    out_pair = jnp.concatenate([out_own, out_other], axis=1)
-
-    early = min(2, chunks - 1)
-    ready = []
-    for shard in chunk_shards[:early]:
-        shard, last = lax.optimization_barrier((shard, last))
-        ready.append(lax.all_gather(shard, "dp", axis=0, tiled=True))
-
-    tokens_pair = both_cores(tokens, tokens_other, 2)
     down_in = both_cores(cotangent, cotangent_other, 2)
 
     core_heads = heads // 2
@@ -1481,29 +1763,32 @@
         value = value.reshape(rows, head_splits, pair_local, parts, item_cols).transpose(0, 2, 3, 1, 4)
         return value.reshape(rows, pair_local, parts * half_inner)
 
-    normed, roots, qkvs, lses, mixes, resids, normed_twos, item_lens = [], [], [], [], [], [], [], []
-    for step in range(micro):
-        rows_in = tokens_pair[step].astype(jnp.float32)
-        root = lax.rsqrt(jnp.mean(rows_in * rows_in, axis=-1, keepdims=True) + eps)
-        roots.append(root)
-        normed.append((rows_in * root * gain_first).astype(jnp.bfloat16))
-    for step in range(micro):
-        made = jnp.einsum("rld,de->rle", normed[step], qkv_weights, preferred_element_type=jnp.float32)
-        qkvs.append(to_items(made.astype(jnp.bfloat16), 3))
-    for step in range(micro):
-        item_len = lax.dynamic_slice_in_dim(lengths[step], item_row, 1, 0)
-        item_lens.append(item_len)
-        mixed, lse = attend(qkvs[step], diag, item_len, head_dim, fused)
-        lses.append(lse)
-        mixed_own = from_items([mixed])
-        mixes.append(mixed_own)
-        mixed_pair = jnp.concatenate([mixed_own, swap_core(mixed_own)], axis=2)
-        resid = tokens_pair[step].astype(jnp.float32) + jnp.einsum(
-            "rle,de->rld", mixed_pair, out_pair, preferred_element_type=jnp.float32
+    rows_in = items.reshape(micro, 1, seq_len, width) if fused else both_cores(tokens, tokens_other, 2)
+    rows_in = rows_in.astype(jnp.float32)
+    root = lax.rsqrt(jnp.mean(rows_in * rows_in, axis=-1, keepdims=True) + eps)
+    normed = lax.optimization_barrier((rows_in * root * gain_first).astype(jnp.bfloat16))
+    made = jnp.einsum("mrld,de->mrle", normed, qkv_weights, preferred_element_type=jnp.float32).astype(jnp.bfloat16)
+    item_lens = lax.dynamic_slice_in_dim(lengths, item_row, 1, 1)
+    if fused:
+        qkvs = made[:, 0]
+        mixes, mixes_there, lses, *ready = mix_ahead(
+            qkvs, diag, item_lens[:, 0], chunk_shards[:2], rows, head_dim, dp_devices, planes
         )
-        root = lax.rsqrt(jnp.mean(resid * resid, axis=-1, keepdims=True) + eps)
-        normed_twos.append((resid * root * gain_second).astype(jnp.bfloat16))
-        resids.append(own_half(resid, 1))
+    else:
+        qkvs = [to_items(made[step], 3) for step in range(micro)]
+        pairs = [attend(qkvs[step], diag, item_lens[step], head_dim) for step in range(micro)]
+        lses = [lse for _, lse in pairs]
+        mixes = jnp.stack([from_items([mixed]) for mixed, _ in pairs])
+        mixes_there = swap_core(mixes)
+        ready = [lax.all_gather(shard, "dp", axis=0, tiled=True) for shard in chunk_shards[:2]]
+    early = 2
+    by_pair = lambda value: value.reshape(micro * rows, pair_local, value.shape[-1])
+    by_row = lambda value: value.reshape(micro * rows, local, value.shape[-1])
+    resids, normed_two = resid_ahead(
+        by_pair(mixes), by_pair(mixes_there), attn_weights, there_weights, by_row(tokens), by_row(tokens_other),
+        gain_second[None],
+        core.astype(jnp.int32)[None],
+    )
 
     def apart(qkvs, grads_items, lses, item_lens, attn_all, mixed_all, normed_all):
         grads_qkv, diag_sum = [], 0.0
@@ -1524,23 +1809,19 @@
         return grads_qkv, diag_sum, total
 
     flat = lambda value: value.reshape(-1, value.shape[-1])
-    normed_two_all = jnp.concatenate([flat(v) for v in normed_twos])
     down_all = flat(down_in)
-    back_kept, back_got, out_kept, out_got, chunk_totals = feed(
-        normed_two_all, down_all, ready, chunk_shards[early:], dp_devices, planes, local
+    inside = chunks - 1 if fused else chunks
+    back_kept, back_got, out_kept, out_got, chunk_totals, chunk_grads = feed(
+        [flat(normed_two)], down_all, ready, chunk_shards[early:], dp_devices, planes, local, inside
     )
-    by_row = lambda value: value.reshape(micro * rows, local, value.shape[-1])
     grad_resid, attn_in, made_own, made_other, output, gain_two_sum = resid_back(
-        back_kept, back_got, out_kept, out_got, jnp.concatenate(resids), by_row(cotangent), gain_second[None],
-        out_own, out_other,
+        back_kept, back_got, out_kept, out_got, resids, by_row(cotangent), gain_second[None], attn_weights, there_weights
     )
 
-    normed_all = jnp.concatenate([flat(v) for v in normed])
-    mixed_all = jnp.concatenate([flat(v) for v in mixes])
     if fused:
-        own, there, diag_sum, attn_totals, _ = mix_back(
-            qkvs, made_own, made_other, attn_in, mixed_all, normed_all, jnp.concatenate(lses), diag,
-            jnp.concatenate(item_lens), head_dim, dp_devices, planes,
+        own, there, diag_sum, attn_totals, _, last_totals, _ = mix_back(
+            qkvs, made_own, made_other, attn_in, flat(mixes), flat(normed), chunk_grads, lses, diag, item_lens[:, 0],
+            head_dim, dp_devices, planes,
         )
         input_grad, gain_one_sum = input_back(
             own, there, attn_weights, there_weights, by_row(tokens), grad_resid, gain_first[None]
@@ -1550,7 +1831,7 @@
         split_micro = lambda value: value.reshape(micro, rows, local, -1)
         grads_mixed = both_cores(split_micro(made_own), swap_core(split_micro(made_other)), 2)
         grads_qkv, diag_sum, attn_totals = apart(
-            qkvs, [to_items(g, 1) for g in grads_mixed], lses, item_lens, split_micro(attn_in), mixed_all, normed_all
+            qkvs, [to_items(g, 1) for g in grads_mixed], lses, item_lens, split_micro(attn_in), flat(mixes), flat(normed)
         )
         grads_qkv = jnp.stack(grads_qkv)
         own = by_row(own_half(grads_qkv, 2))
@@ -1567,7 +1848,7 @@
             got = lax.ppermute(low, "seq", [(i, i ^ 2) for i in range(4)])
             total = low.astype(jnp.float32) + got.astype(jnp.float32)
         else:
-            total = lax.psum(total, "seq", axis_index_groups=plane_groups)
+            total = lax.psum(total.astype(jnp.float32), "seq", axis_index_groups=plane_groups)
         return total, swap_core(total)
 
     def whole_columns(own, other, size):
@@ -1589,7 +1870,10 @@
         parts = [slice(i * half_inner, (i + 1) * half_inner) for i in range(4)]
         grad_out, grad_query, grad_key, grad_value = [whole_columns(own[:, p], other[:, p], inner) for p in parts]
     own, other = finish(chunk_totals)
-    done = [(own[n], other[n]) for n in range(chunks)]
+    done = [(own[n], other[n]) for n in range(inside)]
+    if fused:
+        own, other = finish(last_totals)
+        done.append((own[0], other[0]))
     parts = [slice(i * chunk, (i + 1) * chunk) for i in range(3)]
     grad_gate, grad_up, grad_down = [
         whole_columns(

time: 767 us -> 736 us (0.960)
  Pallas kernels: 586 us -> 657 us
  other arithmetic: 76.8 us -> 36.8 us
  local copies, waits for them, and re-layouts: 42.3 us -> 12.3 us
  between operations: 15.4 us -> 1.57 us
  waiting for transfers between devices: 13.4 us -> 4.57 us
    pallas_call x2, Pallas kernels: 42.2 us -> 106 us  [the longest x1 90.9 us: mix_ahead(): pl.pallas_call(functools.partial(mix_ahead_kernel, plan), in_specs=[pl.Bl...]
    pallas_call x1, Pallas kernels: 152 us -> 192 us  [mix_back(): pl.pallas_call(functools.partial(mix_back_kernel, plan), in_specs=[pl.Blo...]
    pallas_call x1, Pallas kernels: 269 us -> 244 us  [feed(): pl.pallas_call(functools.partial(feed_kernel, plan), in_specs=[anywhere]...]
    concatenate x8 -> x0, other arithmetic: 21.3 us -> none  [the longest x1 6.6 us: body(): normed_all = jnp.concatenate([flat(v) for v in normed])]
    unnamed x128 -> x57, local copies, waits for them, and re-layouts: 12.4 us -> 2.64 us
    pallas_call x1, Pallas kernels: 76.2 us -> 68 us  [gather_first(): pl.pallas_call(functools.partial(gather_kernel, count, planes, rows), in_...]
  transfers between devices with their start and end apart: 13 -> 7, of which waited for: 2 -> 1; matrix products, arithmetic and copies ran while one was open for 15% -> 7% of each run, Pallas kernels for 42% -> 45%
where the time goes in v5:
time: 736 us; the launch traced here: 731 us
  Pallas kernels  657 us (89%)
  other arithmetic  36.8 us (5%)
  matrix products  14.1 us (2%)
  local copies, waits for them, and re-layouts  12.3 us (2%)
    pallas_call x1, Pallas kernels, feed(): pl.pallas_call(functools.partial(feed_kernel, plan), in_specs=[anywhere]...  244 us
    pallas_call x1, Pallas kernels, mix_back(): pl.pallas_call(functools.partial(mix_back_kernel, plan), in_specs=[pl.Blo...  192 us
    pallas_call x1, Pallas kernels, mix_ahead(): pl.pallas_call(functools.partial(mix_ahead_kernel, plan), in_specs=[pl.Bl...  90.9 us
    pallas_call x1, Pallas kernels, gather_first(): pl.pallas_call(functools.partial(gather_kernel, count, planes, rows), in_...  68 us
    pallas_call x1, Pallas kernels, small_sum(): pl.pallas_call(functools.partial(small_sum_kernel, sizes), in_specs=[pl.B...  15.9 us
    pallas_call x1, Pallas kernels, input_back(): pl.pallas_call(input_back_kernel, grid=(groups,), in_specs=[tall(cols), t...  15.7 us
    pallas_call x1, Pallas kernels, resid_ahead(): pl.pallas_call(resid_ahead_kernel, grid_spec=pltpu.PrefetchScalarGridSpec...  15.3 us
    pallas_call x1, Pallas kernels, resid_back(): pl.pallas_call(resid_back_kernel, grid=(groups,), in_specs=[tall(depth)]...  14.8 us
  transfers between devices with their start and end apart: 7, of which 1 were waited for; matrix products, arithmetic and copies ran while one was open for 7% of the time, Pallas kernels for 45%

profile of v5, /device:TPU:0, one launch (start us, length us, event | category | flops | bytes accessed | tf_op | source)
XLA Modules:
  0.0 730.5 jit_solution(18006187141385201063)
XLA Ops:
  0.7 1.0 slice_select_fusion.7
  1.8 1.0 slice_select_fusion.6
  2.8 1.0 slice_select_fusion.5
  4.2 0.7 pad.30.small
  4.9 0.1 copy-done.10
  5.1 68.0 %gather_first.1 = (bf16[1536,1536]{1,0:T(8,128)(2,1)}, bf16[128,512]{1,0:T(8,128)(2,1)}, bf16[2,2,256,1536]{3,2,1,0:T(8,128)(2,1)}, bf16[2,2,256,1536]{3,2,1,0:T(8,128)(2,1)}, bf16[2,4,256,1536]{3,2,1,0:T(8,128)(2,1)}) custom-call(bf16[192,1536]{1,0:T(8,128)(2,1)} %copy-done.10, bf16[16,512]{1,0:T(8,128)(2,1)} %pad.30.small, ...), custom_call_target="tpu_custom_call" | custom-call | tf_op jit(solution)/shard_map/gather_first/pallas_call | solution.py:477
  73.1 0.5 collective-permute-start
  73.6 0.8 slice.340
  74.6 4.2 multiply_reduce_fusion
  78.9 0.3 copy-done.3
  79.2 4.2 fusion.1
  83.5 0.3 iota_compare_fusion
  83.9 0.3 fusion.9
  84.2 0.7 broadcast_in_dim.17.diag_ref
  84.9 0.2 slice_select_fusion.3
  85.3 1.3 copy-done.5
  86.5 0.3 slice-done.3
  86.9 0.2 pad_select_fusion.1
  87.1 0.7 broadcast_in_dim_reshape.8.gain
  87.8 0.7 dynamic-slice_reduce_fusion.len_ref
  88.5 0.6 copy-done.4
  89.2 0.2 pad_select_fusion
  89.4 0.9 pad_maximum_fusion.10.shard_2
  90.3 0.9 pad_maximum_fusion.9.shard
  91.2 12.0 %fusion.4.made.refs_0_ = bf16[2,1024,1152]{2,1,0:T(8,128)(2,1)} fusion(bf16[2,1,1024,1536]{3,2,0,1:T(8,128)(2,1)} %fusion.1, bf16[1536,1536]{1,0:T(8,128)(2,1)S(1)} %bitcast.102), kind=kOutput, calls=%fused_computation.7 | convolution fusion | flops 7250116608 | bytes 14548992 | tf_op jit(solution)/shard_map/mrld,de->mrle/dot_general | solution.py:1770
  103.1 90.9 %mix_ahead.1 = (bf16[2,2,512,384]{3,2,1,0:T(8,128)(2,1)}, bf16[2,2,512,384]{3,2,1,0:T(8,128)(2,1)}, f32[12,1,1024]{2,1,0:T(1,128)}, bf16[1536,1536]{1,0:T(8,128)(2,1)}, bf16[1536,1536]{1,0:T(8,128)(2,1)}) custom-call(s32[2]{0:T(128)} %dynamic-slice_reduce_fusion.len_ref, f32[6,1,2048]{2,1,0:T(1,128)} %broadcast_in_dim.17.diag_ref, ...), custom_call_target="tpu_custom_call" | custom-call | tf_op jit(solution)/shard_map/mix_ahead/pallas_call | solution.py:1047
  194.1 0.9 pad_maximum_fusion.11.refs_4_
  194.9 0.9 pad_maximum_fusion.12.refs_5_
  195.8 2.3 broadcast_select_fusion.1
  198.1 3.2 pad_maximum_fusion
  201.3 15.3 %resid_ahead.1 = (f32[4,256,1536]{2,1,0:T(8,128)}, bf16[4,512,1536]{2,1,0:T(8,128)(2,1)}) custom-call(s32[1]{0:T(128)} %bitcast.core_ref, bf16[4,512,384]{2,1,0:T(8,128)(2,1)} %bitcast.107, bf16[4,512,384]{2,1,0:T(8,128)(2,1)} %bitcast.111, bf16[1536,1536]{1,0:T(8,128)(2,1)} %get-tuple-element.45.w_own, bf16[1536,1536]{1,0:T(8,128)(2,1)} %collective-permute-done.w_other, ...), custom_call_target="tpu_custom_call" | custom-call | tf_op jit(solution)/shard_map/resid_ahead/pallas_call | solution.py:1090
  216.6 244.5 %feed.1 = (bf16[4,256,1536]{2,1,0:T(8,128)(2,1)}, bf16[4,256,1536]{2,1,0:T(8,128)(2,1)}, bf16[4,256,1536]{2,1,0:T(8,128)(2,1)}, bf16[4,256,1536]{2,1,0:T(8,128)(...) custom-call(bf16[2048,1536]{1,0:T(8,128)(2,1)} %bitcast.123, ...), custom_call_target="tpu_custom_call" | custom-call | flops 115964116992 | bytes 31457280 | tf_op jit(solution)/shard_map/feed/pallas_call | solution.py:835
  461.1 0.9 collective-permute-start.3
  462.0 14.8 %resid_back.1 = (f32[4,256,1536]{2,1,0:T(8,128)}, bf16[4,256,1536]{2,1,0:T(8,128)(2,1)}, bf16[4,256,384]{2,1,0:T(8,128)(2,1)}, bf16[4,256,384]{2,1,0:T(8,128)(2,...) custom-call(bf16[4,256,1536]{2,1,0:T(8,128)(2,1)} %get-tuple-element.53.kept, ...), custom_call_target="tpu_custom_call" | custom-call | tf_op jit(solution)/shard_map/resid_back/pallas_call | solution.py:1506
  476.8 191.8 %mix_back.1 = (bf16[4,256,1152]{2,1,0:T(8,128)(2,1)}, bf16[4,256,1152]{2,1,0:T(8,128)(2,1)}, f32[6,1,2048]{2,1,0:T(1,128)}, bf16[4,192,384]{2,1,0:T(8,128)(2,1)}...) custom-call(s32[2]{0:T(128)} %dynamic-slice_reduce_fusion.len_ref, ...), custom_call_target="tpu_custom_call" | custom-call | tf_op jit(solution)/shard_map/mix_back/pallas_call | solution.py:1421
  668.8 0.7 broadcast_in_dim_reshape.9.gain
  669.4 2.0 collective-permute-start.4
  671.4 1.8 fusion.11
  673.2 0.2 dynamic_update_slice.3
  673.6 15.7 %input_back.1 = (f32[4,256,1536]{2,1,0:T(8,128)}, f32[1,1536]{1,0:T(1,128)}) custom-call(bf16[4,256,1152]{2,1,0:T(8,128)(2,1)} %get-tuple-element.64.own, bf16[4,256,1152]{2,1,0:T(8,128)(2,1)} %get-tuple-element.65.there, bf16[1536,1536]{1,0:T(8,128)(2,1)} %get-tuple-element.45.w_own, bf16[1536,1536]{1,0:T(8,128)(2,1)} %collective-permute-done.w_other, ...), custom_call_target="tpu_custom_call" | custom-call | tf_op jit(solution)/shard_map/input_back/pallas_call | solution.py:1539
  689.3 0.8 reduce.2
  690.2 0.6 fusion.22.x_ref
  690.8 15.9 %small_sum.1 = f32[32,128]{1,0:T(8,128)} custom-call(f32[32,128]{1,0:T(8,128)} %fusion.22.x_ref), custom_call_target="tpu_custom_call" | custom-call | tf_op jit(solution)/shard_map/small_sum/pallas_call | solution.py:1577
  706.7 0.7 slice.293
  707.5 0.6 constant_dynamic-slice_fusion
  708.1 1.4 fusion.44
  709.5 1.3 convert_add_fusion.2
  710.9 2.1 convert_add_fusion
  713.0 0.5 collective-permute-start.5
  713.5 0.2 convert_add_fusion.1
  713.6 0.2 collective-permute-start.6
  714.2 1.1 pad_maximum_fusion.15
  715.3 1.1 pad_maximum_fusion.13
  716.4 4.6 collective-permute-done.6
  721.1 0.2 slice_bitcast_fusion.5
  721.7 0.2 slice_bitcast_fusion.2
  722.2 0.6 broadcast_select_fusion.2
  722.8 0.6 broadcast_select_fusion.3
  723.5 0.5 slice_select_fusion
  723.9 1.8 maximum_bitcast_fusion
  725.8 1.8 pad_maximum_fusion.2
  727.6 0.6 broadcast_select_fusion.4
  728.2 0.2 slice_select_fusion.2
  728.4 1.8 pad_maximum_fusion.1
  (96 shorter events, 2.4 us)
Async XLA Ops:
  0.6 87.1 %copy-start = (s32[2,2]{1,0:T(2,128)S(1)}, s32[2,2]{1,0:T(2,128)}, u32[]{:S(2)}) copy-start(s32[2,2]{1,0:T(2,128)} %param.16) | copy-start | bytes 52
  0.7 3.3 copy-start.20
  0.7 3.4 copy-start.19
  0.7 3.4 copy-start.18
  0.7 3.5 copy-start.13
  4.2 0.8 copy-start.10
  73.1 128.2 %collective-permute-start = (bf16[1536,1536]{1,0:T(8,128)(2,1)}, bf16[1536,1536]{1,0:T(8,128)(2,1)}, u32[]{:S(2)}, u32[]{:S(2)}) collective-permute-start(bf16[1536,1536]{1,0:T(8,128)(2,1)} %get-tuple-element.45.w_own), channel_id=1, source_target_pairs={{0,1},{1,0},{2,3},{3,2},{4,5},{5,4},{6,7},{7,6},{8,9},{9,8},{10,11... | collective-permute-start | bytes 14155784 | tf_op jit(solution)/shard_map/ppermute | solution.py:1675
  74.5 4.3 copy-start.14
  74.6 4.6 copy-start.3
  79.2 4.3 copy-start.16
  79.2 5.7 copy-start.9
  83.8 1.3 copy-start.6
  85.1 1.4 copy-start.5
  85.2 1.7 slice-start.3
  85.2 5.9 slice-start
  87.1 1.5 slice-start.2
  87.8 1.4 copy-start.4
  88.5 2.7 slice-start.1
  103.1 92.7 %copy-start.2 = (bf16[2,2,256,1536]{3,2,1,0:T(8,128)(2,1)S(1)}, bf16[2,2,256,1536]{3,2,1,0:T(8,128)(2,1)}, u32[]{:S(2)}) copy-start(bf16[2,2,256,1536]{3,2,1,0:T(8,128)(2,1)} %cotangent.1) | copy-start | bytes 9437188
  461.1 249.7 %collective-permute-start.3 = (bf16[3,192,1536]{2,1,0:T(8,128)(2,1)}, bf16[3,192,1536]{2,1,0:T(8,128)(2,1)}, u32[]{:S(2)}, u32[]{:S(2)}) collective-permute-start(bf16[3,192,1536]{2,1,0:T(8,128)(2,1)} %get-tuple-element.72), channel_id=1, source_target_pairs={{0,2},{1,3},{2,0},{3,1},{4,6},{5,7},{6,4},{7,5},{8,10},{9,11},{10,... | collective-permute-start | bytes 5308424 | tf_op jit(solution)/shard_map/ppermute | solution.py:1848
  476.8 192.0 %copy-start.15 = (f32[8,192]{1,0:T(8,128)S(1)}, f32[8,192]{1,0:T(8,128)}, u32[]{:S(2)}) copy-start(f32[8,192]{1,0:T(8,128)} %copy-done.14) | copy-start | bytes 18436
  476.8 194.6 %copy-start.7 = (pred[2047,32]{1,0:T(8,128)(4,1)S(1)}, pred[2047,32]{1,0:T(8,128)(4,1)}, u32[]{:S(2)}) copy-start(pred[2047,32]{1,0:T(8,128)(4,1)} %copy-done.6) | copy-start | bytes 196516
  668.7 40.8 %collective-permute-start.1 = (bf16[4,192,384]{2,1,0:T(8,128)(2,1)}, bf16[4,192,384]{2,1,0:T(8,128)(2,1)}, u32[]{:S(2)}, u32[]{:S(2)}) collective-permute-start(bf16[4,192,384]{2,1,0:T(8,128)(2,1)} %get-tuple-element.71), channel_id=1, source_target_pairs={{0,2},{1,3},{2,0},{3,1},{4,6},{5,7},{6,4},{7,5},{8,10},{9,11},{10,... | collective-permute-start | bytes 1769480 | tf_op jit(solution)/shard_map/ppermute | solution.py:1848
  669.4 44.0 %collective-permute-start.4 = (bf16[1,192,1536]{2,1,0:T(8,128)(2,1)}, bf16[1,192,1536]{2,1,0:T(8,128)(2,1)S(1)}, u32[]{:S(2)}, u32[]{:S(2)}) collective-permute-start(bf16[1,192,1536]{2,1,0:T(8,128)(2,1)} %get-tuple-element.73), channel_id=1, source_target_pairs={{0,2},{1,3},{2,0},{3,1},{4,6},{5,7},{6,4},{7,5},{8,10},{9,11},{10,... | collective-permute-start | bytes 1769480 | tf_op jit(solution)/shard_map/ppermute | solution.py:1848
  673.6 16.6 %copy-start.17 = (f32[1,1536]{1,0:T(1,128)S(1)}, f32[1,1536]{1,0:T(1,128)}, u32[]{:S(2)}) copy-start(f32[1,1536]{1,0:T(1,128)} %get-tuple-element.69) | copy-start | bytes 18436
  673.6 35.9 %copy-start.12 = (bf16[4,192,384]{2,1,0:T(8,128)(2,1)S(1)}, bf16[4,192,384]{2,1,0:T(8,128)(2,1)}, u32[]{:S(2)}) copy-start(bf16[4,192,384]{2,1,0:T(8,128)(2,1)} %get-tuple-element.71) | copy-start | bytes 1769476
  689.3 21.6 %copy-start.8 = (bf16[3,192,1536]{2,1,0:T(8,128)(2,1)S(1)}, bf16[3,192,1536]{2,1,0:T(8,128)(2,1)}, u32[]{:S(2)}) copy-start(bf16[3,192,1536]{2,1,0:T(8,128)(2,1)} %get-tuple-element.72) | copy-start | bytes 5308420
  710.8 2.7 copy-start.11
  710.8 3.2 collective-permute-start.2
  713.0 8.7 %collective-permute-start.5 = (f32[3,192,1536]{2,1,0:T(8,128)S(1)}, f32[3,192,1536]{2,1,0:T(8,128)S(1)}, u32[]{:S(2)}, u32[]{:S(2)}) collective-permute-start(f32[3,192,1536]{2,1,0:T(8,128)S(1)} %convert_add_fusion), channel_id=1, source_target_pairs={{0,1},{1,0},{2,3},{3,2},{4,5},{5,4},{6,7},{7,6},{8,9},{9,8},{10,11... | collective-permute-start | bytes 10616840 | tf_op jit(solution)/shard_map/ppermute | solution.py:1675
  713.6 7.4 %collective-permute-start.6 = (f32[1,192,1536]{2,1,0:T(8,128)S(1)}, f32[1,192,1536]{2,1,0:T(8,128)S(1)}, u32[]{:S(2)}, u32[]{:S(2)}) collective-permute-start(f32[1,192,1536]{2,1,0:T(8,128)S(1)} %get-tuple-element.117), channel_id=1, source_target_pairs={{0,1},{1,0},{2,3},{3,2},{4,5},{5,4},{6,7},{7,6},{8,9},{9,8},{10,11... | collective-permute-start | bytes 3538952 | tf_op jit(solution)/shard_map/ppermute | solution.py:1675
  728.4 1.9 copy-start.1

commit v6 on v5

--- a/solution.py
+++ b/solution.py
@@ -1251,8 +1251,8 @@
 
     per_pair = micro * steps
     work = pairs * per_pair
-    begins = [4] + [per_pair * (p + 1) for p in range(pairs)]
-    gap = 1
+    begins = [4] + [per_pair * (p + 1) + 3 for p in range(pairs - 1)] + [work + 2]
+    gap = max(1, 8 // far)
     last = begins[-1] + 2 * far * gap
 
     def item(i, carry):

time: 736 us -> 708 us (0.962)
  Pallas kernels: 657 us -> 630 us
    pallas_call x1, Pallas kernels: 192 us -> 163 us  [mix_back(): pl.pallas_call(functools.partial(mix_back_kernel, plan), in_specs=[pl.Blo...]
  transfers between devices with their start and end apart: 7 -> 7, of which waited for: 1 -> 1; matrix products, arithmetic and copies ran while one was open for 7% -> 7% of each run, Pallas kernels for 45% -> 43%
where the time goes in v6:
time: 708 us; the launch traced here: 703 us
  Pallas kernels  630 us (89%)
  other arithmetic  36.8 us (5%)
  matrix products  14.1 us (2%)
  local copies, waits for them, and re-layouts  12.3 us (2%)
    pallas_call x1, Pallas kernels, feed(): pl.pallas_call(functools.partial(feed_kernel, plan), in_specs=[anywhere]...  244 us
    pallas_call x1, Pallas kernels, mix_back(): pl.pallas_call(functools.partial(mix_back_kernel, plan), in_specs=[pl.Blo...  163 us
    pallas_call x1, Pallas kernels, mix_ahead(): pl.pallas_call(functools.partial(mix_ahead_kernel, plan), in_specs=[pl.Bl...  90.9 us
    pallas_call x1, Pallas kernels, gather_first(): pl.pallas_call(functools.partial(gather_kernel, count, planes, rows), in_...  68 us
    pallas_call x1, Pallas kernels, small_sum(): pl.pallas_call(functools.partial(small_sum_kernel, sizes), in_specs=[pl.B...  17.5 us
    pallas_call x1, Pallas kernels, input_back(): pl.pallas_call(input_back_kernel, grid=(groups,), in_specs=[tall(cols), t...  15.7 us
    pallas_call x1, Pallas kernels, resid_ahead(): pl.pallas_call(resid_ahead_kernel, grid_spec=pltpu.PrefetchScalarGridSpec...  15.3 us
    pallas_call x1, Pallas kernels, resid_back(): pl.pallas_call(resid_back_kernel, grid=(groups,), in_specs=[tall(depth)]...  14.8 us
  transfers between devices with their start and end apart: 7, of which 1 were waited for; matrix products, arithmetic and copies ran while one was open for 7% of the time, Pallas kernels for 43%

profile of v6, /device:TPU:0, one launch (start us, length us, event | category | flops | bytes accessed | tf_op | source)
XLA Modules:
  0.0 703.1 jit_solution(1317681419075811912)
XLA Ops:
  0.7 1.0 slice_select_fusion.7
  1.8 1.0 slice_select_fusion.6
  2.8 1.0 slice_select_fusion.5
  4.2 0.7 pad.30.small
  5.1 68.0 %gather_first.1 = (bf16[1536,1536]{1,0:T(8,128)(2,1)}, bf16[128,512]{1,0:T(8,128)(2,1)}, bf16[2,2,256,1536]{3,2,1,0:T(8,128)(2,1)}, bf16[2,2,256,1536]{3,2,1,0:T(8,128)(2,1)}, bf16[2,4,256,1536]{3,2,1,0:T(8,128)(2,1)}) custom-call(bf16[192,1536]{1,0:T(8,128)(2,1)} %copy-done.10, bf16[16,512]{1,0:T(8,128)(2,1)} %pad.30.small, ...), custom_call_target="tpu_custom_call" | custom-call | tf_op jit(solution)/shard_map/gather_first/pallas_call | solution.py:477
  73.1 0.5 collective-permute-start
  73.6 0.8 slice.340
  74.6 4.2 multiply_reduce_fusion
  78.9 0.3 copy-done.3
  79.2 4.2 fusion.1
  83.5 0.3 iota_compare_fusion
  83.9 0.3 fusion.9
  84.2 0.7 broadcast_in_dim.17.diag_ref
  84.9 0.2 slice_select_fusion.3
  85.3 1.3 copy-done.5
  86.5 0.3 slice-done.3
  86.9 0.2 pad_select_fusion.1
  87.1 0.7 broadcast_in_dim_reshape.8.gain
  87.8 0.7 dynamic-slice_reduce_fusion.len_ref
  88.5 0.6 copy-done.4
  89.2 0.2 pad_select_fusion
  89.4 0.9 pad_maximum_fusion.10.shard_2
  90.3 0.9 pad_maximum_fusion.9.shard
  91.2 12.0 %fusion.4.made.refs_0_ = bf16[2,1024,1152]{2,1,0:T(8,128)(2,1)} fusion(bf16[2,1,1024,1536]{3,2,0,1:T(8,128)(2,1)} %fusion.1, bf16[1536,1536]{1,0:T(8,128)(2,1)S(1)} %bitcast.102), kind=kOutput, calls=%fused_computation.7 | convolution fusion | flops 7250116608 | bytes 14548992 | tf_op jit(solution)/shard_map/mrld,de->mrle/dot_general | solution.py:1770
  103.1 90.9 %mix_ahead.1 = (bf16[2,2,512,384]{3,2,1,0:T(8,128)(2,1)}, bf16[2,2,512,384]{3,2,1,0:T(8,128)(2,1)}, f32[12,1,1024]{2,1,0:T(1,128)}, bf16[1536,1536]{1,0:T(8,128)(2,1)}, bf16[1536,1536]{1,0:T(8,128)(2,1)}) custom-call(s32[2]{0:T(128)} %dynamic-slice_reduce_fusion.len_ref, f32[6,1,2048]{2,1,0:T(1,128)} %broadcast_in_dim.17.diag_ref, ...), custom_call_target="tpu_custom_call" | custom-call | tf_op jit(solution)/shard_map/mix_ahead/pallas_call | solution.py:1047
  194.1 0.9 pad_maximum_fusion.11.refs_4_
  194.9 0.9 pad_maximum_fusion.12.refs_5_
  195.8 2.3 broadcast_select_fusion.1
  198.1 3.2 pad_maximum_fusion
  201.3 15.3 %resid_ahead.1 = (f32[4,256,1536]{2,1,0:T(8,128)}, bf16[4,512,1536]{2,1,0:T(8,128)(2,1)}) custom-call(s32[1]{0:T(128)} %bitcast.core_ref, bf16[4,512,384]{2,1,0:T(8,128)(2,1)} %bitcast.107, bf16[4,512,384]{2,1,0:T(8,128)(2,1)} %bitcast.111, bf16[1536,1536]{1,0:T(8,128)(2,1)} %get-tuple-element.45.w_own, bf16[1536,1536]{1,0:T(8,128)(2,1)} %collective-permute-done.w_other, ...), custom_call_target="tpu_custom_call" | custom-call | tf_op jit(solution)/shard_map/resid_ahead/pallas_call | solution.py:1090
  216.6 244.5 %feed.1 = (bf16[4,256,1536]{2,1,0:T(8,128)(2,1)}, bf16[4,256,1536]{2,1,0:T(8,128)(2,1)}, bf16[4,256,1536]{2,1,0:T(8,128)(2,1)}, bf16[4,256,1536]{2,1,0:T(8,128)(...) custom-call(bf16[2048,1536]{1,0:T(8,128)(2,1)} %bitcast.123, ...), custom_call_target="tpu_custom_call" | custom-call | flops 115964116992 | bytes 31457280 | tf_op jit(solution)/shard_map/feed/pallas_call | solution.py:835
  461.1 0.9 collective-permute-start.3
  462.0 14.8 %resid_back.1 = (f32[4,256,1536]{2,1,0:T(8,128)}, bf16[4,256,1536]{2,1,0:T(8,128)(2,1)}, bf16[4,256,384]{2,1,0:T(8,128)(2,1)}, bf16[4,256,384]{2,1,0:T(8,128)(2,...) custom-call(bf16[4,256,1536]{2,1,0:T(8,128)(2,1)} %get-tuple-element.53.kept, ...), custom_call_target="tpu_custom_call" | custom-call | tf_op jit(solution)/shard_map/resid_back/pallas_call | solution.py:1506
  476.8 162.9 %mix_back.1 = (bf16[4,256,1152]{2,1,0:T(8,128)(2,1)}, bf16[4,256,1152]{2,1,0:T(8,128)(2,1)}, f32[6,1,2048]{2,1,0:T(1,128)}, bf16[4,192,384]{2,1,0:T(8,128)(2,1)}...) custom-call(s32[2]{0:T(128)} %dynamic-slice_reduce_fusion.len_ref, ...), custom_call_target="tpu_custom_call" | custom-call | tf_op jit(solution)/shard_map/mix_back/pallas_call | solution.py:1421
  639.7 1.7 collective-permute-start.1
  641.4 0.7 broadcast_in_dim_reshape.9.gain
  642.1 0.4 collective-permute-start.4
  642.5 1.8 fusion.11
  644.2 0.2 dynamic_update_slice.3
  644.6 15.7 %input_back.1 = (f32[4,256,1536]{2,1,0:T(8,128)}, f32[1,1536]{1,0:T(1,128)}) custom-call(bf16[4,256,1152]{2,1,0:T(8,128)(2,1)} %get-tuple-element.64.own, bf16[4,256,1152]{2,1,0:T(8,128)(2,1)} %get-tuple-element.65.there, bf16[1536,1536]{1,0:T(8,128)(2,1)} %get-tuple-element.45.w_own, bf16[1536,1536]{1,0:T(8,128)(2,1)} %collective-permute-done.w_other, ...), custom_call_target="tpu_custom_call" | custom-call | tf_op jit(solution)/shard_map/input_back/pallas_call | solution.py:1539
  660.3 0.8 reduce.2
  661.2 0.6 fusion.22.x_ref
  661.8 17.5 %small_sum.1 = f32[32,128]{1,0:T(8,128)} custom-call(f32[32,128]{1,0:T(8,128)} %fusion.22.x_ref), custom_call_target="tpu_custom_call" | custom-call | tf_op jit(solution)/shard_map/small_sum/pallas_call | solution.py:1577
  679.3 0.7 slice.293
  680.1 0.6 constant_dynamic-slice_fusion
  680.7 1.4 fusion.44
  682.1 1.3 convert_add_fusion.2
  683.5 2.1 convert_add_fusion
  685.6 0.5 collective-permute-start.5
  686.1 0.2 convert_add_fusion.1
  686.2 0.2 collective-permute-start.6
  686.8 1.1 pad_maximum_fusion.15
  687.9 1.1 pad_maximum_fusion.13
  689.0 4.6 collective-permute-done.6
  693.7 0.2 slice_bitcast_fusion.5
  694.3 0.2 slice_bitcast_fusion.2
  694.8 0.6 broadcast_select_fusion.2
  695.4 0.6 broadcast_select_fusion.3
  696.0 0.5 slice_select_fusion
  696.5 1.8 maximum_bitcast_fusion
  698.4 1.8 pad_maximum_fusion.2
  700.2 0.6 broadcast_select_fusion.4
  700.8 0.2 slice_select_fusion.2
  701.0 1.8 pad_maximum_fusion.1
  (96 shorter events, 2.5 us)
Async XLA Ops:
  0.6 87.1 %copy-start = (s32[2,2]{1,0:T(2,128)S(1)}, s32[2,2]{1,0:T(2,128)}, u32[]{:S(2)}) copy-start(s32[2,2]{1,0:T(2,128)} %param.16) | copy-start | bytes 52
  0.7 3.3 copy-start.20
  0.7 3.4 copy-start.19
  0.7 3.4 copy-start.18
  0.7 3.5 copy-start.13
  4.2 0.8 copy-start.10
  73.1 128.2 %collective-permute-start = (bf16[1536,1536]{1,0:T(8,128)(2,1)}, bf16[1536,1536]{1,0:T(8,128)(2,1)}, u32[]{:S(2)}, u32[]{:S(2)}) collective-permute-start(bf16[1536,1536]{1,0:T(8,128)(2,1)} %get-tuple-element.45.w_own), channel_id=1, source_target_pairs={{0,1},{1,0},{2,3},{3,2},{4,5},{5,4},{6,7},{7,6},{8,9},{9,8},{10,11... | collective-permute-start | bytes 14155784 | tf_op jit(solution)/shard_map/ppermute | solution.py:1675
  74.5 4.3 copy-start.14
  74.6 4.6 copy-start.3
  79.2 4.3 copy-start.16
  79.2 5.7 copy-start.9
  83.8 1.3 copy-start.6
  85.1 1.4 copy-start.5
  85.2 1.7 slice-start.3
  85.2 5.9 slice-start
  87.1 1.5 slice-start.2
  87.8 1.4 copy-start.4
  88.5 2.7 slice-start.1
  103.1 92.7 %copy-start.2 = (bf16[2,2,256,1536]{3,2,1,0:T(8,128)(2,1)S(1)}, bf16[2,2,256,1536]{3,2,1,0:T(8,128)(2,1)}, u32[]{:S(2)}) copy-start(bf16[2,2,256,1536]{3,2,1,0:T(8,128)(2,1)} %cotangent.1) | copy-start | bytes 9437188
  461.1 222.3 %collective-permute-start.3 = (bf16[3,192,1536]{2,1,0:T(8,128)(2,1)}, bf16[3,192,1536]{2,1,0:T(8,128)(2,1)}, u32[]{:S(2)}, u32[]{:S(2)}) collective-permute-start(bf16[3,192,1536]{2,1,0:T(8,128)(2,1)} %get-tuple-element.72), channel_id=1, source_target_pairs={{0,2},{1,3},{2,0},{3,1},{4,6},{5,7},{6,4},{7,5},{8,10},{9,11},{10,... | collective-permute-start | bytes 5308424 | tf_op jit(solution)/shard_map/ppermute | solution.py:1848
  476.8 164.6 %copy-start.15 = (f32[8,192]{1,0:T(8,128)S(1)}, f32[8,192]{1,0:T(8,128)}, u32[]{:S(2)}) copy-start(f32[8,192]{1,0:T(8,128)} %copy-done.14) | copy-start | bytes 18436
  476.8 165.7 %copy-start.7 = (pred[2047,32]{1,0:T(8,128)(4,1)S(1)}, pred[2047,32]{1,0:T(8,128)(4,1)}, u32[]{:S(2)}) copy-start(pred[2047,32]{1,0:T(8,128)(4,1)} %copy-done.6) | copy-start | bytes 196516
  639.7 42.4 %collective-permute-start.1 = (bf16[4,192,384]{2,1,0:T(8,128)(2,1)}, bf16[4,192,384]{2,1,0:T(8,128)(2,1)}, u32[]{:S(2)}, u32[]{:S(2)}) collective-permute-start(bf16[4,192,384]{2,1,0:T(8,128)(2,1)} %get-tuple-element.71), channel_id=1, source_target_pairs={{0,2},{1,3},{2,0},{3,1},{4,6},{5,7},{6,4},{7,5},{8,10},{9,11},{10,... | collective-permute-start | bytes 1769480 | tf_op jit(solution)/shard_map/ppermute | solution.py:1848
  642.1 44.0 %collective-permute-start.4 = (bf16[1,192,1536]{2,1,0:T(8,128)(2,1)}, bf16[1,192,1536]{2,1,0:T(8,128)(2,1)S(1)}, u32[]{:S(2)}, u32[]{:S(2)}) collective-permute-start(bf16[1,192,1536]{2,1,0:T(8,128)(2,1)} %get-tuple-element.73), channel_id=1, source_target_pairs={{0,2},{1,3},{2,0},{3,1},{4,6},{5,7},{6,4},{7,5},{8,10},{9,11},{10,... | collective-permute-start | bytes 1769480 | tf_op jit(solution)/shard_map/ppermute | solution.py:1848
  644.6 16.6 %copy-start.17 = (f32[1,1536]{1,0:T(1,128)S(1)}, f32[1,1536]{1,0:T(1,128)}, u32[]{:S(2)}) copy-start(f32[1,1536]{1,0:T(1,128)} %get-tuple-element.69) | copy-start | bytes 18436
  644.6 37.5 %copy-start.12 = (bf16[4,192,384]{2,1,0:T(8,128)(2,1)S(1)}, bf16[4,192,384]{2,1,0:T(8,128)(2,1)}, u32[]{:S(2)}) copy-start(bf16[4,192,384]{2,1,0:T(8,128)(2,1)} %get-tuple-element.71) | copy-start | bytes 1769476
  660.3 23.1 %copy-start.8 = (bf16[3,192,1536]{2,1,0:T(8,128)(2,1)S(1)}, bf16[3,192,1536]{2,1,0:T(8,128)(2,1)}, u32[]{:S(2)}) copy-start(bf16[3,192,1536]{2,1,0:T(8,128)(2,1)} %get-tuple-element.72) | copy-start | bytes 5308420
  683.4 2.7 copy-start.11
  683.4 3.2 collective-permute-start.2
  685.6 8.7 %collective-permute-start.5 = (f32[3,192,1536]{2,1,0:T(8,128)S(1)}, f32[3,192,1536]{2,1,0:T(8,128)S(1)}, u32[]{:S(2)}, u32[]{:S(2)}) collective-permute-start(f32[3,192,1536]{2,1,0:T(8,128)S(1)} %convert_add_fusion), channel_id=1, source_target_pairs={{0,1},{1,0},{2,3},{3,2},{4,5},{5,4},{6,7},{7,6},{8,9},{9,8},{10,11... | collective-permute-start | bytes 10616840 | tf_op jit(solution)/shard_map/ppermute | solution.py:1675
  686.2 7.4 %collective-permute-start.6 = (f32[1,192,1536]{2,1,0:T(8,128)S(1)}, f32[1,192,1536]{2,1,0:T(8,128)S(1)}, u32[]{:S(2)}, u32[]{:S(2)}) collective-permute-start(f32[1,192,1536]{2,1,0:T(8,128)S(1)} %get-tuple-element.117), channel_id=1, source_target_pairs={{0,1},{1,0},{2,3},{3,2},{4,5},{5,4},{6,7},{7,6},{8,9},{9,8},{10,11... | collective-permute-start | bytes 3538952 | tf_op jit(solution)/shard_map/ppermute | solution.py:1675
  701.0 1.9 copy-start.1
